TPU v7x, 128 devices: a whole 4x4x4 slice. The times are simulated.
128 devices in a mesh: ctx: 16 (over x, y_lo, core), head: 8 (over y_hi, z).
Axes of the slice: x: 4, y: 4 (y_hi: 2, y_lo: 2; y = y_hi * 2 + y_lo), z: 4, core: 2. Of those that a mesh axis runs over, the one named last changes fastest.
Arguments:
- clean_q: bfloat16 [8192, 2048], P('ctx', 'head')
- clean_k: bfloat16 [8192, 2048], P('ctx', 'head')
- clean_v: bfloat16 [8192, 2048], P('ctx', 'head'), may hold values from -6 to 6
- noisy_q: bfloat16 [8192, 2048], P('ctx', 'head')
- noisy_k: bfloat16 [8192, 2048], P('ctx', 'head')
- noisy_v: bfloat16 [8192, 2048], P('ctx', 'head'), may hold values from -6 to 6
- q_gain: float32 [2048], P('head'), may hold values from 0.5 to 4
- k_gain: float32 [2048], P('head'), may hold values from 0.5 to 4
- grad_clean: bfloat16 [8192, 2048], P('ctx', 'head'), may hold values from -6 to 6
- grad_noisy: bfloat16 [8192, 2048], P('ctx', 'head'), may hold values from -6 to 6
- owned_blocks: int32 [32], P('ctx'), may hold values from 0 to 31, as said below
- block_doc: int32 [32], replicated, may hold values from 0 to 7, never falling along the last dimension, each value on 1 to 16 neighbouring positions
Outputs:
- out_clean: float32 [8192, 2048], P('ctx', 'head')
- out_noisy: float32 [8192, 2048], P('ctx', 'head')
- dq_clean: float32 [8192, 2048], P('ctx', 'head')
- dk_clean: float32 [8192, 2048], P('ctx', 'head')
- dv_clean: float32 [8192, 2048], P('ctx', 'head')
- dq_noisy: float32 [8192, 2048], P('ctx', 'head')
- dk_noisy: float32 [8192, 2048], P('ctx', 'head')
- dv_noisy: float32 [8192, 2048], P('ctx', 'head')
Inputs may be any that keep to these rules, and one draw needn't show every extreme that they name: `owned_blocks`: every block appears once; entries 2i and 2i+1 sum to 31.
All inputs are finite; a program needn't handle non-finite values.
Results may differ from a plain program's by a relative error of at most 0.035.
The roundings to bfloat16 on the way count: a program that leaves them out, or rounds other values in their place, can miss the bound.
Values may be sent and summed in bfloat16 or wider, within the bound.
A program may use at most 128 MiB of HBM per device.

v0:
```python
import math

import jax
import jax.numpy as jnp
from jax import lax
from jax.sharding import PartitionSpec as P

HD = 128


NEGATIVE = -1e30
EPSILON = 1e-06


def doc_lookup(block_doc, block_id):
    return jnp.sum(jnp.where(jnp.arange(block_doc.shape[0]) == block_id, block_doc, 0))


def docs_of(block_doc, block_ids):
    matches = jnp.arange(block_doc.shape[0])[None, :] == block_ids[:, None]
    return jnp.sum(jnp.where(matches, block_doc[None, :], 0), axis=1)


def blocks_per_step(block_count):
    for candidate in range(min(block_count, 8), 0, -1):
        return candidate
    return 1


def forward_tile(softmax_state, query_rows, key_rows, value_rows, visible_mask, score_scale):
    row_peak, row_total, weighted = softmax_state
    scores = (
        jnp.einsum("qhd,khd->hqk", query_rows, key_rows, preferred_element_type=jnp.float32)
        * score_scale
    )
    scores = jnp.where(visible_mask[None], scores, NEGATIVE)
    new_peak = jnp.maximum(row_peak, jnp.max(scores, axis=2))
    weights = jnp.where(visible_mask[None], jnp.exp(scores - new_peak[:, :, None]), 0.0)
    factor = jnp.exp(row_peak - new_peak)
    row_total = row_total * factor + jnp.sum(weights, axis=2)
    weighted = weighted * jnp.transpose(factor)[:, :, None] + jnp.einsum(
        "hqk,khd->qhd", weights.astype(jnp.bfloat16), value_rows, preferred_element_type=jnp.float32
    )
    return (new_peak, row_total, weighted)


def backward_tile(
    query_rows, grad_rows, log_total, delta_rows, key_rows, value_rows, visible_mask, score_scale
):
    scores = (
        jnp.einsum("qhd,khd->hqk", query_rows, key_rows, preferred_element_type=jnp.float32)
        * score_scale
    )
    probability = jnp.where(visible_mask[None], jnp.exp(scores - log_total[:, :, None]), 0.0)
    value_grad = jnp.einsum(
        "hqk,qhd->khd",
        probability.astype(jnp.bfloat16),
        grad_rows,
        preferred_element_type=jnp.float32,
    )
    prob_grad = jnp.einsum(
        "qhd,khd->hqk", grad_rows, value_rows, preferred_element_type=jnp.float32
    )
    score_grad = (probability * (prob_grad - delta_rows[:, :, None])).astype(jnp.bfloat16)
    query_grad = (
        jnp.einsum("hqk,khd->qhd", score_grad, key_rows, preferred_element_type=jnp.float32)
        * score_scale
    )
    key_grad = (
        jnp.einsum("hqk,qhd->khd", score_grad, query_rows, preferred_element_type=jnp.float32)
        * score_scale
    )
    return (query_grad, key_grad, value_grad)


def local(
    clean_q,
    clean_k,
    clean_v,
    noisy_q,
    noisy_k,
    noisy_v,
    q_gain,
    k_gain,
    grad_clean,
    grad_noisy,
    owned_blocks,
    block_doc,
):
    local_rows, local_width = clean_q.shape
    half = local_rows // 2
    local_heads = local_width // HD
    score_scale = 1.0 / math.sqrt(HD)
    full_width = local_width * lax.axis_size("head")
    raw_cq = clean_q.astype(jnp.float32)
    raw_ck = clean_k.astype(jnp.float32)
    raw_nq = noisy_q.astype(jnp.float32)
    raw_nk = noisy_k.astype(jnp.float32)
    squares = lax.psum(
        (
            jnp.sum(raw_cq * raw_cq, axis=1),
            jnp.sum(raw_ck * raw_ck, axis=1),
            jnp.sum(raw_nq * raw_nq, axis=1),
            jnp.sum(raw_nk * raw_nk, axis=1),
        ),
        "head",
    )
    inverses = [lax.rsqrt(total_sq / full_width + EPSILON)[:, None] for total_sq in squares]
    clean_qn = (raw_cq * inverses[0] * q_gain).astype(jnp.bfloat16)
    clean_kn = (raw_ck * inverses[1] * k_gain).astype(jnp.bfloat16)
    noisy_qn = (raw_nq * inverses[2] * q_gain).astype(jnp.bfloat16)
    noisy_kn = (raw_nk * inverses[3] * k_gain).astype(jnp.bfloat16)

    def to_pairs(clean_rows, noisy_rows):
        both = jnp.stack(
            [clean_rows.reshape(2, half, local_width), noisy_rows.reshape(2, half, local_width)],
            axis=1,
        )
        return both.reshape(2, 2 * half, local_heads, HD)

    def from_pairs(paired):
        flat = paired.reshape(2, 2, half, local_width)
        return (
            flat[:, 0].reshape(local_rows, local_width),
            flat[:, 1].reshape(local_rows, local_width),
        )

    query_pairs = to_pairs(clean_qn, noisy_qn)
    grad_pairs = to_pairs(grad_clean, grad_noisy)
    row_kind = (jnp.arange(2 * half) >= half).astype(jnp.int32)
    my_blocks = [owned_blocks[0], owned_blocks[1]]
    my_docs = [doc_lookup(block_doc, my_blocks[0]), doc_lookup(block_doc, my_blocks[1])]
    own_keys = noisy_kn.reshape(2, half, local_heads, HD)
    own_values = noisy_v.reshape(2, half, local_heads, HD)
    own_mask = jnp.broadcast_to((row_kind == 1)[:, None], (2 * half, half))

    def clean_mask(pair_slot, key_blocks):
        width_blocks = key_blocks.shape[0]
        same_doc = docs_of(block_doc, key_blocks) == my_docs[pair_slot]
        rows_ok = (key_blocks[None, :] + row_kind[:, None] <= my_blocks[pair_slot]) & same_doc[
            None, :
        ]
        tile_live = jnp.any(same_doc & (key_blocks <= my_blocks[pair_slot]))
        visible_mask = jnp.broadcast_to(
            rows_ok[:, :, None], (2 * half, width_blocks, half)
        ).reshape(2 * half, width_blocks * half)
        return (tile_live, visible_mask)

    def split_steps(key_rows, value_rows, block_ids):
        block_count = block_ids.shape[0]
        step_blocks = blocks_per_step(block_count)
        step_count = block_count // step_blocks
        key_rows = key_rows.reshape(step_count, step_blocks * half, local_heads, HD)
        value_rows = value_rows.reshape(step_count, step_blocks * half, local_heads, HD)
        return (key_rows, value_rows, block_ids.reshape(step_count, step_blocks))

    start_state = (
        jnp.full((local_heads, 2 * half), NEGATIVE, jnp.float32),
        jnp.zeros((local_heads, 2 * half), jnp.float32),
        jnp.zeros((2 * half, local_heads, HD), jnp.float32),
    )
    states = (start_state, start_state)
    shard_piece = (
        lax.all_gather(clean_kn, "ctx", axis=0, tiled=True),
        lax.all_gather(clean_v, "ctx", axis=0, tiled=True),
        lax.all_gather(owned_blocks, "ctx", axis=0, tiled=True),
    )
    key_rows, value_rows, block_ids = split_steps(shard_piece[0], shard_piece[1], shard_piece[2])

    def forward_advance(running, block_item):
        key_step_rows, value_step_rows, key_blocks = block_item
        updated = []
        for pair_slot in range(2):
            tile_live, visible_mask = clean_mask(pair_slot, key_blocks)

            def forward_live(softmax_state, pair_slot=pair_slot, visible_mask=visible_mask):
                return forward_tile(
                    softmax_state,
                    query_pairs[pair_slot],
                    key_step_rows,
                    value_step_rows,
                    visible_mask,
                    score_scale,
                )

            def forward_skipped(softmax_state):
                return softmax_state

            updated.append(lax.cond(tile_live, forward_live, forward_skipped, running[pair_slot]))
        return (tuple(updated), None)

    states, _ = lax.scan(forward_advance, states, (key_rows, value_rows, block_ids))
    out_list = []
    lse_list = []
    for pair_slot in range(2):
        row_peak, row_total, weighted = forward_tile(
            states[pair_slot],
            query_pairs[pair_slot],
            own_keys[pair_slot],
            own_values[pair_slot],
            own_mask,
            score_scale,
        )
        out_list.append(weighted / jnp.transpose(row_total)[:, :, None])
        lse_list.append(row_peak + jnp.log(row_total))
    out_pairs = jnp.stack(out_list)
    lse_pairs = jnp.stack(lse_list)
    delta_pairs = jnp.transpose(
        jnp.sum(grad_pairs.astype(jnp.float32) * out_pairs, axis=3), (0, 2, 1)
    )
    out_clean, out_noisy = from_pairs(out_pairs)

    def backward_block(dq_pairs, key_step_rows, value_step_rows, key_blocks):
        key_sum = jnp.zeros(key_step_rows.shape, jnp.float32)
        value_sum = jnp.zeros(key_step_rows.shape, jnp.float32)
        updated = []
        for pair_slot in range(2):
            tile_live, visible_mask = clean_mask(pair_slot, key_blocks)

            def backward_live(running, pair_slot=pair_slot, visible_mask=visible_mask):
                query_grad, key_grad, value_grad = backward_tile(
                    query_pairs[pair_slot],
                    grad_pairs[pair_slot],
                    lse_pairs[pair_slot],
                    delta_pairs[pair_slot],
                    key_step_rows,
                    value_step_rows,
                    visible_mask,
                    score_scale,
                )
                return (running[0] + query_grad, running[1] + key_grad, running[2] + value_grad)

            def backward_skipped(running):
                return running

            result = lax.cond(
                tile_live,
                backward_live,
                backward_skipped,
                (dq_pairs[pair_slot], key_sum, value_sum),
            )
            key_sum = result[1]
            value_sum = result[2]
            updated.append(result[0])
        return (tuple(updated), key_sum, value_sum)

    zero_pair = jnp.zeros((2 * half, local_heads, HD), jnp.float32)
    shard_piece = (
        lax.all_gather(clean_kn, "ctx", axis=0, tiled=True),
        lax.all_gather(clean_v, "ctx", axis=0, tiled=True),
        lax.all_gather(owned_blocks, "ctx", axis=0, tiled=True),
    )
    dq_pairs = (zero_pair, zero_pair)
    key_rows, value_rows, block_ids = split_steps(shard_piece[0], shard_piece[1], shard_piece[2])

    def returned_advance(dq_running, block_item):
        dq_running, key_sum, value_sum = backward_block(
            dq_running, block_item[0], block_item[1], block_item[2]
        )
        return (dq_running, (key_sum, value_sum))

    dq_pairs, (key_parts, value_parts) = lax.scan(
        returned_advance, dq_pairs, (key_rows, value_rows, block_ids)
    )
    key_all = key_parts.reshape(-1, local_width)
    value_all = value_parts.reshape(-1, local_width)
    dq_list = list(dq_pairs)
    key_clean, value_clean = (
        lax.psum_scatter(
            key_all.astype(jnp.bfloat16), "ctx", scatter_dimension=0, tiled=True
        ).astype(jnp.float32),
        lax.psum_scatter(
            value_all.astype(jnp.bfloat16), "ctx", scatter_dimension=0, tiled=True
        ).astype(jnp.float32),
    )
    noisy_key_parts = []
    noisy_value_parts = []
    for pair_slot in range(2):
        query_grad, key_grad, value_grad = backward_tile(
            query_pairs[pair_slot],
            grad_pairs[pair_slot],
            lse_pairs[pair_slot],
            delta_pairs[pair_slot],
            own_keys[pair_slot],
            own_values[pair_slot],
            own_mask,
            score_scale,
        )
        dq_list[pair_slot] = dq_list[pair_slot] + query_grad
        noisy_key_parts.append(key_grad)
        noisy_value_parts.append(value_grad)
    query_clean, query_noisy = from_pairs(jnp.stack(dq_list))
    key_noisy = jnp.concatenate(noisy_key_parts, axis=0).reshape(local_rows, local_width)
    value_noisy = jnp.concatenate(noisy_value_parts, axis=0).reshape(local_rows, local_width)
    scaled_cq = q_gain * query_clean
    scaled_ck = k_gain * key_clean
    scaled_nq = q_gain * query_noisy
    scaled_nk = k_gain * key_noisy
    inners = lax.psum(
        (
            jnp.sum(raw_cq * scaled_cq, axis=1),
            jnp.sum(raw_ck * scaled_ck, axis=1),
            jnp.sum(raw_nq * scaled_nq, axis=1),
            jnp.sum(raw_nk * scaled_nk, axis=1),
        ),
        "head",
    )

    def through_norm(raw_input, inverse, scaled, inner):
        cubed = inverse * inverse * inverse
        return inverse * scaled - raw_input * cubed * (inner / full_width)[:, None]

    dq_clean = through_norm(raw_cq, inverses[0], scaled_cq, inners[0])
    dk_clean = through_norm(raw_ck, inverses[1], scaled_ck, inners[1])
    dq_noisy = through_norm(raw_nq, inverses[2], scaled_nq, inners[2])
    dk_noisy = through_norm(raw_nk, inverses[3], scaled_nk, inners[3])
    return (out_clean, out_noisy, dq_clean, dk_clean, value_clean, dq_noisy, dk_noisy, value_noisy)


def solution(mesh):
    placed = (
        P("ctx", "head"),
        P("ctx", "head"),
        P("ctx", "head"),
        P("ctx", "head"),
        P("ctx", "head"),
        P("ctx", "head"),
        P("head"),
        P("head"),
        P("ctx", "head"),
        P("ctx", "head"),
        P("ctx"),
        P(),
    )
    return jax.shard_map(
        local,
        mesh=mesh,
        in_specs=placed,
        out_specs=(
            P("ctx", "head"),
            P("ctx", "head"),
            P("ctx", "head"),
            P("ctx", "head"),
            P("ctx", "head"),
            P("ctx", "head"),
            P("ctx", "head"),
            P("ctx", "head"),
        ),
        check_vma=False,
    )
```

profile of v0, /device:TPU:1, one launch (start us, length us, event | category | flops | bytes accessed | tf_op | source)
XLA Modules:
  0.0 597.5 jit_solution(16988666460407210970)
XLA Ops:
  12.8 23.0 %all-reduce.2 = (f32[512]{0:T(512)S(1)}, f32[512]{0:T(512)S(1)}, f32[512]{0:T(512)S(1)}, f32[512]{0:T(512)S(1)}) all-reduce(f32[512]{0:T(512)S(1)} %fusion.127, f32[512]{0:T(512)S(1)} %fusion.133, f32[512]{0:T(512)S(1)} %fusion.139, f32[512]{0:T(512)S(1)} %fusion.121), channel_id=1, replica_groups=mesh['ctx'=16,'head'=8] {'head'}, use_global_device_ids=true, to_apply=%region_4.0 | all-reduce | flops 2048 | bytes 16384 | tf_op jit(solution)/shard_map/psum | solution.py:99
  44.6 13.0 %all-reduce = s32[32]{0:T(128)S(1)} all-reduce(s32[32]{0:T(128)S(1)} %dynamic-update-slice), channel_id=1, replica_groups=mesh['ctx'=16,'head'=8] {'ctx'}, use_global_device_ids=true, to_apply=%add | all-reduce | flops 32 | bytes 256
  80.8 9.6 %all-gather.3.cloned.1.call-done = bf16[8192,256]{0,1:T(8,128)(2,1)} async-done(((bf16[512,256]{0,1:T(8,128)(2,1)}), bf16[8192,256]{0,1:T(8,128)(2,1)}) %all-gather.3.cloned.1.call-update) | async-done | bytes 4194320 | tf_op jit(solution)/shard_map/all_gather | solution.py:164
  98.2 7.9 %copy.123 = bf16[4,2048,2,128]{3,1,2,0:T(8,128)(2,1)} copy(bf16[4,2048,2,128]{1,0,3,2:T(4,128)(2,1)} %reshape.295) | data formatting | bytes 8388608
  107.0 107.9 %while.41 = (s32[]{:T(128)}, f32[2,512]{1,0:T(2,128)S(1)}, f32[2,512]{1,0:T(2,128)S(1)}, f32[512,2,128]{2,0,1:T(8,128)}, f32[2,512]{1,0:T(2,128)S(1)}, /*index=5...) while((s32[]{:T(128)}, f32[2,512]{1,0:T(2,128)S(1)}, ...), condition=%wide.region_20.21_spmd.clone, body=%wide.region_8.20_spmd.clone.sunk | while | flops 2202562304 | bytes 78320768 | solution.py:192
  115.8 12.3 %conditional.12 = ((f32[2,512]{1,0:T(2,128)S(1)}, f32[2,512]{1,0:T(2,128)S(1)}, f32[512,2,128]{2,0,1:T(8,128)})) conditional(s32[]{:T(128)} %convert_element_type.264, (f32[2,512]{1,0:T(2,128)S(1)}, f32[2,512]{1,0:T(2,128)S(1)}, f32[512,2,128]{2,0,1:T(8,128)}) %tuple.154, (s32[]{:T(128)}, s32[512,8,1]{1,0,2:T(8,128)S(1)}, s32[]{:T(128)}, ...), branch_computations={%region_11.11_spmd, %region_12.14_spmd} | conditional | flops 1101278208 | bytes 39149712 | solution.py:189
  128.1 12.2 %conditional.13 = ((f32[2,512]{1,0:T(2,128)S(1)}, f32[2,512]{1,0:T(2,128)S(1)}, f32[512,2,128]{2,0,1:T(8,128)S(1)})) conditional(s32[]{:T(128)} %convert_element_type.265, (f32[2,512]{1,0:T(2,128)S(1)}, f32[2,512]{1,0:T(2,128)S(1)}, f32[512,2,128]{2,0,1:T(8,128)S(1)}) %tuple.156, (s32[]{:T(128)}, s32[512,8,1]{1,0,2:T(8,128)S(1)}, s32[]{:T(128)}, ...), branch_computations={%region_16.16_spmd, %region_17.19_spmd} | conditional | flops 1101278208 | bytes 34955352 | solution.py:189
  148.9 12.2 %conditional.13 = ((f32[2,512]{1,0:T(2,128)S(1)}, f32[2,512]{1,0:T(2,128)S(1)}, f32[512,2,128]{2,0,1:T(8,128)S(1)})) conditional(s32[]{:T(128)} %convert_element_type.265, (f32[2,512]{1,0:T(2,128)S(1)}, f32[2,512]{1,0:T(2,128)S(1)}, f32[512,2,128]{2,0,1:T(8,128)S(1)}) %tuple.156, (s32[]{:T(128)}, s32[512,8,1]{1,0,2:T(8,128)S(1)}, s32[]{:T(128)}, ...), branch_computations={%region_16.16_spmd, %region_17.19_spmd} | conditional | flops 1101278208 | bytes 34955352 | solution.py:189
  169.6 12.3 %conditional.12 = ((f32[2,512]{1,0:T(2,128)S(1)}, f32[2,512]{1,0:T(2,128)S(1)}, f32[512,2,128]{2,0,1:T(8,128)})) conditional(s32[]{:T(128)} %convert_element_type.264, (f32[2,512]{1,0:T(2,128)S(1)}, f32[2,512]{1,0:T(2,128)S(1)}, f32[512,2,128]{2,0,1:T(8,128)}) %tuple.154, (s32[]{:T(128)}, s32[512,8,1]{1,0,2:T(8,128)S(1)}, s32[]{:T(128)}, ...), branch_computations={%region_11.11_spmd, %region_12.14_spmd} | conditional | flops 1101278208 | bytes 39149712 | solution.py:189
  181.9 12.2 %conditional.13 = ((f32[2,512]{1,0:T(2,128)S(1)}, f32[2,512]{1,0:T(2,128)S(1)}, f32[512,2,128]{2,0,1:T(8,128)S(1)})) conditional(s32[]{:T(128)} %convert_element_type.265, (f32[2,512]{1,0:T(2,128)S(1)}, f32[2,512]{1,0:T(2,128)S(1)}, f32[512,2,128]{2,0,1:T(8,128)S(1)}) %tuple.156, (s32[]{:T(128)}, s32[512,8,1]{1,0,2:T(8,128)S(1)}, s32[]{:T(128)}, ...), branch_computations={%region_16.16_spmd, %region_17.19_spmd} | conditional | flops 1101278208 | bytes 34955352 | solution.py:189
  202.7 12.2 %conditional.13 = ((f32[2,512]{1,0:T(2,128)S(1)}, f32[2,512]{1,0:T(2,128)S(1)}, f32[512,2,128]{2,0,1:T(8,128)S(1)})) conditional(s32[]{:T(128)} %convert_element_type.265, (f32[2,512]{1,0:T(2,128)S(1)}, f32[2,512]{1,0:T(2,128)S(1)}, f32[512,2,128]{2,0,1:T(8,128)S(1)}) %tuple.156, (s32[]{:T(128)}, s32[512,8,1]{1,0,2:T(8,128)S(1)}, s32[]{:T(128)}, ...), branch_computations={%region_16.16_spmd, %region_17.19_spmd} | conditional | flops 1101278208 | bytes 34955352 | solution.py:189
  226.8 189.9 %while.42 = (s32[]{:T(128)}, f32[512,2,128]{2,0,1:T(8,128)}, f32[512,2,128]{2,0,1:T(8,128)}, bf16[4,2048,2,128]{3,1,2,0:T(8,128)(2,1)}, bf16[4,2048,2,128]{3,1,2...) while((s32[]{:T(128)}, f32[512,2,128]{2,0,1:T(8,128)}, ...), condition=%wide.region_36.37_spmd.clone, body=%wide.region_28.36_spmd.clone.sunk | while | flops 5413296128 | bytes 142718192 | solution.py:262
  249.6 17.8 %conditional.14 = (f32[512,2,128]{2,0,1:T(8,128)S(1)}, f32[2048,2,128]{2,0,1:T(8,128)S(1)}, f32[2048,2,128]{2,0,1:T(8,128)}) conditional(s32[]{:T(128)} %convert_element_type.267, f32[512,2,128]{2,0,1:T(8,128)S(1)} %copy-done.9, (s32[]{:T(128)}, s32[512,8,1]{1,0,2:T(8,128)S(1)}, s32[]{:T(128)}, s32[1,8]{1,0:T(1,128)S(1)}, ...), branch_computations={%region_31.31_spmd, %region_32.32_spmd} | conditional | flops 2706120704 | bytes 56668296 | solution.py:236
  268.2 20.3 %conditional.15 = (f32[512,2,128]{2,0,1:T(8,128)}, f32[1,2048,2,128]{3,1,2,0:T(8,128)S(1)}, f32[1,2048,2,128]{3,1,2,0:T(8,128)}) conditional(s32[]{:T(128)} %convert_element_type.268, (f32[512,2,128]{2,0,1:T(8,128)}, f32[2048,2,128]{2,0,1:T(8,128)S(1)}, f32[2048,2,128]{2,0,1:T(8,128)}) %tuple.178, (s32[]{:T(128)}, s32[512,8,1]{1,0,2:T(8,128)S(1)}, ...), branch_computations={%region_34.34_spmd, %region_35.35_spmd} | conditional | flops 2707169280 | bytes 65056960 | solution.py:236
  304.3 20.4 %conditional.15 = (f32[512,2,128]{2,0,1:T(8,128)}, f32[1,2048,2,128]{3,1,2,0:T(8,128)S(1)}, f32[1,2048,2,128]{3,1,2,0:T(8,128)}) conditional(s32[]{:T(128)} %convert_element_type.268, (f32[512,2,128]{2,0,1:T(8,128)}, f32[2048,2,128]{2,0,1:T(8,128)S(1)}, f32[2048,2,128]{2,0,1:T(8,128)}) %tuple.178, (s32[]{:T(128)}, s32[512,8,1]{1,0,2:T(8,128)S(1)}, ...), branch_computations={%region_34.34_spmd, %region_35.35_spmd} | conditional | flops 2707169280 | bytes 65056960 | solution.py:236
  337.8 17.8 %conditional.14 = (f32[512,2,128]{2,0,1:T(8,128)S(1)}, f32[2048,2,128]{2,0,1:T(8,128)S(1)}, f32[2048,2,128]{2,0,1:T(8,128)}) conditional(s32[]{:T(128)} %convert_element_type.267, f32[512,2,128]{2,0,1:T(8,128)S(1)} %copy-done.9, (s32[]{:T(128)}, s32[512,8,1]{1,0,2:T(8,128)S(1)}, s32[]{:T(128)}, s32[1,8]{1,0:T(1,128)S(1)}, ...), branch_computations={%region_31.31_spmd, %region_32.32_spmd} | conditional | flops 2706120704 | bytes 56668296 | solution.py:236
  356.4 20.3 %conditional.15 = (f32[512,2,128]{2,0,1:T(8,128)}, f32[1,2048,2,128]{3,1,2,0:T(8,128)S(1)}, f32[1,2048,2,128]{3,1,2,0:T(8,128)}) conditional(s32[]{:T(128)} %convert_element_type.268, (f32[512,2,128]{2,0,1:T(8,128)}, f32[2048,2,128]{2,0,1:T(8,128)S(1)}, f32[2048,2,128]{2,0,1:T(8,128)}) %tuple.178, (s32[]{:T(128)}, s32[512,8,1]{1,0,2:T(8,128)S(1)}, ...), branch_computations={%region_34.34_spmd, %region_35.35_spmd} | conditional | flops 2707169280 | bytes 65056960 | solution.py:236
  392.3 20.4 %conditional.15 = (f32[512,2,128]{2,0,1:T(8,128)}, f32[1,2048,2,128]{3,1,2,0:T(8,128)S(1)}, f32[1,2048,2,128]{3,1,2,0:T(8,128)}) conditional(s32[]{:T(128)} %convert_element_type.268, (f32[512,2,128]{2,0,1:T(8,128)}, f32[2048,2,128]{2,0,1:T(8,128)S(1)}, f32[2048,2,128]{2,0,1:T(8,128)}) %tuple.178, (s32[]{:T(128)}, s32[512,8,1]{1,0,2:T(8,128)S(1)}, ...), branch_computations={%region_34.34_spmd, %region_35.35_spmd} | conditional | flops 2707169280 | bytes 65056960 | solution.py:236
  416.7 7.9 %copy.157 = bf16[4,2048,2,128]{1,0,3,2:T(4,128)(2,1)} copy(bf16[4,2048,2,128]{3,1,2,0:T(8,128)(2,1)} %get-tuple-element.423) | data formatting | bytes 8388608 | tf_op jit(solution)/shard_map/convert_element_type | solution.py:270
  424.7 8.6 %copy.195 = bf16[32,8,4,2048]{3,1,2,0:T(8,128)(2,1)} copy(bf16[32,8,4,2048]{3,2,1,0:T(4,128)(2,1)} %bitcast.300) | data formatting | bytes 8388608
  433.3 8.4 %copy.158 = bf16[4,2048,2,128]{3,2,1,0:T(2,128)(2,1)S(1)} copy(bf16[4,2048,2,128]{3,1,2,0:T(8,128)(2,1)} %get-tuple-element.424) | data formatting | bytes 8388608 | tf_op jit(solution)/shard_map/convert_element_type | solution.py:273
  486.2 34.2 %reduce-scatter.3.cloned.1.call-done = bf16[512,256]{0,1:T(8,128)(2,1)} async-done(((bf16[8192,256]{0,1:T(8,128)(2,1)}), bf16[512,256]{0,1:T(8,128)(2,1)}) %reduce-scatter.3.cloned.1.call-update) | async-done | bytes 262160 | tf_op jit(solution)/shard_map/reduce_scatter | solution.py:269
  521.7 21.7 %all-reduce.1 = (f32[512]{0:T(512)S(1)}, f32[512]{0:T(512)S(1)}, f32[512]{0:T(512)S(1)}, f32[512]{0:T(512)S(1)}) all-reduce(f32[512]{0:T(512)S(1)} %get-tuple-element.647, f32[512]{0:T(512)S(1)} %get-tuple-element.645, f32[512]{0:T(512)S(1)} %get-tuple-element.646, ...), channel_id=1, replica_groups=mesh['ctx'=16,'head'=8] {'head'}, use_global_device_ids=true, to_apply=%region_38.39 | all-reduce | flops 2048 | bytes 16384 | tf_op jit(solution)/shard_map/psum | solution.py:299
  550.0 38.8 %reduce-scatter.5.cloned.1.call-done = bf16[512,256]{1,0:T(8,128)(2,1)} async-done(((bf16[8192,256]{1,0:T(8,128)(2,1)}), bf16[512,256]{1,0:T(8,128)(2,1)}) %reduce-scatter.5.cloned.1.call-update) | async-done | bytes 262160 | tf_op jit(solution)/shard_map/reduce_scatter | solution.py:272
  (472 shorter events, 386.3 us)
Async XLA Ops:
  7.2 53.6 %copy-start.21 = (bf16[512,256]{1,0:T(8,128)(2,1)S(1)}, bf16[512,256]{1,0:T(8,128)(2,1)}, u32[]{:S(2)}) copy-start(bf16[512,256]{1,0:T(8,128)(2,1)} %param.24) | copy-start | bytes 786436
  7.2 53.6 %copy-start.19 = (bf16[512,256]{1,0:T(8,128)(2,1)S(1)}, bf16[512,256]{1,0:T(8,128)(2,1)}, u32[]{:S(2)}) copy-start(bf16[512,256]{1,0:T(8,128)(2,1)} %param.27) | copy-start | bytes 786436
  7.2 54.7 %copy-start.56 = (s32[2]{0:T(128)S(1)}, s32[2]{0:T(128)}, u32[]{:S(2)}) copy-start(s32[2]{0:T(128)} %param.34) | copy-start | bytes 28
  7.2 53.6 %copy-start.52 = (f32[256]{0:T(256)S(1)}, f32[256]{0:T(256)}, u32[]{:S(2)}) copy-start(f32[256]{0:T(256)} %param.30) | copy-start | bytes 3076
  7.2 61.8 %all-gather.5.cloned.1.call-start = ((), (), s32[]{:S(2)}) async-start(), calls=%async_computation.3 | async-start | bytes 4456448 | tf_op jit(solution)/shard_map/all_gather | solution.py:165
  7.9 82.4 %all-gather.3.cloned.1.call-start = ((), (), s32[]{:S(2)}) async-start(), calls=%async_computation.2 | async-start | bytes 4456448 | tf_op jit(solution)/shard_map/all_gather | solution.py:164
  9.1 52.0 %copy-start.13 = (bf16[512,256]{0,1:T(8,128)(2,1)}, bf16[512,256]{0,1:T(8,128)(2,1)S(1)}, u32[]{:S(2)}) copy-start(bf16[512,256]{0,1:T(8,128)(2,1)S(1)} %copy.120) | copy-start | bytes 786436
  10.3 50.8 %copy-start.15 = (bf16[512,256]{0,1:T(8,128)(2,1)}, bf16[512,256]{0,1:T(8,128)(2,1)S(1)}, u32[]{:S(2)}) copy-start(bf16[512,256]{0,1:T(8,128)(2,1)S(1)} %copy.126) | copy-start | bytes 786436
  36.4 32.7 %copy-start.40 = (f32[512]{0:T(512)}, f32[512]{0:T(512)S(1)}, u32[]{:S(2)}) copy-start(f32[512]{0:T(512)S(1)} %get-tuple-element.785) | copy-start | bytes 6148
  37.0 32.1 %copy-start.42 = (f32[512]{0:T(512)}, f32[512]{0:T(512)S(1)}, u32[]{:S(2)}) copy-start(f32[512]{0:T(512)S(1)} %get-tuple-element.783) | copy-start | bytes 6148
  38.5 481.9 %reduce-scatter.3.cloned.1.call-start = ((), (), s32[]{:S(2)}) async-start(), calls=%async_computation.4 | async-start | bytes 4456448 | tf_op jit(solution)/shard_map/reduce_scatter | solution.py:269
  107.0 114.0 %copy-start.35 = (bf16[256,256]{0,1:T(8,128)(2,1)S(1)}, bf16[256,256]{0,1:T(8,128)(2,1)}, u32[]{:S(2)}) copy-start(bf16[256,256]{0,1:T(8,128)(2,1)} %copy.135) | copy-start | bytes 393220
  433.3 155.5 %reduce-scatter.5.cloned.1.call-start = ((), (), s32[]{:S(2)}) async-start(), calls=%async_computation.5 | async-start | bytes 4456448 | tf_op jit(solution)/shard_map/reduce_scatter | solution.py:272
  473.4 47.0 %copy-start.14 = (bf16[512,256]{0,1:T(8,128)(2,1)S(1)}, bf16[512,256]{0,1:T(8,128)(2,1)}, u32[]{:S(2)}) copy-start(bf16[512,256]{0,1:T(8,128)(2,1)} %copy-done.13) | copy-start | bytes 786436
  473.4 47.0 %copy-start.16 = (bf16[512,256]{0,1:T(8,128)(2,1)S(1)}, bf16[512,256]{0,1:T(8,128)(2,1)}, u32[]{:S(2)}) copy-start(bf16[512,256]{0,1:T(8,128)(2,1)} %copy-done.15) | copy-start | bytes 786436
  473.5 47.0 %copy-start.51 = (f32[256]{0:T(256)S(1)}, f32[256]{0:T(256)}, u32[]{:S(2)}) copy-start(f32[256]{0:T(256)} %param.31) | copy-start | bytes 3076
  474.5 68.9 %copy-start.45 = (f32[512]{0:T(512)S(1)}, f32[512]{0:T(512)}, u32[]{:S(2)}) copy-start(f32[512]{0:T(512)} %copy-done.44) | copy-start | bytes 6148
  474.5 69.0 %copy-start.47 = (f32[512]{0:T(512)S(1)}, f32[512]{0:T(512)}, u32[]{:S(2)}) copy-start(f32[512]{0:T(512)} %copy-done.46) | copy-start | bytes 6148
  477.5 71.0 %copy-start.22 = (bf16[512,256]{1,0:T(8,128)(2,1)S(1)}, bf16[512,256]{1,0:T(8,128)(2,1)}, u32[]{:S(2)}) copy-start(bf16[512,256]{1,0:T(8,128)(2,1)} %param.24) | copy-start | bytes 786436
  477.5 71.0 %copy-start.41 = (f32[512]{0:T(512)S(1)}, f32[512]{0:T(512)}, u32[]{:S(2)}) copy-start(f32[512]{0:T(512)} %copy-done.40) | copy-start | bytes 6148
  477.5 71.0 %copy-start.43 = (f32[512]{0:T(512)S(1)}, f32[512]{0:T(512)}, u32[]{:S(2)}) copy-start(f32[512]{0:T(512)} %copy-done.42) | copy-start | bytes 6148
  477.5 71.0 %copy-start.53 = (f32[256]{0:T(256)S(1)}, f32[256]{0:T(256)}, u32[]{:S(2)}) copy-start(f32[256]{0:T(256)} %param.30) | copy-start | bytes 3076
  477.6 71.0 %copy-start.54 = (f32[512]{0:T(512)S(1)}, f32[512]{0:T(512)}, u32[]{:S(2)}) copy-start(f32[512]{0:T(512)} %get-tuple-element.786) | copy-start | bytes 6148
  477.6 71.0 %copy-start.55 = (f32[512]{0:T(512)S(1)}, f32[512]{0:T(512)}, u32[]{:S(2)}) copy-start(f32[512]{0:T(512)} %get-tuple-element.784) | copy-start | bytes 6148
  (68 other events, 418.2 us)
Sparse Core Ops, SparseCore 0:
  9.8 40.9 all-gather.4
  52.9 37.3 all-gather.2
  433.4 86.9 reduce-scatter.2
  522.7 66.0 reduce-scatter.4
where the time goes:
time: 609 us; the launch traced here: 597 us
  local copies, waits for them, and re-layouts  178 us (29%)
  matrix products  138 us (23%)
  other arithmetic  99.1 us (16%)
  waiting for transfers between devices  83.4 us (14%)
  blocking collectives  57.8 us (9%)
  loops' own time  25.6 us (4%)
  between operations  15.6 us (3%)
    unnamed x104, local copies, waits for them, and re-layouts  38.9 us
    reduce_scatter x1, waiting for transfers between devices, local(): lax.psum_scatter(value_all.astype(jnp.bfloat16), 'ctx', scatter_dimension...  38.8 us
    reduce_scatter x1, waiting for transfers between devices, local(): lax.psum_scatter(key_all.astype(jnp.bfloat16), 'ctx', scatter_dimension=0...  34.2 us
    dot_general x8, matrix products, backward_tile(): jnp.einsum('hqk,qhd->khd', probability.astype(jnp.bfloat16), grad_rows, p...  33.1 us
    reduce_or x8, other arithmetic, clean_mask(): tile_live = jnp.any(same_doc & (key_blocks <= my_blocks[pair_slot]))  30.4 us
    dot_general x8, matrix products, backward_tile(): jnp.einsum('qhd,khd->hqk', grad_rows, value_rows, preferred_element_type=...  28.9 us
    psum x1, blocking collectives, local(): lax.psum((jnp.sum(raw_cq * raw_cq, axis=1), jnp.sum(raw_ck * raw_ck, axis...  23 us
    dot_general x8, matrix products, forward_tile(): jnp.einsum('hqk,khd->qhd', weights.astype(jnp.bfloat16), value_rows, pref...  22 us
  transfers between devices with their start and end apart: 4, of which 3 were waited for; matrix products, arithmetic and copies ran while one was open for 16% of the time, Pallas kernels for 0%

commit v1 on v0

v1 whole, which is shorter than its diff:
```python
import math

import jax
import jax.numpy as jnp
from jax import lax
from jax.experimental import pallas as pl
from jax.experimental.pallas import tpu as pltpu
from jax.sharding import PartitionSpec as P

HD = 128
BLK = 256
FEAT = 2048
EPSILON = 1e-06
NEGATIVE = -1e30
MESH = pl.DeviceIdType.MESH
F32 = jnp.float32
BF16 = jnp.bfloat16
VMEM = pl.BlockSpec(memory_space=pltpu.VMEM)
SMEM = pl.BlockSpec(memory_space=pltpu.SMEM)
ANY = pl.BlockSpec(memory_space=pl.ANY)
LAST = (((1,), (1,)), ((), ()))
FIRST = (((0,), (0,)), ((), ()))
PLAIN = (((1,), (0,)), ((), ()))
PACKET = 528


def dot(a, b, dims):
    return lax.dot_general(a, b, dims, preferred_element_type=F32)


def row_sums(products):
    high = products.astype(BF16)
    low = (products - high.astype(F32)).astype(BF16)
    ones = jnp.ones((8, products.shape[1]), BF16)
    return dot(ones, high, LAST) + dot(ones, low, LAST)


def place():
    ctx = lax.axis_index("ctx")
    head = lax.axis_index("head")
    core = ctx % 2
    y = (ctx // 2) % 2
    x = ctx // 4
    return ctx, head, core, y, x


def ctx_of(x, y, core):
    return (x * 2 + y) * 2 + core


def chip_of(x, y):
    return x * 2 + y


class Copies:
    def __init__(self, send, recv, head):
        self.send, self.recv, self.head = send, recv, head
        self.started = []
        self.count = 0

    def start(self, src, dst, ctx, head=None):
        copy = pltpu.make_async_remote_copy(
            src_ref=src,
            dst_ref=dst,
            send_sem=self.send.at[self.count],
            recv_sem=self.recv.at[self.count],
            device_id={"ctx": ctx, "head": self.head if head is None else head},
            device_id_type=MESH,
        )
        self.count += 1
        copy.start()
        self.started.append(copy)
        return copy


class Locals:
    def __init__(self, sems):
        self.sems = sems
        self.count = 0

    def start(self, src, dst):
        copy = pltpu.make_async_copy(src, dst, self.sems.at[self.count])
        self.count += 1
        copy.start()
        return copy


def enter(ctx, head, core, y, x):
    barrier = pltpu.get_barrier_semaphore()
    right, left = (x + 1) % 4, (x + 3) % 4
    for other in (
        ctx_of(x, y, 1 - core),
        ctx_of(x, 1 - y, core),
        ctx_of(right, y, core),
        ctx_of(left, y, core),
    ):
        pl.semaphore_signal(barrier, inc=1, device_id={"ctx": other, "head": head}, device_id_type=MESH)
    for step in range(1, 8):
        pl.semaphore_signal(
            barrier, inc=1, device_id={"ctx": ctx, "head": (head + step) % 8}, device_id_type=MESH
        )
    pl.semaphore_wait(barrier, 11)


def gather_kernel(
    cq, ck, nq, nk, qg, kg, cv, nv, gc, gn, owned,
    kall, vall, loc, inv_out, ids_out,
    normed, id_rows, id_all, sums, send, recv, lsem,
):
    ctx, head, core, y, x = place()
    right, left = (x + 1) % 4, (x + 3) % 4
    mine = pl.ds(pl.multiple_of(core * HD, HD), HD)
    theirs = pl.ds(pl.multiple_of((1 - core) * HD, HD), HD)
    partner = ctx_of(x, y, 1 - core)
    lane = lax.broadcasted_iota(jnp.int32, (16, HD), 1)
    id_rows[...] = jnp.where(lane == 0, owned[0], owned[1]).astype(F32).astype(BF16)
    enter(ctx, head, core, y, x)
    remote = Copies(send, recv, head)
    local = Locals(lsem)

    own_v = vall.at[ctx, pl.ds(0, 512)]
    own_i = vall.at[ctx, pl.ds(512, 16)]
    v_swap = [remote.start(cv.at[:, theirs], own_v, partner), remote.start(id_rows, own_i, partner)]
    v_own = [local.start(cv.at[:, mine], own_v), local.start(id_rows, own_i)]

    row = lax.broadcasted_iota(jnp.int32, (8, 512), 0)
    total = jnp.zeros((8, 512), F32)
    for index, ref in enumerate((cq, ck, nq, nk)):
        raw = ref[...].astype(F32)
        total = jnp.where(row == index, row_sums(raw * raw), total)
    sums[0] = total
    exchange = [
        remote.start(sums.at[0], sums.at[step], ctx, (head + step) % 8) for step in range(1, 8)
    ]

    for copy in v_own:
        copy.wait()
    for copy in v_swap:
        copy.wait_recv()

    def slot(buf, sx, sy):
        return buf.at[pl.ds(2 * chip_of(sx, sy), 2)]

    def part(buf, sx, sy, half):
        return buf.at[2 * chip_of(sx, sy) + half]

    def to(px, py):
        return ctx_of(px, py, core)

    def spread(buf, sx, sy, px, py):
        view = slot(buf, sx, sy)
        return remote.start(view, view, to(px, py))

    def spread_part(buf, sx, sy, half, px, py):
        view = part(buf, sx, sy, half)
        return remote.start(view, view, to(px, py))

    v_right = spread(vall, x, y, right, y)
    v_left = spread(vall, x, y, left, y)
    v_y = [spread(vall, x, y, x, 1 - y)]

    late = []
    for index, ref in ((3, nv), (4, gc), (5, gn)):
        late.append(remote.start(ref.at[:, theirs], loc.at[index, core], partner))
    late_own = [
        local.start(ref.at[:, mine], loc.at[index, core]) for index, ref in ((3, nv), (4, gc), (5, gn))
    ]

    for copy in exchange:
        copy.wait_recv()
    total = sums[0]
    for step in range(1, 8):
        total = total + sums[step]
    inverse = lax.rsqrt(total / FEAT + EPSILON)
    inv_out[...] = inverse
    columns = jnp.transpose(inverse)

    def normalize(index, ref, gain, where):
        normed[where] = (ref[...].astype(F32) * columns[:, index : index + 1] * gain[...]).astype(BF16)

    normalize(1, ck, kg, 0)
    k_swap = remote.start(normed.at[0, :, theirs], kall.at[ctx], partner)
    k_own = local.start(normed.at[0, :, mine], kall.at[ctx])
    normalize(0, cq, qg, 1)
    normalize(2, nq, qg, 2)
    normalize(3, nk, kg, 3)
    k_own.wait()
    k_swap.wait_recv()
    k_y = spread(kall, x, y, x, 1 - y)
    k_right = [spread(kall, x, y, right, y)]
    k_left = [spread(kall, x, y, left, y)]
    for index in range(3):
        late.append(remote.start(normed.at[index + 1, :, theirs], loc.at[index, core], partner))
        late_own.append(local.start(normed.at[index + 1, :, mine], loc.at[index, core]))

    v_right.wait_recv()
    v_half = [spread_part(vall, left, y, 0, right, y)]
    v_y.append(spread(vall, left, y, x, 1 - y))
    v_left.wait_recv()
    v_half.append(spread_part(vall, right, y, 1, left, y))
    v_y.append(spread(vall, right, y, x, 1 - y))
    k_y.wait_recv()
    k_right.append(spread(kall, x, 1 - y, right, y))
    k_left.append(spread(kall, x, 1 - y, left, y))
    k_half = []
    opposite = (x + 2) % 4
    k_right[0].wait_recv()
    k_half.append(spread_part(kall, left, y, 0, right, y))
    k_left[0].wait_recv()
    k_half.append(spread_part(kall, right, y, 1, left, y))
    v_half[0].wait_recv()
    v_y.append(spread_part(vall, opposite, y, 0, x, 1 - y))
    v_half[1].wait_recv()
    v_y.append(spread_part(vall, opposite, y, 1, x, 1 - y))
    k_right[1].wait_recv()
    k_half.append(spread_part(kall, left, 1 - y, 0, right, y))
    k_left[1].wait_recv()
    k_half.append(spread_part(kall, right, 1 - y, 1, left, y))

    for copy in late_own:
        copy.wait()
    for copy in late + v_y + k_half:
        copy.wait_recv()
    gathered = local.start(vall.at[:, pl.ds(512, 16)], id_all)
    gathered.wait()
    ids_out[...] = jnp.max(id_all[...].astype(F32), axis=1).astype(jnp.int32)
    for copy in remote.started:
        copy.wait_send()


def gather_call(cq, ck, nq, nk, qg, kg, cv, nv, gc, gn, owned):
    return pl.pallas_call(
        gather_kernel,
        name="gather_keys",
        out_shape=(
            jax.ShapeDtypeStruct((16, 512, HD), BF16),
            jax.ShapeDtypeStruct((16, PACKET, HD), BF16),
            jax.ShapeDtypeStruct((6, 2, 512, HD), BF16),
            jax.ShapeDtypeStruct((8, 512), F32),
            jax.ShapeDtypeStruct((16, HD), jnp.int32),
        ),
        in_specs=[VMEM] * 6 + [ANY] * 4 + [SMEM],
        out_specs=(ANY, ANY, ANY, VMEM, VMEM),
        scratch_shapes=[
            pltpu.VMEM((4, 512, 256), BF16),
            pltpu.VMEM((16, HD), BF16),
            pltpu.VMEM((16, 16, HD), BF16),
            pltpu.VMEM((8, 8, 512), F32),
            pltpu.SemaphoreType.DMA((40,)),
            pltpu.SemaphoreType.DMA((40,)),
            pltpu.SemaphoreType.DMA((16,)),
        ],
        compiler_params=pltpu.CompilerParams(
            collective_id=0, has_side_effects=True, vmem_limit_bytes=48 * 2**20
        ),
    )(cq, ck, nq, nk, qg, kg, cv, nv, gc, gn, owned)


def attention_kernel(
    ids, docs, loc, kall, vall,
    res, dkp, dvp,
    where_is, first_of, weights, dk_acc, dv_acc, out_acc, dq_acc,
):
    ctx = lax.axis_index("ctx")
    chip = ctx // 2
    scale = 1.0 / math.sqrt(HD)
    scale2 = scale * math.log2(math.e)

    @pl.loop(0, 16)
    def _(packet):
        where_is[ids[packet, 0]] = packet * 2
        where_is[ids[packet, 1]] = packet * 2 + 1

    first_of[0] = 0

    @pl.loop(1, 32)
    def _(block):
        first_of[block] = jnp.where(docs[block] == docs[block - 1], first_of[block - 1], block)

    @pl.loop(0, 32)
    def _(block):
        dk_acc[block] = jnp.zeros((BLK, HD), F32)
        dv_acc[block] = jnp.zeros((BLK, HD), F32)

    def key_rows(buf, stored):
        start = pl.multiple_of((stored % 2) * BLK, BLK)
        return buf[stored // 2, pl.ds(start, BLK), :]

    def tops(scores):
        return jnp.max(scores.reshape(BLK // 8, 8, scores.shape[1]), axis=0)

    def totals(values):
        return jnp.sum(values.reshape(BLK // 8, 8, values.shape[1]), axis=0)

    @pl.loop(0, 4)
    def _(index):
        stored_own = chip * 4 + index
        side = index // 2
        block = ids[chip * 2 + side, index % 2]
        rows = pl.ds(pl.multiple_of((index % 2) * BLK, BLK), BLK)
        begin = first_of[block]
        count = block - begin
        query_clean = loc[0, side, rows, :]
        query_noisy = loc[1, side, rows, :]
        key_noisy = loc[2, side, rows, :]
        value_noisy = loc[3, side, rows, :]
        grad_clean = loc[4, side, rows, :]
        grad_noisy = loc[5, side, rows, :]
        queries = jnp.concatenate([query_clean, query_noisy], axis=0)
        grads = jnp.concatenate([grad_clean, grad_noisy], axis=0)
        key_own = key_rows(kall, stored_own)
        value_own = key_rows(vall, stored_own)

        own_scores = jnp.concatenate(
            [dot(key_own, query_clean, LAST), dot(key_noisy, query_noisy, LAST)], axis=1
        )
        weights[0] = own_scores

        def score_step(step, peak):
            keys = key_rows(kall, where_is[begin + step])
            scores = dot(keys, queries, LAST)
            weights[step + 1] = scores
            return jnp.maximum(peak, tops(scores))

        peak = lax.fori_loop(0, count, score_step, tops(own_scores))
        peak = jnp.max(peak, axis=0, keepdims=True) * scale2

        own = jnp.exp2(weights[0] * scale2 - peak)
        weights[0] = own
        own_low = own.astype(BF16)
        out_acc[...] = jnp.concatenate(
            [
                dot(value_own, own_low[:, :BLK], FIRST),
                dot(value_noisy, own_low[:, BLK:], FIRST),
            ],
            axis=1,
        )

        def value_step(step, total):
            values = key_rows(vall, where_is[begin + step])
            weight = jnp.exp2(weights[step + 1] * scale2 - peak)
            weights[step + 1] = weight
            out_acc[...] += dot(values, weight.astype(BF16), FIRST)
            return total + totals(weight)

        total = lax.fori_loop(0, count, value_step, totals(own))
        inverse_total = 1.0 / jnp.sum(total, axis=0, keepdims=True)
        out = out_acc[...] * inverse_total
        grads_t = jnp.transpose(grads.astype(F32))
        delta = jnp.sum(out * grads_t, axis=0, keepdims=True)
        out_rows = jnp.transpose(out)
        res[0, side, rows, :] = out_rows[:BLK]
        res[1, side, rows, :] = out_rows[BLK:]

        own = weights[0] * inverse_total
        own_low = own.astype(BF16)
        own_dp = jnp.concatenate(
            [dot(value_own, grad_clean, LAST), dot(value_noisy, grad_noisy, LAST)], axis=1
        )
        own_ds = (own * (own_dp - delta)).astype(BF16)
        dv_acc[stored_own] += dot(own_low[:, :BLK], grad_clean, PLAIN)
        dk_acc[stored_own] += dot(own_ds[:, :BLK], query_clean, PLAIN)
        res[5, side, rows, :] = dot(own_low[:, BLK:], grad_noisy, PLAIN)
        res[4, side, rows, :] = dot(own_ds[:, BLK:], query_noisy, PLAIN) * scale
        dq_acc[...] = jnp.concatenate(
            [dot(key_own, own_ds[:, :BLK], FIRST), dot(key_noisy, own_ds[:, BLK:], FIRST)], axis=1
        )

        @pl.loop(0, count)
        def _(step):
            stored = where_is[begin + step]
            keys = key_rows(kall, stored)
            values = key_rows(vall, stored)
            probs = weights[step + 1] * inverse_total
            dv_acc[stored] += dot(probs.astype(BF16), grads, PLAIN)
            dp = dot(values, grads, LAST)
            ds = (probs * (dp - delta)).astype(BF16)
            dk_acc[stored] += dot(ds, queries, PLAIN)
            dq_acc[...] += dot(keys, ds, FIRST)

        dq_rows = jnp.transpose(dq_acc[...] * scale)
        res[2, side, rows, :] = dq_rows[:BLK]
        res[3, side, rows, :] = dq_rows[BLK:]

    @pl.loop(0, 32)
    def _(stored):
        start = pl.multiple_of((stored % 2) * BLK, BLK)
        dkp[stored // 4, (stored // 2) % 2, pl.ds(start, BLK), :] = (dk_acc[stored] * scale).astype(BF16)
        dvp[stored // 4, (stored // 2) % 2, pl.ds(start, BLK), :] = dv_acc[stored].astype(BF16)


def attention_call(ids, docs, loc, kall, vall):
    return pl.pallas_call(
        attention_kernel,
        name="attention",
        out_shape=(
            jax.ShapeDtypeStruct((6, 2, 512, HD), F32),
            jax.ShapeDtypeStruct((8, 2, 512, HD), BF16),
            jax.ShapeDtypeStruct((8, 2, 512, HD), BF16),
        ),
        in_specs=[SMEM, SMEM, VMEM, VMEM, VMEM],
        out_specs=(VMEM, VMEM, VMEM),
        scratch_shapes=[
            pltpu.SMEM((32,), jnp.int32),
            pltpu.SMEM((32,), jnp.int32),
            pltpu.VMEM((17, BLK, 2 * BLK), F32),
            pltpu.VMEM((32, BLK, HD), F32),
            pltpu.VMEM((32, BLK, HD), F32),
            pltpu.VMEM((HD, 2 * BLK), F32),
            pltpu.VMEM((HD, 2 * BLK), F32),
        ],
        compiler_params=pltpu.CompilerParams(vmem_limit_bytes=56 * 2**20),
    )(ids, docs, loc, kall, vall)


def scatter_kernel(
    cq, ck, nq, nk, qg, kg, res, dkp, dvp,
    back, fin, inner_out,
    va, vy, vh, vx, ka, kh, kx, ks, ky, sums, ksums, send, recv, lsem,
):
    ctx, head, core, y, x = place()
    right, left = (x + 1) % 4, (x + 3) % 4
    partner = ctx_of(x, y, 1 - core)
    to_right, to_left = ctx_of(right, y, core), ctx_of(left, y, core)
    to_y = ctx_of(x, 1 - y, core)
    enter(ctx, head, core, y, x)
    remote = Copies(send, recv, head)
    local = Locals(lsem)

    def chip(step, row):
        return chip_of((x + step) % 4, y if row == 0 else 1 - y)

    v_y = {}
    k_half = {}
    v_y[2] = remote.start(dvp.at[chip(2, 1)], vy.at[2], to_y)
    for row in (1, 0):
        k_half[row, 0] = remote.start(dkp.at[chip(2, row), 0], kh.at[row, 0], to_left)
        k_half[row, 1] = remote.start(dkp.at[chip(2, row), 1], kh.at[row, 1], to_right)
    for step in (3, 1, 0):
        v_y[step] = remote.start(dvp.at[chip(step, 1)], vy.at[step], to_y)
    k_own = {}
    for row in (1, 0):
        for step in (3, 1, 0):
            k_own[row, step] = local.start(dkp.at[chip(step, row)], ka.at[row, step])
    v_own = {step: local.start(dvp.at[chip(step, 0)], va.at[step]) for step in (2, 3, 1, 0)}
    order = (2, 3, 4, 0, 1, 5)
    back_swap = {i: remote.start(res.at[i, 1 - core], back.at[i, core], partner) for i in order}
    back_own = {i: local.start(res.at[i, core], back.at[i, core]) for i in order}

    row = lax.broadcasted_iota(jnp.int32, (8, 512), 0)

    def inner(raw, gain, first, second):
        products = 0.0
        for half, values in ((0, first), (1, second)):
            columns = slice(half * HD, half * HD + HD)
            products = products + raw[:, columns].astype(F32) * (gain[:, columns] * values)
        return row_sums(products)

    for i in (2, 3, 4):
        back_own[i].wait()
        back_swap[i].wait_recv()
    total = jnp.zeros((8, 512), F32)
    for index, raw, gain, i in ((0, cq, qg, 2), (2, nq, qg, 3), (3, nk, kg, 4)):
        total = jnp.where(row == index, inner(raw, gain, back[i, 0], back[i, 1]), total)
    sums[0] = total
    exchange = [
        remote.start(sums.at[0], sums.at[step], ctx, (head + step) % 8) for step in range(1, 8)
    ]

    def add(target, other):
        target[...] = (target[...].astype(F32) + other[...].astype(F32)).astype(BF16)

    k_x = {}

    def k_forward(row):
        k_own[row, 3].wait()
        k_half[row, 0].wait_recv()
        add(ka.at[row, 3, 0], kh.at[row, 0])
        k_x[row, 0] = remote.start(ka.at[row, 3], kx.at[row, 0], to_left)
        k_own[row, 1].wait()
        k_half[row, 1].wait_recv()
        add(ka.at[row, 1, 1], kh.at[row, 1])
        k_x[row, 1] = remote.start(ka.at[row, 1], kx.at[row, 1], to_right)

    k_forward(1)
    v_own[2].wait()
    v_y[2].wait_recv()
    add(va.at[2], vy.at[2])
    v_half = [
        remote.start(va.at[2, 0], vh.at[0], to_left),
        remote.start(va.at[2, 1], vh.at[1], to_right),
    ]
    k_forward(0)
    k_own[1, 0].wait()
    k_x[1, 0].wait_recv()
    k_x[1, 1].wait_recv()
    ks[...] = (ka[1, 0].astype(F32) + kx[1, 0].astype(F32) + kx[1, 1].astype(F32)).astype(BF16)
    k_y = remote.start(ks, ky, to_y)

    v_own[3].wait()
    v_y[3].wait_recv()
    add(va.at[3], vy.at[3])
    v_half[0].wait_recv()
    add(va.at[3, 0], vh.at[0])
    v_x = [remote.start(va.at[3], vx.at[0], to_left)]
    v_own[1].wait()
    v_y[1].wait_recv()
    add(va.at[1], vy.at[1])
    v_half[1].wait_recv()
    add(va.at[1, 1], vh.at[1])
    v_x.append(remote.start(va.at[1], vx.at[1], to_right))

    k_own[0, 0].wait()
    k_x[0, 0].wait_recv()
    k_x[0, 1].wait_recv()
    k_y.wait_recv()

    def finish(index, terms):
        values = [
            sum(term[half].astype(F32) for term in terms[1:]) + terms[0][half].astype(F32)
            for half in range(2)
        ]
        first_core = core == 0
        fin[index, core] = jnp.where(first_core, values[0], values[1])
        away[index] = jnp.where(first_core, values[1], values[0])
        return remote.start(away.at[index], fin.at[index, core], partner)

    away = ksums
    k_fin = finish(0, (ka.at[0, 0], kx.at[0, 0], kx.at[0, 1], ky))
    k_fin.wait_recv()
    sums[8] = inner(ck, kg, fin[0, 0], fin[0, 1])
    k_exchange = [
        remote.start(sums.at[8], sums.at[8 + step], ctx, (head + step) % 8) for step in range(1, 8)
    ]
    v_own[0].wait()
    v_y[0].wait_recv()
    v_x[0].wait_recv()
    v_x[1].wait_recv()
    v_fin = finish(1, (va.at[0], vy.at[0], vx.at[0], vx.at[1]))

    for copy in exchange + k_exchange:
        copy.wait_recv()
    total = sums[0]
    k_total = sums[8]
    for step in range(1, 8):
        total = total + sums[step]
        k_total = k_total + sums[8 + step]
    inner_out[...] = jnp.where(row == 1, k_total, total)
    v_fin.wait_recv()
    for i in (0, 1, 5):
        back_own[i].wait()
        back_swap[i].wait_recv()
    for copy in remote.started:
        copy.wait_send()


def scatter_call(cq, ck, nq, nk, qg, kg, res, dkp, dvp):
    return pl.pallas_call(
        scatter_kernel,
        name="scatter_grads",
        out_shape=(
            jax.ShapeDtypeStruct((6, 2, 512, HD), F32),
            jax.ShapeDtypeStruct((2, 2, 512, HD), F32),
            jax.ShapeDtypeStruct((8, 512), F32),
        ),
        in_specs=[VMEM] * 6 + [ANY] * 3,
        out_specs=(VMEM, VMEM, VMEM),
        scratch_shapes=[
            pltpu.VMEM((4, 2, 512, HD), BF16),
            pltpu.VMEM((4, 2, 512, HD), BF16),
            pltpu.VMEM((2, 512, HD), BF16),
            pltpu.VMEM((2, 2, 512, HD), BF16),
            pltpu.VMEM((2, 4, 2, 512, HD), BF16),
            pltpu.VMEM((2, 2, 512, HD), BF16),
            pltpu.VMEM((2, 2, 2, 512, HD), BF16),
            pltpu.VMEM((2, 512, HD), BF16),
            pltpu.VMEM((2, 512, HD), BF16),
            pltpu.VMEM((16, 8, 512), F32),
            pltpu.VMEM((2, 512, HD), F32),
            pltpu.SemaphoreType.DMA((44,)),
            pltpu.SemaphoreType.DMA((44,)),
            pltpu.SemaphoreType.DMA((20,)),
        ],
        compiler_params=pltpu.CompilerParams(
            collective_id=1, has_side_effects=True, vmem_limit_bytes=56 * 2**20
        ),
    )(cq, ck, nq, nk, qg, kg, res, dkp, dvp)


def finish_kernel(
    cq, ck, nq, nk, qg, kg, inv, inner, back, fin,
    out_clean, out_noisy, dq_clean, dk_clean, dv_clean, dq_noisy, dk_noisy, dv_noisy,
):
    inverse = jnp.transpose(inv[...])
    means = jnp.transpose(inner[...]) / FEAT
    for half in range(2):
        columns = slice(half * HD, half * HD + HD)
        out_clean[:, columns] = back[0, half]
        out_noisy[:, columns] = back[1, half]
        dv_noisy[:, columns] = back[5, half]
        dv_clean[:, columns] = fin[1, half]
        for index, raw, gain, grad, target in (
            (0, cq, qg, back[2, half], dq_clean),
            (1, ck, kg, fin[0, half], dk_clean),
            (2, nq, qg, back[3, half], dq_noisy),
            (3, nk, kg, back[4, half], dk_noisy),
        ):
            scale = inverse[:, index : index + 1]
            factor = scale * scale * scale * means[:, index : index + 1]
            target[:, columns] = scale * (gain[:, columns] * grad) - raw[:, columns].astype(F32) * factor


def finish_call(cq, ck, nq, nk, qg, kg, inv, inner, back, fin):
    rows = 128
    wide = pl.BlockSpec((rows, 256), lambda i: (i, 0))
    gain = pl.BlockSpec((1, 256), lambda i: (0, 0))
    stat = pl.BlockSpec((8, rows), lambda i: (0, i))
    return pl.pallas_call(
        finish_kernel,
        name="finish",
        grid=(512 // rows,),
        out_shape=tuple(jax.ShapeDtypeStruct((512, 256), F32) for _ in range(8)),
        in_specs=[wide] * 4
        + [gain] * 2
        + [stat] * 2
        + [
            pl.BlockSpec((6, 2, rows, HD), lambda i: (0, 0, i, 0)),
            pl.BlockSpec((2, 2, rows, HD), lambda i: (0, 0, i, 0)),
        ],
        out_specs=tuple([wide] * 8),
        compiler_params=pltpu.CompilerParams(vmem_limit_bytes=32 * 2**20),
    )(cq, ck, nq, nk, qg, kg, inv, inner, back, fin)


def local(
    clean_q, clean_k, clean_v, noisy_q, noisy_k, noisy_v,
    q_gain, k_gain, grad_clean, grad_noisy, owned_blocks, block_doc,
):
    qg = q_gain.reshape(1, 256)
    kg = k_gain.reshape(1, 256)
    raws = (clean_q, clean_k, noisy_q, noisy_k, qg, kg)
    kall, vall, loc, inv, ids = gather_call(
        *raws, clean_v, noisy_v, grad_clean, grad_noisy, owned_blocks
    )
    res, dkp, dvp = attention_call(ids, block_doc, loc, kall, vall)
    back, fin, inner = scatter_call(*raws, res, dkp, dvp)
    return finish_call(*raws, inv, inner, back, fin)


def solution(mesh):
    placed = (P("ctx", "head"),) * 6 + (P("head"),) * 2 + (P("ctx", "head"),) * 2 + (P("ctx"), P())
    return jax.shard_map(
        local,
        mesh=mesh,
        in_specs=placed,
        out_specs=(P("ctx", "head"),) * 8,
        check_vma=False,
    )
```

time: 609 us -> 161 us (0.26); the launches traced: 597 us -> 160 us
  local copies, waits for them, and re-layouts: 178 us -> 16.6 us
  Pallas kernels: 0 us -> 143 us
  matrix products: 138 us -> 0 us
  other arithmetic: 99.1 us -> 0 us
  waiting for transfers between devices: 83.4 us -> 0 us
  blocking collectives: 57.8 us -> 0 us
  loops' own time: 25.6 us -> 0 us
  between operations: 15.6 us -> 0.77 us
    pallas_call x0 -> x4, Pallas kernels: none -> 143 us  [the longest x1 64.4 us: scatter_call(): pl.pallas_call(scatter_kernel, name='scatter_grads', out_shape=(jax.Shape...]
    dot_general x54 -> x0, matrix products: 138 us -> none  [the longest x8 33.1 us: backward_tile(): jnp.einsum('hqk,qhd->khd', probability.astype(jnp.bfloat16), grad_rows, p...]
    reduce_scatter x2 -> x0, waiting for transfers between devices: 73 us -> none  [the longest x1 38.8 us: local(): lax.psum_scatter(value_all.astype(jnp.bfloat16), 'ctx', scatter_dimension...]
    psum x2 -> x0, blocking collectives: 44.7 us -> none  [the longest x1 23 us: local(): lax.psum((jnp.sum(raw_cq * raw_cq, axis=1), jnp.sum(raw_ck * raw_ck, axis...]
    reduce_sum x23 -> x0, other arithmetic: 33.3 us -> none  [the longest x7 18.9 us: forward_tile(): row_total = row_total * factor + jnp.sum(weights, axis=2)]
    reduce_or x8 -> x0, other arithmetic: 30.4 us -> none  [clean_mask(): tile_live = jnp.any(same_doc & (key_blocks <= my_blocks[pair_slot]))]
    another operation x18 -> x0, loops' own time: 25.6 us -> none  [the longest x1 18.6 us: local(): lax.scan(returned_advance, dq_pairs, (key_rows, value_rows, block_ids))]
    squeeze x16 -> x0, local copies, waits for them, and re-layouts: 23.5 us -> none  [the longest x8 17.5 us: local(): lax.scan(forward_advance, states, (key_rows, value_rows, block_ids))]
  transfers between devices with their start and end apart: 4 -> 0, of which waited for: 3 -> 0; matrix products, arithmetic and copies ran while one was open for 16% -> 0% of each run, Pallas kernels for 0% -> 0%
where the time goes in v1:
time: 161 us; the launch traced here: 160 us
  Pallas kernels  143 us (89%)
  local copies, waits for them, and re-layouts  16.6 us (10%)
    pallas_call x1, Pallas kernels, scatter_call(): pl.pallas_call(scatter_kernel, name='scatter_grads', out_shape=(jax.Shape...  64.4 us
    pallas_call x1, Pallas kernels, gather_call(): pl.pallas_call(gather_kernel, name='gather_keys', out_shape=(jax.ShapeDty...  42.3 us
    pallas_call x1, Pallas kernels, attention_call(): pl.pallas_call(attention_kernel, name='attention', out_shape=(jax.ShapeDt...  33.1 us
    unnamed x46, local copies, waits for them, and re-layouts  16.6 us

profile of v1, /device:TPU:1, one launch (start us, length us, event | category | flops | bytes accessed | tf_op | source)
XLA Modules:
  0.0 160.3 jit_solution(12832459128530591430)
XLA Ops:
  0.6 0.0 copy-start.1
  0.6 0.9 copy-done.1
  1.6 0.9 copy-done.3
  2.5 0.9 copy-done.5
  3.5 0.9 copy-done.7
  4.4 0.9 copy-done.12
  5.4 0.9 copy-done.13
  6.3 0.9 copy-done.14
  7.3 0.9 copy-done.15
  8.2 0.7 copy-done.17
  8.9 0.7 copy-done.19
  9.6 0.7 copy-done.22
  10.3 42.3 %gather_keys.1 = (bf16[16,512,128]{2,1,0:T(8,128)(2,1)S(1)}, bf16[16,528,128]{2,1,0:T(8,128)(2,1)}, bf16[6,2,512,128]{3,2,1,0:T(8,128)(2,1)S(1)}, f32[8,512]{1,0:T(8,128)S(1)}, s32[16,128]{1,0:T(8,128)S(1)}) custom-call(bf16[512,256]{1,0:T(8,128)(2,1)S(1)} %copy-done.1, bf16[512,256]{1,0:T(8,128)(2,1)S(1)} %copy-done.3, bf16[512,256]{1,0:T(8,128)(2,1)S(1)} %copy-done.5, ...), custom_call_target="tpu_custom_call" | custom-call | tf_op jit(solution)/shard_map/gather_keys/pallas_call | solution.py:232
  52.5 1.3 copy-done.9
  53.8 1.2 copy-done.10
  55.1 0.6 copy-done.21
  55.7 33.1 %attention.1 = (f32[6,2,512,128]{3,2,1,0:T(8,128)}, bf16[8,2,512,128]{3,2,1,0:T(8,128)(2,1)}, bf16[8,2,512,128]{3,2,1,0:T(8,128)(2,1)}) custom-call(s32[16,128]{1,0:T(8,128)} %copy-done.21, s32[32]{0:T(128)} %docs.1, bf16[6,2,512,128]{3,2,1,0:T(8,128)(2,1)} %copy-done.10, bf16[16,512,128]{2,1,0:T(8,128)(2,1)} %copy-done.9, ...), custom_call_target="tpu_custom_call" | custom-call | tf_op jit(solution)/shard_map/attention/pallas_call | solution.py:393
  88.7 0.0 copy-start.8
  88.8 0.0 copy-start.20
  88.8 64.4 %scatter_grads.1 = (f32[6,2,512,128]{3,2,1,0:T(8,128)}, f32[2,2,512,128]{3,2,1,0:T(8,128)}, f32[8,512]{1,0:T(8,128)}) custom-call(bf16[512,256]{1,0:T(8,128)(2,1)} %cq.5, bf16[512,256]{1,0:T(8,128)(2,1)} %ck.5, bf16[512,256]{1,0:T(8,128)(2,1)} %nq.5, bf16[512,256]{1,0:T(8,128)(2,1)} %nk.5, f32[1,256]{1,0:T(1,128)} %bitcast.2, f32[1,256]{1,0:T(1,128)} %bitcast.5, ...), custom_call_target="tpu_custom_call" | custom-call | tf_op jit(solution)/shard_map/scatter_grads/pallas_call | solution.py:558
  153.3 1.9 %copy-done = f32[6,2,512,128]{3,2,1,0:T(8,128)S(1)} copy-done((f32[6,2,512,128]{3,2,1,0:T(8,128)S(1)}, f32[6,2,512,128]{3,2,1,0:T(8,128)}, u32[]{:S(2)}) %copy-start) | copy-done | bytes 3145752
  155.1 1.2 copy-done.11
  156.4 0.7 copy-done.16
  157.1 3.2 %finish.1 = (f32[512,256]{1,0:T(8,128)}, f32[512,256]{1,0:T(8,128)}, f32[512,256]{1,0:T(8,128)}, f32[512,256]{1,0:T(8,128)}, f32[512,256]{1,0:T(8,128)}, /*index...) custom-call(bf16[512,256]{1,0:T(8,128)(2,1)S(1)} %copy-done.2, bf16[512,256]{1,0:T(8,128)(2,1)S(1)} %copy-done.4, ...), custom_call_target="tpu_custom_call" | custom-call | tf_op jit(solution)/shard_map/finish/pallas_call | solution.py:618
  (26 shorter events, 0.0 us)
Async XLA Ops:
  0.6 1.0 copy-start.1
  1.6 0.9 copy-start.3
  2.5 0.9 copy-start.5
  3.5 0.9 copy-start.7
  4.4 0.9 copy-start.12
  5.4 0.9 copy-start.13
  6.3 0.9 copy-start.14
  7.3 0.9 copy-start.15
  8.2 0.7 copy-start.17
  8.9 0.7 copy-start.19
  9.6 0.7 copy-start.22
  52.5 1.3 copy-start.9
  53.8 1.2 copy-start.10
  55.1 0.6 copy-start.21
  88.7 64.5 %copy-start.2 = (bf16[512,256]{1,0:T(8,128)(2,1)S(1)}, bf16[512,256]{1,0:T(8,128)(2,1)}, u32[]{:S(2)}) copy-start(bf16[512,256]{1,0:T(8,128)(2,1)} %cq.5) | copy-start | bytes 786436
  88.7 64.5 %copy-start.4 = (bf16[512,256]{1,0:T(8,128)(2,1)S(1)}, bf16[512,256]{1,0:T(8,128)(2,1)}, u32[]{:S(2)}) copy-start(bf16[512,256]{1,0:T(8,128)(2,1)} %ck.5) | copy-start | bytes 786436
  88.7 64.5 %copy-start.6 = (bf16[512,256]{1,0:T(8,128)(2,1)S(1)}, bf16[512,256]{1,0:T(8,128)(2,1)}, u32[]{:S(2)}) copy-start(bf16[512,256]{1,0:T(8,128)(2,1)} %nq.5) | copy-start | bytes 786436
  88.7 64.5 %copy-start.8 = (bf16[512,256]{1,0:T(8,128)(2,1)S(1)}, bf16[512,256]{1,0:T(8,128)(2,1)}, u32[]{:S(2)}) copy-start(bf16[512,256]{1,0:T(8,128)(2,1)} %nk.5) | copy-start | bytes 786436
  88.8 64.5 %copy-start.18 = (f32[256]{0:T(256)S(1)}, f32[256]{0:T(256)}, u32[]{:S(2)}) copy-start(f32[256]{0:T(256)} %param.18) | copy-start | bytes 3076
  88.8 64.5 %copy-start.20 = (f32[256]{0:T(256)S(1)}, f32[256]{0:T(256)}, u32[]{:S(2)}) copy-start(f32[256]{0:T(256)} %param.19) | copy-start | bytes 3076
  153.3 1.9 %copy-start = (f32[6,2,512,128]{3,2,1,0:T(8,128)S(1)}, f32[6,2,512,128]{3,2,1,0:T(8,128)}, u32[]{:S(2)}) copy-start(f32[6,2,512,128]{3,2,1,0:T(8,128)} %get-tuple-element.28.back) | copy-start | bytes 9437188
  155.1 1.2 copy-start.11
  156.4 0.7 copy-start.16

commit v2 on v1

--- a/solution.py
+++ b/solution.py
@@ -18,6 +18,7 @@
 VMEM = pl.BlockSpec(memory_space=pltpu.VMEM)
 SMEM = pl.BlockSpec(memory_space=pltpu.SMEM)
 ANY = pl.BlockSpec(memory_space=pl.ANY)
+HBM = pl.BlockSpec(memory_space=pltpu.HBM)
 LAST = (((1,), (1,)), ((), ()))
 FIRST = (((0,), (0,)), ((), ()))
 PLAIN = (((1,), (0,)), ((), ()))
@@ -103,26 +104,33 @@
 
 
 def gather_kernel(
-    cq, ck, nq, nk, qg, kg, cv, nv, gc, gn, owned,
-    kall, vall, loc, inv_out, ids_out,
-    normed, id_rows, id_all, sums, send, recv, lsem,
+    cq_h, ck_h, nq_h, nk_h, qg_h, kg_h, cv, nv, gc, gn, owned,
+    kall, vall, loc, own_s, own_d, grads_t, inv_out, ids_out,
+    owned_s, raws, qg, kg, normed, id_rows, id_all, sums, send, recv, lsem,
 ):
     ctx, head, core, y, x = place()
     right, left = (x + 1) % 4, (x + 3) % 4
     mine = pl.ds(pl.multiple_of(core * HD, HD), HD)
     theirs = pl.ds(pl.multiple_of((1 - core) * HD, HD), HD)
     partner = ctx_of(x, y, 1 - core)
+    local = Locals(lsem)
+    owned_load = local.start(owned, owned_s)
+    loads = [local.start(ref, raws.at[i]) for i, ref in enumerate((cq_h, ck_h, nq_h, nk_h))]
+    loads += [local.start(qg_h, qg), local.start(kg_h, kg)]
+    cq, ck, nq, nk = [raws.at[i] for i in range(4)]
+    owned_load.wait()
     lane = lax.broadcasted_iota(jnp.int32, (16, HD), 1)
-    id_rows[...] = jnp.where(lane == 0, owned[0], owned[1]).astype(F32).astype(BF16)
+    id_rows[...] = jnp.where(lane == 0, owned_s[0], owned_s[1]).astype(F32).astype(BF16)
     enter(ctx, head, core, y, x)
     remote = Copies(send, recv, head)
-    local = Locals(lsem)
 
     own_v = vall.at[ctx, pl.ds(0, 512)]
     own_i = vall.at[ctx, pl.ds(512, 16)]
     v_swap = [remote.start(cv.at[:, theirs], own_v, partner), remote.start(id_rows, own_i, partner)]
     v_own = [local.start(cv.at[:, mine], own_v), local.start(id_rows, own_i)]
 
+    for copy in loads:
+        copy.wait()
     row = lax.broadcasted_iota(jnp.int32, (8, 512), 0)
     total = jnp.zeros((8, 512), F32)
     for index, ref in enumerate((cq, ck, nq, nk)):
@@ -192,6 +200,21 @@
     for index in range(3):
         late.append(remote.start(normed.at[index + 1, :, theirs], loc.at[index, core], partner))
         late_own.append(local.start(normed.at[index + 1, :, mine], loc.at[index, core]))
+
+    for copy in late_own:
+        copy.wait()
+    for copy in late:
+        copy.wait_recv()
+    for index in range(4):
+        side, rows = index // 2, slice(index % 2 * BLK, index % 2 * BLK + BLK)
+        packet = 2 * chip_of(x, y) + side
+        grad_clean, grad_noisy = loc[4, side, rows, :], loc[5, side, rows, :]
+        own_s[index, :, :BLK] = dot(kall[packet, rows, :], loc[0, side, rows, :], LAST)
+        own_s[index, :, BLK:] = dot(loc[2, side, rows, :], loc[1, side, rows, :], LAST)
+        own_d[index, :, :BLK] = dot(vall[packet, rows, :], grad_clean, LAST)
+        own_d[index, :, BLK:] = dot(loc[3, side, rows, :], grad_noisy, LAST)
+        grads_t[index, :, :BLK] = jnp.transpose(grad_clean.astype(F32))
+        grads_t[index, :, BLK:] = jnp.transpose(grad_noisy.astype(F32))
 
     v_right.wait_recv()
     v_half = [spread_part(vall, left, y, 0, right, y)]
@@ -217,9 +240,7 @@
     k_left[1].wait_recv()
     k_half.append(spread_part(kall, right, 1 - y, 1, left, y))
 
-    for copy in late_own:
-        copy.wait()
-    for copy in late + v_y + k_half:
+    for copy in v_y + k_half:
         copy.wait_recv()
     gathered = local.start(vall.at[:, pl.ds(512, 16)], id_all)
     gathered.wait()
@@ -236,30 +257,37 @@
             jax.ShapeDtypeStruct((16, 512, HD), BF16),
             jax.ShapeDtypeStruct((16, PACKET, HD), BF16),
             jax.ShapeDtypeStruct((6, 2, 512, HD), BF16),
+            jax.ShapeDtypeStruct((4, BLK, 2 * BLK), F32),
+            jax.ShapeDtypeStruct((4, BLK, 2 * BLK), F32),
+            jax.ShapeDtypeStruct((4, HD, 2 * BLK), F32),
             jax.ShapeDtypeStruct((8, 512), F32),
             jax.ShapeDtypeStruct((16, HD), jnp.int32),
         ),
-        in_specs=[VMEM] * 6 + [ANY] * 4 + [SMEM],
-        out_specs=(ANY, ANY, ANY, VMEM, VMEM),
+        in_specs=[HBM] * 11,
+        out_specs=(VMEM,) * 8,
         scratch_shapes=[
+            pltpu.SMEM((2,), jnp.int32),
+            pltpu.VMEM((4, 512, 256), BF16),
+            pltpu.VMEM((1, 256), F32),
+            pltpu.VMEM((1, 256), F32),
             pltpu.VMEM((4, 512, 256), BF16),
             pltpu.VMEM((16, HD), BF16),
             pltpu.VMEM((16, 16, HD), BF16),
             pltpu.VMEM((8, 8, 512), F32),
             pltpu.SemaphoreType.DMA((40,)),
             pltpu.SemaphoreType.DMA((40,)),
-            pltpu.SemaphoreType.DMA((16,)),
+            pltpu.SemaphoreType.DMA((24,)),
         ],
         compiler_params=pltpu.CompilerParams(
-            collective_id=0, has_side_effects=True, vmem_limit_bytes=48 * 2**20
+            collective_id=0, has_side_effects=True, vmem_limit_bytes=20 * 2**20
         ),
     )(cq, ck, nq, nk, qg, kg, cv, nv, gc, gn, owned)
 
 
 def attention_kernel(
-    ids, docs, loc, kall, vall,
-    res, dkp, dvp,
-    where_is, first_of, weights, dk_acc, dv_acc, out_acc, dq_acc,
+    ids, docs, loc, kall, vall, own_s, own_d, grads_t,
+    out_t, dq_t, dk_noisy, dv_noisy, dk_acc, dv_acc,
+    where_is, first_of, weights,
 ):
     ctx = lax.axis_index("ctx")
     chip = ctx // 2
@@ -291,6 +319,14 @@
 
     def totals(values):
         return jnp.sum(values.reshape(BLK // 8, 8, values.shape[1]), axis=0)
+
+    def in_pairs(count, body, carry):
+        pairs = count // 2
+        carry = lax.fori_loop(0, pairs, lambda i, c: body((2 * i, 2 * i + 1), c), carry)
+        return lax.fori_loop(2 * pairs, count, lambda i, c: body((i,), c), carry)
+
+    def join(parts):
+        return parts[0] if len(parts) == 1 else jnp.concatenate(parts, axis=0)
 
     @pl.loop(0, 4)
     def _(index):
@@ -308,144 +344,177 @@
         grad_noisy = loc[5, side, rows, :]
         queries = jnp.concatenate([query_clean, query_noisy], axis=0)
         grads = jnp.concatenate([grad_clean, grad_noisy], axis=0)
+
+        def score_step(steps, peak):
+            scores = [dot(key_rows(kall, where_is[begin + step]), queries, LAST) for step in steps]
+            for step, score in zip(steps, scores):
+                weights[step] = score
+                peak = jnp.maximum(peak, tops(score))
+            return peak
+
+        peak = in_pairs(count, score_step, tops(own_s[index]))
+        peak = jnp.max(peak, axis=0, keepdims=True) * scale2
+
+        own = jnp.exp2(own_s[index] * scale2 - peak)
+        own_low = own.astype(BF16)
+        value_own = key_rows(vall, stored_own)
+        out_t[index, :, :BLK] = dot(value_own, own_low[:, :BLK], FIRST)
+        out_t[index, :, BLK:] = dot(value_noisy, own_low[:, BLK:], FIRST)
+
+        def value_step(steps, total):
+            values = join([key_rows(vall, where_is[begin + step]) for step in steps])
+            scores = [weights[step] for step in steps]
+            probs = [jnp.exp2(score * scale2 - peak) for score in scores]
+            out_t[index] += dot(values, join([prob.astype(BF16) for prob in probs]), FIRST)
+            for step, prob in zip(steps, probs):
+                weights[step] = prob
+                total = total + totals(prob)
+            return total
+
+        total = in_pairs(count, value_step, totals(own))
+        inverse_total = 1.0 / jnp.sum(total, axis=0, keepdims=True)
+        out = out_t[index] * inverse_total
+        out_t[index] = out
+        delta = jnp.sum(out * grads_t[index], axis=0, keepdims=True)
+
+        own = jnp.exp2(own_s[index] * scale2 - peak) * inverse_total
+        own_low = own.astype(BF16)
+        own_ds = (own * (own_d[index] - delta)).astype(BF16)
         key_own = key_rows(kall, stored_own)
-        value_own = key_rows(vall, stored_own)
-
-        own_scores = jnp.concatenate(
-            [dot(key_own, query_clean, LAST), dot(key_noisy, query_noisy, LAST)], axis=1
-        )
-        weights[0] = own_scores
-
-        def score_step(step, peak):
-            keys = key_rows(kall, where_is[begin + step])
-            scores = dot(keys, queries, LAST)
-            weights[step + 1] = scores
-            return jnp.maximum(peak, tops(scores))
-
-        peak = lax.fori_loop(0, count, score_step, tops(own_scores))
-        peak = jnp.max(peak, axis=0, keepdims=True) * scale2
-
-        own = jnp.exp2(weights[0] * scale2 - peak)
-        weights[0] = own
-        own_low = own.astype(BF16)
-        out_acc[...] = jnp.concatenate(
-            [
-                dot(value_own, own_low[:, :BLK], FIRST),
-                dot(value_noisy, own_low[:, BLK:], FIRST),
-            ],
-            axis=1,
-        )
-
-        def value_step(step, total):
-            values = key_rows(vall, where_is[begin + step])
-            weight = jnp.exp2(weights[step + 1] * scale2 - peak)
-            weights[step + 1] = weight
-            out_acc[...] += dot(values, weight.astype(BF16), FIRST)
-            return total + totals(weight)
-
-        total = lax.fori_loop(0, count, value_step, totals(own))
-        inverse_total = 1.0 / jnp.sum(total, axis=0, keepdims=True)
-        out = out_acc[...] * inverse_total
-        grads_t = jnp.transpose(grads.astype(F32))
-        delta = jnp.sum(out * grads_t, axis=0, keepdims=True)
-        out_rows = jnp.transpose(out)
-        res[0, side, rows, :] = out_rows[:BLK]
-        res[1, side, rows, :] = out_rows[BLK:]
-
-        own = weights[0] * inverse_total
-        own_low = own.astype(BF16)
-        own_dp = jnp.concatenate(
-            [dot(value_own, grad_clean, LAST), dot(value_noisy, grad_noisy, LAST)], axis=1
-        )
-        own_ds = (own * (own_dp - delta)).astype(BF16)
         dv_acc[stored_own] += dot(own_low[:, :BLK], grad_clean, PLAIN)
         dk_acc[stored_own] += dot(own_ds[:, :BLK], query_clean, PLAIN)
-        res[5, side, rows, :] = dot(own_low[:, BLK:], grad_noisy, PLAIN)
-        res[4, side, rows, :] = dot(own_ds[:, BLK:], query_noisy, PLAIN) * scale
-        dq_acc[...] = jnp.concatenate(
-            [dot(key_own, own_ds[:, :BLK], FIRST), dot(key_noisy, own_ds[:, BLK:], FIRST)], axis=1
-        )
-
-        @pl.loop(0, count)
-        def _(step):
-            stored = where_is[begin + step]
-            keys = key_rows(kall, stored)
-            values = key_rows(vall, stored)
-            probs = weights[step + 1] * inverse_total
-            dv_acc[stored] += dot(probs.astype(BF16), grads, PLAIN)
-            dp = dot(values, grads, LAST)
-            ds = (probs * (dp - delta)).astype(BF16)
-            dk_acc[stored] += dot(ds, queries, PLAIN)
-            dq_acc[...] += dot(keys, ds, FIRST)
-
-        dq_rows = jnp.transpose(dq_acc[...] * scale)
-        res[2, side, rows, :] = dq_rows[:BLK]
-        res[3, side, rows, :] = dq_rows[BLK:]
-
-    @pl.loop(0, 32)
-    def _(stored):
-        start = pl.multiple_of((stored % 2) * BLK, BLK)
-        dkp[stored // 4, (stored // 2) % 2, pl.ds(start, BLK), :] = (dk_acc[stored] * scale).astype(BF16)
-        dvp[stored // 4, (stored // 2) % 2, pl.ds(start, BLK), :] = dv_acc[stored].astype(BF16)
-
-
-def attention_call(ids, docs, loc, kall, vall):
+        dv_noisy[side, rows, :] = dot(own_low[:, BLK:], grad_noisy, PLAIN)
+        dk_noisy[side, rows, :] = dot(own_ds[:, BLK:], query_noisy, PLAIN) * scale
+        dq_t[index, :, :BLK] = dot(key_own, own_ds[:, :BLK], FIRST)
+        dq_t[index, :, BLK:] = dot(key_noisy, own_ds[:, BLK:], FIRST)
+
+        def grad_step(steps, carry):
+            stored = [where_is[begin + step] for step in steps]
+            keys = [key_rows(kall, place) for place in stored]
+            probs = [weights[step] * inverse_total for step in steps]
+            dv_old = [dv_acc[place] for place in stored]
+            dk_old = [dk_acc[place] for place in stored]
+            dps = [dot(key_rows(vall, place), grads, LAST) for place in stored]
+            dvs = [dot(prob.astype(BF16), grads, PLAIN) for prob in probs]
+            dss = [(prob * (dp - delta)).astype(BF16) for prob, dp in zip(probs, dps)]
+            dks = [dot(ds, queries, PLAIN) for ds in dss]
+            dq_t[index] += dot(join(keys), join(dss), FIRST)
+            for i, place in enumerate(stored):
+                dv_acc[place] = dv_old[i] + dvs[i]
+                dk_acc[place] = dk_old[i] + dks[i]
+            return carry
+
+        in_pairs(count, grad_step, 0)
+
+
+def attention_call(ids, docs, loc, kall, vall, own_s, own_d, grads_t):
     return pl.pallas_call(
         attention_kernel,
         name="attention",
         out_shape=(
-            jax.ShapeDtypeStruct((6, 2, 512, HD), F32),
-            jax.ShapeDtypeStruct((8, 2, 512, HD), BF16),
-            jax.ShapeDtypeStruct((8, 2, 512, HD), BF16),
+            jax.ShapeDtypeStruct((4, HD, 2 * BLK), F32),
+            jax.ShapeDtypeStruct((4, HD, 2 * BLK), F32),
+            jax.ShapeDtypeStruct((2, 512, HD), F32),
+            jax.ShapeDtypeStruct((2, 512, HD), F32),
+            jax.ShapeDtypeStruct((32, BLK, HD), F32),
+            jax.ShapeDtypeStruct((32, BLK, HD), F32),
         ),
-        in_specs=[SMEM, SMEM, VMEM, VMEM, VMEM],
-        out_specs=(VMEM, VMEM, VMEM),
+        in_specs=[SMEM, SMEM] + [VMEM] * 6,
+        out_specs=(VMEM,) * 6,
         scratch_shapes=[
             pltpu.SMEM((32,), jnp.int32),
             pltpu.SMEM((32,), jnp.int32),
-            pltpu.VMEM((17, BLK, 2 * BLK), F32),
-            pltpu.VMEM((32, BLK, HD), F32),
-            pltpu.VMEM((32, BLK, HD), F32),
-            pltpu.VMEM((HD, 2 * BLK), F32),
-            pltpu.VMEM((HD, 2 * BLK), F32),
+            pltpu.VMEM((16, BLK, 2 * BLK), F32),
         ],
-        compiler_params=pltpu.CompilerParams(vmem_limit_bytes=56 * 2**20),
-    )(ids, docs, loc, kall, vall)
+        compiler_params=pltpu.CompilerParams(vmem_limit_bytes=18 * 2**20),
+    )(ids, docs, loc, kall, vall, own_s, own_d, grads_t)
 
 
 def scatter_kernel(
-    cq, ck, nq, nk, qg, kg, res, dkp, dvp,
+    cq_h, ck_h, nq_h, nk_h, qg_h, kg_h, out_t, dq_t, dk_noisy, dv_noisy, dk, dv,
     back, fin, inner_out,
-    va, vy, vh, vx, ka, kh, kx, ks, ky, sums, ksums, send, recv, lsem,
+    raws, qg, kg, stage, k_out, v_out, vy, vh, vx, kh, kx, ky, away, sums, send, recv, lsem,
 ):
     ctx, head, core, y, x = place()
     right, left = (x + 1) % 4, (x + 3) % 4
     partner = ctx_of(x, y, 1 - core)
     to_right, to_left = ctx_of(right, y, core), ctx_of(left, y, core)
     to_y = ctx_of(x, 1 - y, core)
+    score_scale = 1.0 / math.sqrt(HD)
+    local = Locals(lsem)
+    loads = [local.start(ref, raws.at[i]) for i, ref in enumerate((cq_h, ck_h, nq_h, nk_h))]
+    loads += [local.start(qg_h, qg), local.start(kg_h, kg)]
+    cq, ck, nq, nk = [raws.at[i] for i in range(4)]
+    remote = Copies(send, recv, head)
+
+    def mine(ref, step, row, half):
+        chip = chip_of((x + step) % 4, y if row == 0 else 1 - y)
+        return ref[pl.ds(chip * 4 + half * 2, 2)].reshape(512, HD)
+
+    def pack_v(step):
+        for half in range(2):
+            v_out[step, half] = mine(dv, step, 1, half).astype(BF16)
+
+    def pack_k(row, step, half, *others):
+        value = mine(dk, step, row, half) * score_scale
+        for other in others:
+            value = value + other[...].astype(F32)
+        k_out[row, step, half] = value.astype(BF16)
+
+    pack_v(2)
+    pack_k(1, 2, 0)
+    pack_k(1, 2, 1)
     enter(ctx, head, core, y, x)
-    remote = Copies(send, recv, head)
-    local = Locals(lsem)
-
-    def chip(step, row):
-        return chip_of((x + step) % 4, y if row == 0 else 1 - y)
-
-    v_y = {}
+    v_y = {2: remote.start(v_out.at[2], vy.at[2], to_y)}
     k_half = {}
-    v_y[2] = remote.start(dvp.at[chip(2, 1)], vy.at[2], to_y)
+
+    def start_half(row):
+        k_half[row, 0] = remote.start(k_out.at[row, 2, 0], kh.at[row, 0], to_left)
+        k_half[row, 1] = remote.start(k_out.at[row, 2, 1], kh.at[row, 1], to_right)
+
+    start_half(1)
+    pack_k(0, 2, 0)
+    pack_k(0, 2, 1)
+    start_half(0)
+    pack_v(3)
+    v_y[3] = remote.start(v_out.at[3], vy.at[3], to_y)
+    pack_v(1)
     for row in (1, 0):
-        k_half[row, 0] = remote.start(dkp.at[chip(2, row), 0], kh.at[row, 0], to_left)
-        k_half[row, 1] = remote.start(dkp.at[chip(2, row), 1], kh.at[row, 1], to_right)
-    for step in (3, 1, 0):
-        v_y[step] = remote.start(dvp.at[chip(step, 1)], vy.at[step], to_y)
-    k_own = {}
-    for row in (1, 0):
-        for step in (3, 1, 0):
-            k_own[row, step] = local.start(dkp.at[chip(step, row)], ka.at[row, step])
-    v_own = {step: local.start(dvp.at[chip(step, 0)], va.at[step]) for step in (2, 3, 1, 0)}
-    order = (2, 3, 4, 0, 1, 5)
-    back_swap = {i: remote.start(res.at[i, 1 - core], back.at[i, core], partner) for i in order}
-    back_own = {i: local.start(res.at[i, core], back.at[i, core]) for i in order}
+        pack_k(row, 3, 1)
+        pack_k(row, 1, 0)
+
+    swap = {}
+    swap[4] = remote.start(dk_noisy.at[1 - core], back.at[4, core], partner)
+    own_noisy = [
+        local.start(dk_noisy.at[core], back.at[4, core]),
+        local.start(dv_noisy.at[core], back.at[5, core]),
+    ]
+
+    def turn(ref, first, factor):
+        for part in range(2):
+            rows = slice(part * BLK, part * BLK + BLK)
+            values = jnp.transpose(ref[2 * core + part]) * factor
+            back[first, core, rows, :] = values[:BLK]
+            back[first + 1, core, rows, :] = values[BLK:]
+            values = jnp.transpose(ref[2 * (1 - core) + part]) * factor
+            stage[first, rows, :] = values[:BLK]
+            stage[first + 1, rows, :] = values[BLK:]
+        for i in (first, first + 1):
+            swap[i] = remote.start(stage.at[i], back.at[i, core], partner)
+
+    turn(dq_t, 2, score_scale)
+
+    k_x = {}
+
+    def k_forward(row):
+        k_half[row, 0].wait_recv()
+        pack_k(row, 3, 0, kh.at[row, 0])
+        k_x[row, 0] = remote.start(k_out.at[row, 3], kx.at[row, 0], to_left)
+        k_half[row, 1].wait_recv()
+        pack_k(row, 1, 1, kh.at[row, 1])
+        k_x[row, 1] = remote.start(k_out.at[row, 1], kx.at[row, 1], to_right)
+
+    k_forward(1)
 
     row = lax.broadcasted_iota(jnp.int32, (8, 512), 0)
 
@@ -456,9 +525,10 @@
             products = products + raw[:, columns].astype(F32) * (gain[:, columns] * values)
         return row_sums(products)
 
+    for copy in loads + own_noisy:
+        copy.wait()
     for i in (2, 3, 4):
-        back_own[i].wait()
-        back_swap[i].wait_recv()
+        swap[i].wait_recv()
     total = jnp.zeros((8, 512), F32)
     for index, raw, gain, i in ((0, cq, qg, 2), (2, nq, qg, 3), (3, nk, kg, 4)):
         total = jnp.where(row == index, inner(raw, gain, back[i, 0], back[i, 1]), total)
@@ -467,76 +537,66 @@
         remote.start(sums.at[0], sums.at[step], ctx, (head + step) % 8) for step in range(1, 8)
     ]
 
-    def add(target, other):
-        target[...] = (target[...].astype(F32) + other[...].astype(F32)).astype(BF16)
-
-    k_x = {}
-
-    def k_forward(row):
-        k_own[row, 3].wait()
-        k_half[row, 0].wait_recv()
-        add(ka.at[row, 3, 0], kh.at[row, 0])
-        k_x[row, 0] = remote.start(ka.at[row, 3], kx.at[row, 0], to_left)
-        k_own[row, 1].wait()
-        k_half[row, 1].wait_recv()
-        add(ka.at[row, 1, 1], kh.at[row, 1])
-        k_x[row, 1] = remote.start(ka.at[row, 1], kx.at[row, 1], to_right)
-
-    k_forward(1)
-    v_own[2].wait()
+    def pack_x(step, half, *others):
+        value = mine(dv, step, 0, half) + vy[step, half].astype(F32)
+        for other in others:
+            value = value + other[...].astype(F32)
+        vx_out[step, half] = value.astype(BF16)
+
+    vx_out = k_out.at[2]
     v_y[2].wait_recv()
-    add(va.at[2], vy.at[2])
-    v_half = [
-        remote.start(va.at[2, 0], vh.at[0], to_left),
-        remote.start(va.at[2, 1], vh.at[1], to_right),
-    ]
+    pack_x(2, 0)
+    v_half = [remote.start(vx_out.at[2, 0], vh.at[0], to_left)]
+    pack_x(2, 1)
+    v_half.append(remote.start(vx_out.at[2, 1], vh.at[1], to_right))
+    v_y[1] = remote.start(v_out.at[1], vy.at[1], to_y)
     k_forward(0)
-    k_own[1, 0].wait()
+    turn(out_t, 0, 1.0)
+    swap[5] = remote.start(dv_noisy.at[1 - core], back.at[5, core], partner)
+    pack_v(0)
     k_x[1, 0].wait_recv()
     k_x[1, 1].wait_recv()
-    ks[...] = (ka[1, 0].astype(F32) + kx[1, 0].astype(F32) + kx[1, 1].astype(F32)).astype(BF16)
-    k_y = remote.start(ks, ky, to_y)
-
-    v_own[3].wait()
+    for half in range(2):
+        pack_k(1, 0, half, kx.at[1, 0, half], kx.at[1, 1, half])
+    k_y = remote.start(k_out.at[1, 0], ky, to_y)
+    v_y[0] = remote.start(v_out.at[0], vy.at[0], to_y)
+
     v_y[3].wait_recv()
-    add(va.at[3], vy.at[3])
     v_half[0].wait_recv()
-    add(va.at[3, 0], vh.at[0])
-    v_x = [remote.start(va.at[3], vx.at[0], to_left)]
-    v_own[1].wait()
+    pack_x(3, 0, vh.at[0])
+    pack_x(3, 1)
+    v_x = [remote.start(vx_out.at[3], vx.at[0], to_left)]
     v_y[1].wait_recv()
-    add(va.at[1], vy.at[1])
     v_half[1].wait_recv()
-    add(va.at[1, 1], vh.at[1])
-    v_x.append(remote.start(va.at[1], vx.at[1], to_right))
-
-    k_own[0, 0].wait()
-    k_x[0, 0].wait_recv()
-    k_x[0, 1].wait_recv()
-    k_y.wait_recv()
-
-    def finish(index, terms):
-        values = [
-            sum(term[half].astype(F32) for term in terms[1:]) + terms[0][half].astype(F32)
-            for half in range(2)
-        ]
+    pack_x(1, 0)
+    pack_x(1, 1, vh.at[1])
+    v_x.append(remote.start(vx_out.at[1], vx.at[1], to_right))
+
+    def finish(index, ref, factor, terms):
+        values = []
+        for half in range(2):
+            value = mine(ref, 0, 0, half) * factor
+            for term in terms:
+                value = value + term[half].astype(F32)
+            values.append(value)
         first_core = core == 0
         fin[index, core] = jnp.where(first_core, values[0], values[1])
         away[index] = jnp.where(first_core, values[1], values[0])
         return remote.start(away.at[index], fin.at[index, core], partner)
 
-    away = ksums
-    k_fin = finish(0, (ka.at[0, 0], kx.at[0, 0], kx.at[0, 1], ky))
+    k_x[0, 0].wait_recv()
+    k_x[0, 1].wait_recv()
+    k_y.wait_recv()
+    k_fin = finish(0, dk, score_scale, (kx.at[0, 0], kx.at[0, 1], ky))
     k_fin.wait_recv()
     sums[8] = inner(ck, kg, fin[0, 0], fin[0, 1])
     k_exchange = [
         remote.start(sums.at[8], sums.at[8 + step], ctx, (head + step) % 8) for step in range(1, 8)
     ]
-    v_own[0].wait()
     v_y[0].wait_recv()
     v_x[0].wait_recv()
     v_x[1].wait_recv()
-    v_fin = finish(1, (va.at[0], vy.at[0], vx.at[0], vx.at[1]))
+    v_fin = finish(1, dv, 1.0, (vy.at[0], vx.at[0], vx.at[1]))
 
     for copy in exchange + k_exchange:
         copy.wait_recv()
@@ -548,13 +608,12 @@
     inner_out[...] = jnp.where(row == 1, k_total, total)
     v_fin.wait_recv()
     for i in (0, 1, 5):
-        back_own[i].wait()
-        back_swap[i].wait_recv()
+        swap[i].wait_recv()
     for copy in remote.started:
         copy.wait_send()
 
 
-def scatter_call(cq, ck, nq, nk, qg, kg, res, dkp, dvp):
+def scatter_call(cq, ck, nq, nk, qg, kg, out_t, dq_t, dk_noisy, dv_noisy, dk, dv):
     return pl.pallas_call(
         scatter_kernel,
         name="scatter_grads",
@@ -563,28 +622,31 @@
             jax.ShapeDtypeStruct((2, 2, 512, HD), F32),
             jax.ShapeDtypeStruct((8, 512), F32),
         ),
-        in_specs=[VMEM] * 6 + [ANY] * 3,
+        in_specs=[HBM] * 6 + [VMEM] * 6,
         out_specs=(VMEM, VMEM, VMEM),
         scratch_shapes=[
+            pltpu.VMEM((4, 512, 256), BF16),
+            pltpu.VMEM((1, 256), F32),
+            pltpu.VMEM((1, 256), F32),
+            pltpu.VMEM((4, 512, HD), F32),
+            pltpu.VMEM((3, 4, 2, 512, HD), BF16),
             pltpu.VMEM((4, 2, 512, HD), BF16),
             pltpu.VMEM((4, 2, 512, HD), BF16),
             pltpu.VMEM((2, 512, HD), BF16),
             pltpu.VMEM((2, 2, 512, HD), BF16),
-            pltpu.VMEM((2, 4, 2, 512, HD), BF16),
             pltpu.VMEM((2, 2, 512, HD), BF16),
             pltpu.VMEM((2, 2, 2, 512, HD), BF16),
             pltpu.VMEM((2, 512, HD), BF16),
-            pltpu.VMEM((2, 512, HD), BF16),
+            pltpu.VMEM((2, 512, HD), F32),
             pltpu.VMEM((16, 8, 512), F32),
-            pltpu.VMEM((2, 512, HD), F32),
             pltpu.SemaphoreType.DMA((44,)),
             pltpu.SemaphoreType.DMA((44,)),
-            pltpu.SemaphoreType.DMA((20,)),
+            pltpu.SemaphoreType.DMA((8,)),
         ],
         compiler_params=pltpu.CompilerParams(
-            collective_id=1, has_side_effects=True, vmem_limit_bytes=56 * 2**20
+            collective_id=1, has_side_effects=True, vmem_limit_bytes=18 * 2**20
         ),
-    )(cq, ck, nq, nk, qg, kg, res, dkp, dvp)
+    )(cq, ck, nq, nk, qg, kg, out_t, dq_t, dk_noisy, dv_noisy, dk, dv)
 
 
 def finish_kernel(
@@ -639,11 +701,15 @@
     qg = q_gain.reshape(1, 256)
     kg = k_gain.reshape(1, 256)
     raws = (clean_q, clean_k, noisy_q, noisy_k, qg, kg)
-    kall, vall, loc, inv, ids = gather_call(
-        *raws, clean_v, noisy_v, grad_clean, grad_noisy, owned_blocks
-    )
-    res, dkp, dvp = attention_call(ids, block_doc, loc, kall, vall)
-    back, fin, inner = scatter_call(*raws, res, dkp, dvp)
+    pinned = [
+        pltpu.with_memory_space_constraint(a, pltpu.HBM)
+        for a in raws + (clean_v, noisy_v, grad_clean, grad_noisy, owned_blocks)
+    ]
+    *parts, inv, ids = gather_call(*pinned)
+    kall, vall, loc, own_s, own_d, grads_t = parts
+    docs = pltpu.with_memory_space_constraint(block_doc, pltpu.HBM)
+    grads = attention_call(ids, docs, loc, kall, vall, own_s, own_d, grads_t)
+    back, fin, inner = scatter_call(*pinned[:6], *grads)
     return finish_call(*raws, inv, inner, back, fin)
 
 

time: 161 us -> 105 us (0.65)
  the two profiles are of different devices: /device:TPU:1 before, /device:TPU:5 now
where the time goes in v2:
time: 105 us
  Pallas kernels  104 us (99%)
    pallas_call x1, Pallas kernels, gather_call(): pl.pallas_call(gather_kernel, name='gather_keys', out_shape=(jax.ShapeDty...  40.6 us
    pallas_call x1, Pallas kernels, scatter_call(): pl.pallas_call(scatter_kernel, name='scatter_grads', out_shape=(jax.Shape...  37.7 us
    pallas_call x1, Pallas kernels, attention_call(): pl.pallas_call(attention_kernel, name='attention', out_shape=(jax.ShapeDt...  22.3 us
    pallas_call x1, Pallas kernels, finish_call(): pl.pallas_call(finish_kernel, name='finish', grid=(512 // rows,), out_sha...  3.25 us

profile of v2, /device:TPU:5, one launch (start us, length us, event | category | flops | bytes accessed | tf_op | source)
XLA Modules:
  0.0 104.7 jit_solution(15016744886486489079)
XLA Ops:
  0.6 40.6 %gather_keys.1 = (bf16[16,512,128]{2,1,0:T(8,128)(2,1)S(1)}, bf16[16,528,128]{2,1,0:T(8,128)(2,1)S(1)}, bf16[6,2,512,128]{3,2,1,0:T(8,128)(2,1)S(1)}, f32[4,256,...) custom-call(bf16[512,256]{1,0:T(8,128)(2,1)} %cq.1, ...), custom_call_target="tpu_custom_call" | custom-call | tf_op jit(solution)/shard_map/gather_keys/pallas_call | solution.py:253
  41.3 22.3 %attention.1 = (f32[4,128,512]{2,1,0:T(8,128)S(1)}, f32[4,128,512]{2,1,0:T(8,128)S(1)}, f32[2,512,128]{2,1,0:T(8,128)S(1)}, f32[2,512,128]{2,1,0:T(8,128)S(1)}, ...) custom-call(s32[16,128]{1,0:T(8,128)S(1)} %get-tuple-element.26.ids, s32[32]{0:T(128)} %docs.1, ...), custom_call_target="tpu_custom_call" | custom-call | tf_op jit(solution)/shard_map/attention/pallas_call | solution.py:411
  63.6 0.0 copy-start
  63.6 0.0 copy-start.1
  63.6 0.0 copy-start.2
  63.6 0.0 copy-start.3
  63.6 0.0 copy-start.4
  63.6 0.0 copy-start.5
  63.6 37.7 %scatter_grads.1 = (f32[6,2,512,128]{3,2,1,0:T(8,128)S(1)}, f32[2,2,512,128]{3,2,1,0:T(8,128)S(1)}, f32[8,512]{1,0:T(8,128)S(1)}) custom-call(bf16[512,256]{1,0:T(8,128)(2,1)} %cq.1, bf16[512,256]{1,0:T(8,128)(2,1)} %ck.1, bf16[512,256]{1,0:T(8,128)(2,1)} %nq.1, bf16[512,256]{1,0:T(8,128)(2,1)} %nk.1, f32[1,256]{1,0:T(1,128)} %bitcast.3, f32[1,256]{1,0:T(1,128)} %bitcast.6, ...), custom_call_target="tpu_custom_call" | custom-call | tf_op jit(solution)/shard_map/scatter_grads/pallas_call | solution.py:617
  101.4 0.0 copy-done
  101.4 0.0 copy-done.1
  101.4 0.0 copy-done.2
  101.4 0.0 copy-done.3
  101.4 0.0 copy-done.4
  101.4 0.0 copy-done.5
  101.5 3.3 %finish.1 = (f32[512,256]{1,0:T(8,128)}, f32[512,256]{1,0:T(8,128)}, f32[512,256]{1,0:T(8,128)}, f32[512,256]{1,0:T(8,128)}, f32[512,256]{1,0:T(8,128)}, /*index...) custom-call(bf16[512,256]{1,0:T(8,128)(2,1)S(1)} %copy-done, bf16[512,256]{1,0:T(8,128)(2,1)S(1)} %copy-done.1, ...), custom_call_target="tpu_custom_call" | custom-call | tf_op jit(solution)/shard_map/finish/pallas_call | solution.py:680
Async XLA Ops:
  63.6 37.8 %copy-start = (bf16[512,256]{1,0:T(8,128)(2,1)S(1)}, bf16[512,256]{1,0:T(8,128)(2,1)}, u32[]{:S(2)}) copy-start(bf16[512,256]{1,0:T(8,128)(2,1)} %cq.1) | copy-start | bytes 786436
  63.6 37.8 %copy-start.1 = (bf16[512,256]{1,0:T(8,128)(2,1)S(1)}, bf16[512,256]{1,0:T(8,128)(2,1)}, u32[]{:S(2)}) copy-start(bf16[512,256]{1,0:T(8,128)(2,1)} %ck.1) | copy-start | bytes 786436
  63.6 37.8 %copy-start.2 = (bf16[512,256]{1,0:T(8,128)(2,1)S(1)}, bf16[512,256]{1,0:T(8,128)(2,1)}, u32[]{:S(2)}) copy-start(bf16[512,256]{1,0:T(8,128)(2,1)} %nq.1) | copy-start | bytes 786436
  63.6 37.8 %copy-start.3 = (bf16[512,256]{1,0:T(8,128)(2,1)S(1)}, bf16[512,256]{1,0:T(8,128)(2,1)}, u32[]{:S(2)}) copy-start(bf16[512,256]{1,0:T(8,128)(2,1)} %nk.1) | copy-start | bytes 786436
  63.6 37.8 %copy-start.4 = (f32[256]{0:T(256)S(1)}, f32[256]{0:T(256)}, u32[]{:S(2)}) copy-start(f32[256]{0:T(256)} %param.18) | copy-start | bytes 3076
  63.6 37.8 %copy-start.5 = (f32[256]{0:T(256)S(1)}, f32[256]{0:T(256)}, u32[]{:S(2)}) copy-start(f32[256]{0:T(256)} %param.19) | copy-start | bytes 3076

commit v3 on v2

v3 whole, which is shorter than its diff:
```python
import math

import jax
import jax.numpy as jnp
from jax import lax
from jax.experimental import pallas as pl
from jax.experimental.pallas import tpu as pltpu
from jax.sharding import PartitionSpec as P

HD = 128
BLK = 256
FEAT = 2048
EPSILON = 1e-06
NEGATIVE = -1e30
MESH = pl.DeviceIdType.MESH
F32 = jnp.float32
BF16 = jnp.bfloat16
VMEM = pl.BlockSpec(memory_space=pltpu.VMEM)
SMEM = pl.BlockSpec(memory_space=pltpu.SMEM)
ANY = pl.BlockSpec(memory_space=pl.ANY)
HBM = pl.BlockSpec(memory_space=pltpu.HBM)
LAST = (((1,), (1,)), ((), ()))
FIRST = (((0,), (0,)), ((), ()))
PLAIN = (((1,), (0,)), ((), ()))
PACKET = 528
SHIFT = 160
GROUP = 2


def dot(a, b, dims):
    return lax.dot_general(a, b, dims, preferred_element_type=F32)


def row_sums(products):
    high = products.astype(BF16)
    low = (products - high.astype(F32)).astype(BF16)
    ones = jnp.ones((8, products.shape[1]), BF16)
    return dot(ones, high, LAST) + dot(ones, low, LAST)


def place():
    ctx = lax.axis_index("ctx")
    head = lax.axis_index("head")
    core = ctx % 2
    y = (ctx // 2) % 2
    x = ctx // 4
    return ctx, head, core, y, x


def ctx_of(x, y, core):
    return (x * 2 + y) * 2 + core


def chip_of(x, y):
    return x * 2 + y


class Copies:
    def __init__(self, send, recv, head):
        self.send, self.recv, self.head = send, recv, head
        self.started = []
        self.count = 0

    def start(self, src, dst, ctx, head=None):
        copy = pltpu.make_async_remote_copy(
            src_ref=src,
            dst_ref=dst,
            send_sem=self.send.at[self.count],
            recv_sem=self.recv.at[self.count],
            device_id={"ctx": ctx, "head": self.head if head is None else head},
            device_id_type=MESH,
        )
        self.count += 1
        copy.start()
        self.started.append(copy)
        return copy


class Locals:
    def __init__(self, sems):
        self.sems = sems
        self.count = 0

    def start(self, src, dst):
        copy = pltpu.make_async_copy(src, dst, self.sems.at[self.count])
        self.count += 1
        copy.start()
        return copy


def enter(ctx, head, others):
    barrier = pltpu.get_barrier_semaphore()
    for other in others:
        pl.semaphore_signal(barrier, inc=1, device_id={"ctx": other, "head": head}, device_id_type=MESH)
    for step in range(1, 8):
        pl.semaphore_signal(
            barrier, inc=1, device_id={"ctx": ctx, "head": (head + step) % 8}, device_id_type=MESH
        )
    pl.semaphore_wait(barrier, 7 + len(others))


def gather_kernel(
    cq_h, ck_h, nq_h, nk_h, qg_h, kg_h, cv, nv, gc, gn, owned,
    kall, vall, qq, gg, kn, vn, own_s, own_d, grads_t, inv_out, ids_out,
    owned_s, raws, qg, kg, k_packet, normed, sums, send, recv, wide_send, wide_recv, lsem,
):
    ctx, head, core, y, x = place()
    right, left = (x + 1) % 4, (x + 3) % 4
    opposite = (x + 2) % 4
    mine = pl.ds(pl.multiple_of(core * HD, HD), HD)
    theirs = pl.ds(pl.multiple_of((1 - core) * HD, HD), HD)
    partner = ctx_of(x, y, 1 - core)
    local = Locals(lsem)
    owned_load = local.start(owned, owned_s)
    loads = [local.start(ref, raws.at[i]) for i, ref in enumerate((cq_h, ck_h, nq_h, nk_h))]
    loads += [local.start(qg_h, qg), local.start(kg_h, kg)]
    remote = Copies(send, recv, head)
    chips = ((x, 1 - y), (right, y), (left, y))
    enter(ctx, head, [partner] + [ctx_of(*chip, c) for chip in chips for c in range(2)])
    wide = []

    def first_hop(base, columns_of, buf):
        for number, chip in enumerate(chips):
            for target in range(2):
                copy = pltpu.make_async_remote_copy(
                    src_ref=columns_of(target),
                    dst_ref=buf.at[ctx],
                    send_sem=wide_send.at[base + number, target],
                    recv_sem=wide_recv.at[base + number, core],
                    device_id={"ctx": ctx_of(*chip, target), "head": head},
                    device_id_type=MESH,
                )
                copy.start()
                wide.append(copy)

    def arrived(base, number, buf, source):
        chip = ((x, 1 - y), (left, y), (right, y))[number]
        pltpu.make_async_remote_copy(
            src_ref=buf.at[ctx],
            dst_ref=buf.at[ctx_of(*chip, source)],
            send_sem=wide_send.at[base + number, source],
            recv_sem=wide_recv.at[base + number, source],
            device_id={"ctx": partner, "head": head},
            device_id_type=MESH,
        ).wait_recv()

    first_hop(0, lambda target: cv.at[:, target * HD : target * HD + HD], vall)
    v_swap = remote.start(cv.at[:, theirs], vall.at[ctx], partner)
    v_own = local.start(cv.at[:, mine], vall.at[ctx])

    for copy in loads:
        copy.wait()
    row = lax.broadcasted_iota(jnp.int32, (8, 512), 0)
    total = jnp.zeros((8, 512), F32)
    for index in range(4):
        raw = raws[index].astype(F32)
        total = jnp.where(row == index, row_sums(raw * raw), total)
    sums[0] = total
    exchange = [
        remote.start(sums.at[0], sums.at[step], ctx, (head + step) % 8) for step in range(1, 8)
    ]
    owned_load.wait()
    lane = lax.broadcasted_iota(jnp.int32, (16, 2 * HD), 1)
    k_packet[512:, :] = jnp.where(lane % HD == 0, owned_s[0], owned_s[1]).astype(F32).astype(BF16)

    pair = pl.ds(core * 2, 2)
    late, late_own = [], []

    def swap(src, dst):
        late.append(remote.start(src.at[:, :, theirs], dst, partner))
        late_own.append(local.start(src.at[:, :, mine], dst))

    swap(gc, gg.at[pair, 0])
    swap(gn, gg.at[pair, 1])
    swap(nv, vn.at[pair])

    for copy in exchange:
        copy.wait_recv()
    total = sums[0]
    for step in range(1, 8):
        total = total + sums[step]
    inverse = lax.rsqrt(total / FEAT + EPSILON)
    inv_out[...] = inverse
    columns = jnp.transpose(inverse)

    def normalized(index, gain):
        values = raws[index].astype(F32) * columns[:, index : index + 1] * gain[...]
        return values.astype(BF16)

    k_packet[:512, :] = normalized(1, kg)
    first_hop(3, lambda target: k_packet.at[:, target * HD : target * HD + HD], kall)
    k_swap = remote.start(k_packet.at[:, theirs], kall.at[ctx], partner)
    k_own = local.start(k_packet.at[:, mine], kall.at[ctx])
    for index, raw, gain, dst in (
        (0, 0, qg, qq.at[pair, 0]),
        (1, 2, qg, qq.at[pair, 1]),
        (2, 3, kg, kn.at[pair]),
    ):
        normed[index] = normalized(raw, gain).reshape(2, BLK, 2 * HD)
        swap(normed.at[index], dst)

    def slot(buf, sx, sy):
        return buf.at[pl.ds(2 * chip_of(sx, sy), 2)]

    def part(buf, sx, sy, half):
        return buf.at[2 * chip_of(sx, sy) + half]

    def rows_of(sx, sy, half, first, count):
        return vall.at[2 * chip_of(sx, sy) + half, pl.ds(first, count)]

    def spread(view, px, py):
        return remote.start(view, view, ctx_of(px, py, core))

    v_half, v_y = [], []
    for number, near, far, half in ((1, left, right, 0), (2, right, left, 1)):
        arrived(0, number, vall, half)
        v_half.append(spread(part(vall, near, y, half), far, y))
        arrived(0, number, vall, 1 - half)
        v_y.append(spread(slot(vall, near, y), x, 1 - y))
    arrived(3, 0, kall, 0)
    arrived(3, 0, kall, 1)
    k_right = spread(slot(kall, x, 1 - y), right, y)
    k_left = spread(slot(kall, x, 1 - y), left, y)

    v_own.wait()
    k_own.wait()
    v_swap.wait_recv()
    k_swap.wait_recv()
    for copy in late_own:
        copy.wait()
    for copy in late:
        copy.wait_recv()

    def own_block(index):
        side, rows = index // 2, slice(index % 2 * BLK, index % 2 * BLK + BLK)
        packet = 2 * chip_of(x, y) + side
        grad_clean, grad_noisy = gg[index, 0], gg[index, 1]
        own_s[index, :, :BLK] = dot(kall[packet, rows, :], qq[index, 0], LAST)
        own_s[index, :, BLK:] = dot(kn[index], qq[index, 1], LAST)
        own_d[index, :, :BLK] = dot(vall[packet, rows, :], grad_clean, LAST)
        own_d[index, :, BLK:] = dot(vn[index], grad_noisy, LAST)
        grads_t[index, :, :BLK] = jnp.transpose(grad_clean.astype(F32))
        grads_t[index, :, BLK:] = jnp.transpose(grad_noisy.astype(F32))

    own_block(0)
    own_block(1)
    k_half = []
    for number, near, far, half in ((1, left, right, 0), (2, right, left, 1)):
        arrived(3, number, kall, half)
        k_half.append(spread(part(kall, near, y, half), far, y))
        arrived(3, number, kall, 1 - half)
    own_block(2)
    own_block(3)
    for half in range(2):
        v_half[half].wait_recv()
        v_y.append(spread(rows_of(opposite, y, half, SHIFT, 512 - SHIFT), x, 1 - y))
    arrived(0, 0, vall, 0)
    arrived(0, 0, vall, 1)
    v_far = []
    for half, near, far in ((0, left, right), (1, right, left)):
        v_y[half].wait_recv()
        v_far.append(spread(rows_of(near, 1 - y, half, 0, SHIFT), far, y))
    k_right.wait_recv()
    k_half.append(spread(part(kall, left, 1 - y, 0), right, y))
    k_left.wait_recv()
    k_half.append(spread(part(kall, right, 1 - y, 1), left, y))

    for copy in v_y[2:] + v_far + k_half:
        copy.wait_recv()
    names = jnp.max(kall[:, 512:, :].astype(F32), axis=1)
    ids_out[...] = names.astype(jnp.int32)
    for copy in remote.started + wide:
        copy.wait_send()


def gather_call(cq, ck, nq, nk, qg, kg, cv, nv, gc, gn, owned):
    return pl.pallas_call(
        gather_kernel,
        name="gather_keys",
        out_shape=(
            jax.ShapeDtypeStruct((16, PACKET, HD), BF16),
            jax.ShapeDtypeStruct((16, 512, HD), BF16),
            jax.ShapeDtypeStruct((4, 2, BLK, HD), BF16),
            jax.ShapeDtypeStruct((4, 2, BLK, HD), BF16),
            jax.ShapeDtypeStruct((4, BLK, HD), BF16),
            jax.ShapeDtypeStruct((4, BLK, HD), BF16),
            jax.ShapeDtypeStruct((4, BLK, 2 * BLK), F32),
            jax.ShapeDtypeStruct((4, BLK, 2 * BLK), F32),
            jax.ShapeDtypeStruct((4, HD, 2 * BLK), F32),
            jax.ShapeDtypeStruct((8, 512), F32),
            jax.ShapeDtypeStruct((16, HD), jnp.int32),
        ),
        in_specs=[HBM] * 11,
        out_specs=(VMEM,) * 11,
        scratch_shapes=[
            pltpu.SMEM((2,), jnp.int32),
            pltpu.VMEM((4, 512, 256), BF16),
            pltpu.VMEM((1, 256), F32),
            pltpu.VMEM((1, 256), F32),
            pltpu.VMEM((PACKET, 256), BF16),
            pltpu.VMEM((3, 2, BLK, 2 * HD), BF16),
            pltpu.VMEM((8, 8, 512), F32),
            pltpu.SemaphoreType.DMA((32,)),
            pltpu.SemaphoreType.DMA((32,)),
            pltpu.SemaphoreType.DMA((6, 2)),
            pltpu.SemaphoreType.DMA((6, 2)),
            pltpu.SemaphoreType.DMA((16,)),
        ],
        compiler_params=pltpu.CompilerParams(
            collective_id=0, has_side_effects=True, vmem_limit_bytes=20 * 2**20
        ),
    )(cq, ck, nq, nk, qg, kg, cv, nv, gc, gn, owned)


def attention_kernel(
    ids, docs, kall, vall, qq, gg, kn, vn, own_s, own_d, grads_t,
    out_t, dq_t, dk_noisy, dv_noisy, dk_acc, dv_acc,
    where_is, first_of, tile_query, tile_key, weights, peaks, totals_of, deltas,
):
    chip = lax.axis_index("ctx") // 2
    scale = 1.0 / math.sqrt(HD)
    scale2 = scale * math.log2(math.e)

    @pl.loop(0, 16)
    def _(packet):
        where_is[ids[packet, 0]] = packet * 2
        where_is[ids[packet, 1]] = packet * 2 + 1

    first_of[0] = 0

    @pl.loop(1, 32)
    def _(block):
        first_of[block] = jnp.where(docs[block] == docs[block - 1], first_of[block - 1], block)

    @pl.loop(0, 32)
    def _(block):
        dk_acc[block] = jnp.zeros((BLK, HD), F32)
        dv_acc[block] = jnp.zeros((BLK, HD), F32)

    def key_rows(buf, stored):
        start = pl.multiple_of((stored % 2) * BLK, BLK)
        return buf[stored // 2, pl.ds(start, BLK), :]

    def both(ref, index):
        return ref[index].reshape(2 * BLK, HD)

    def tops(scores):
        return jnp.max(scores.reshape(BLK // 8, 8, scores.shape[1]), axis=0)

    def totals(values):
        return jnp.sum(values.reshape(BLK // 8, 8, values.shape[1]), axis=0)

    def two_blocks(side):
        indices = [2 * side, 2 * side + 1]
        count = 0
        for half, index in enumerate(indices):
            block = ids[chip * 2 + side, half]

            def enlist(key_block, count, index=index):
                tile_query[count] = index
                tile_key[count] = where_is[key_block]
                return count + 1

            count = lax.fori_loop(first_of[block], block, enlist, count)

        def over_tiles(body):
            groups = count // GROUP

            @pl.loop(0, groups)
            def _(group):
                body([group * GROUP + i for i in range(GROUP)])

            @pl.loop(groups * GROUP, count)
            def _(tile):
                body([tile])

        for index in indices:
            peaks[index] = tops(own_s[index])

        def score_tiles(tiles):
            queries = [tile_query[tile] for tile in tiles]
            scores = [
                dot(key_rows(kall, tile_key[tile]), both(qq, query), LAST)
                for tile, query in zip(tiles, queries)
            ]
            for tile, query, score in zip(tiles, queries, scores):
                weights[tile] = score
                peaks[query] = jnp.maximum(peaks[query], tops(score))

        over_tiles(score_tiles)

        for index in indices:
            peak = jnp.max(peaks[index], axis=0, keepdims=True) * scale2
            peaks[index] = jnp.broadcast_to(peak, (8, 2 * BLK))
            own = jnp.exp2(own_s[index] * scale2 - peak)
            totals_of[index] = totals(own)
            own_low = own.astype(BF16)
            out_t[index, :, :BLK] = dot(key_rows(vall, chip * 4 + index), own_low[:, :BLK], FIRST)
            out_t[index, :, BLK:] = dot(vn[index], own_low[:, BLK:], FIRST)

        def value_tiles(tiles):
            queries = [tile_query[tile] for tile in tiles]
            probs = [
                jnp.exp2(weights[tile] * scale2 - peaks[query, :1])
                for tile, query in zip(tiles, queries)
            ]
            outs = [
                dot(key_rows(vall, tile_key[tile]), prob.astype(BF16), FIRST)
                for tile, prob in zip(tiles, probs)
            ]
            for tile, query, prob, out in zip(tiles, queries, probs, outs):
                weights[tile] = prob
                totals_of[query] += totals(prob)
                out_t[query] += out

        over_tiles(value_tiles)

        for index in indices:
            stored_own = chip * 4 + index
            inverse_total = 1.0 / jnp.sum(totals_of[index], axis=0, keepdims=True)
            out = out_t[index] * inverse_total
            out_t[index] = out
            delta = jnp.sum(out * grads_t[index], axis=0, keepdims=True)
            totals_of[index] = jnp.broadcast_to(inverse_total, (8, 2 * BLK))
            deltas[index] = jnp.broadcast_to(delta, (8, 2 * BLK))
            own = jnp.exp2(own_s[index] * scale2 - peaks[index, :1]) * inverse_total
            own_low = own.astype(BF16)
            own_ds = (own * (own_d[index] - delta)).astype(BF16)
            dv_acc[stored_own] += dot(own_low[:, :BLK], gg[index, 0], PLAIN)
            dk_acc[stored_own] += dot(own_ds[:, :BLK], qq[index, 0], PLAIN)
            dv_noisy[index] = dot(own_low[:, BLK:], gg[index, 1], PLAIN)
            dk_noisy[index] = dot(own_ds[:, BLK:], qq[index, 1], PLAIN) * scale
            dq_t[index, :, :BLK] = dot(key_rows(kall, stored_own), own_ds[:, :BLK], FIRST)
            dq_t[index, :, BLK:] = dot(kn[index], own_ds[:, BLK:], FIRST)

        def grad_tiles(tiles):
            queries = [tile_query[tile] for tile in tiles]
            stored = [tile_key[tile] for tile in tiles]
            probs = [weights[tile] * totals_of[query, :1] for tile, query in zip(tiles, queries)]
            dps = [
                dot(key_rows(vall, key), both(gg, query), LAST) for key, query in zip(stored, queries)
            ]
            dvs = [dot(prob.astype(BF16), both(gg, query), PLAIN) for prob, query in zip(probs, queries)]
            dss = [
                (prob * (dp - deltas[query, :1])).astype(BF16)
                for prob, dp, query in zip(probs, dps, queries)
            ]
            dks = [dot(ds, both(qq, query), PLAIN) for ds, query in zip(dss, queries)]
            dqs = [dot(key_rows(kall, key), ds, FIRST) for key, ds in zip(stored, dss)]
            for key, query, dv, dk, dq in zip(stored, queries, dvs, dks, dqs):
                dv_acc[key] += dv
                dk_acc[key] += dk
                dq_t[query] += dq

        over_tiles(grad_tiles)

    @pl.loop(0, 2)
    def _(side):
        two_blocks(side)


def attention_call(ids, docs, *parts):
    return pl.pallas_call(
        attention_kernel,
        name="attention",
        out_shape=(
            jax.ShapeDtypeStruct((4, HD, 2 * BLK), F32),
            jax.ShapeDtypeStruct((4, HD, 2 * BLK), F32),
            jax.ShapeDtypeStruct((4, BLK, HD), F32),
            jax.ShapeDtypeStruct((4, BLK, HD), F32),
            jax.ShapeDtypeStruct((32, BLK, HD), F32),
            jax.ShapeDtypeStruct((32, BLK, HD), F32),
        ),
        in_specs=[SMEM, SMEM] + [VMEM] * 9,
        out_specs=(VMEM,) * 6,
        scratch_shapes=[
            pltpu.SMEM((32,), jnp.int32),
            pltpu.SMEM((32,), jnp.int32),
            pltpu.SMEM((32,), jnp.int32),
            pltpu.SMEM((32,), jnp.int32),
            pltpu.VMEM((30, BLK, 2 * BLK), F32),
            pltpu.VMEM((4, 8, 2 * BLK), F32),
            pltpu.VMEM((4, 8, 2 * BLK), F32),
            pltpu.VMEM((4, 8, 2 * BLK), F32),
        ],
        compiler_params=pltpu.CompilerParams(vmem_limit_bytes=28 * 2**20),
    )(ids, docs, *parts)


def scatter_kernel(
    cq_h, ck_h, nq_h, nk_h, qg_h, kg_h, inv, out_t, dq_t, dk_noisy, dv_noisy, dk, dv,
    back, fin, inner_out,
    raws, qg, kg, stage, k_out, v_out, x_out, vy, vq, vh, vx, kh, kx, ky, away, sums,
    send, recv, lsem,
):
    ctx, head, core, y, x = place()
    right, left = (x + 1) % 4, (x + 3) % 4
    partner = ctx_of(x, y, 1 - core)
    to_right, to_left = ctx_of(right, y, core), ctx_of(left, y, core)
    to_y = ctx_of(x, 1 - y, core)
    score_scale = 1.0 / math.sqrt(HD)
    own_columns = pl.ds(pl.multiple_of(core * HD, HD), HD)
    local = Locals(lsem)
    loads = [local.start(ref, raws.at[i]) for i, ref in enumerate((cq_h, ck_h, nq_h, nk_h))]
    loads += [local.start(qg_h, qg), local.start(kg_h, kg)]
    cq, ck, nq, nk = [raws.at[i] for i in range(4)]
    remote = Copies(send, recv, head)

    def mine(ref, step, row, half):
        chip = chip_of((x + step) % 4, y if row == 0 else 1 - y)
        return ref[pl.ds(chip * 4 + half * 2, 2)].reshape(512, HD)

    def pack_v(step):
        for half in range(2):
            v_out[step, half] = mine(dv, step, 1, half).astype(BF16)

    def pack_k(row, step, half, *others):
        value = mine(dk, step, row, half) * score_scale
        for other in others:
            value = value + other[...].astype(F32)
        k_out[row, step, half] = value.astype(BF16)

    pack_v(2)
    pack_k(1, 2, 0)
    pack_k(1, 2, 1)
    enter(ctx, head, [partner, to_right, to_left, to_y])
    first, rest = pl.ds(0, SHIFT), pl.ds(SHIFT, 512 - SHIFT)
    v_far = [
        remote.start(v_out.at[2, 0, first], vq.at[0], to_left),
        remote.start(v_out.at[2, 1, first], vq.at[1], to_right),
    ]
    v_opposite = [
        remote.start(v_out.at[2, half, rest], vy.at[2, half, rest], to_y) for half in range(2)
    ]
    k_half = {}

    def start_half(row):
        k_half[row, 0] = remote.start(k_out.at[row, 2, 0], kh.at[row, 0], to_left)
        k_half[row, 1] = remote.start(k_out.at[row, 2, 1], kh.at[row, 1], to_right)

    start_half(1)
    pack_k(0, 2, 0)
    pack_k(0, 2, 1)
    start_half(0)
    v_y = {}

    def send_v(step, half):
        pack_v(step)
        if half is not None:
            v_far[half].wait_recv()
            v_out[step, half, :SHIFT] = (
                mine(dv, step, 1, half)[:SHIFT] + vq[half].astype(F32)
            ).astype(BF16)
        v_y[step] = remote.start(v_out.at[step], vy.at[step], to_y)

    send_v(3, 0)
    for row in (1, 0):
        pack_k(row, 3, 1)
        pack_k(row, 1, 0)

    def landing(i):
        return back.at[i, :, own_columns]

    swap = {}
    dk_pair, dv_pair = [
        [ref.at[pl.ds(c * 2, 2)] for c in (core, 1 - core)] for ref in (dk_noisy, dv_noisy)
    ]

    def turn(index, ref, first, factor):
        for part in range(2):
            rows = slice(part * BLK, part * BLK + BLK)
            for c, own in ((core, True), (1 - core, False)):
                values = jnp.transpose(ref[2 * c + part]) * factor
                for kind in range(2):
                    if own:
                        back[first + kind, rows, own_columns] = values[kind * BLK : kind * BLK + BLK]
                    else:
                        stage[first + kind, rows, :] = values[kind * BLK : kind * BLK + BLK]
        for i in (first, first + 1):
            swap[i] = remote.start(stage.at[i], landing(i), partner)

    def turn_noisy(ref, i):
        for part in range(2):
            rows = slice(part * BLK, part * BLK + BLK)
            back[i, rows, own_columns] = ref[2 * core + part]
            stage[i, rows, :] = ref[2 * (1 - core) + part]
        swap[i] = remote.start(stage.at[i], landing(i), partner)

    turn(0, dq_t, 2, score_scale)
    turn_noisy(dk_noisy, 4)

    k_x = {}

    def k_forward(row):
        k_half[row, 0].wait_recv()
        pack_k(row, 3, 0, kh.at[row, 0])
        k_x[row, 0] = remote.start(k_out.at[row, 3], kx.at[row, 0], to_left)
        k_half[row, 1].wait_recv()
        pack_k(row, 1, 1, kh.at[row, 1])
        k_x[row, 1] = remote.start(k_out.at[row, 1], kx.at[row, 1], to_right)

    k_forward(1)

    row = lax.broadcasted_iota(jnp.int32, (8, 512), 0)

    def inner(raw, gain, values):
        return row_sums(raw[...].astype(F32) * (gain[...] * values))

    for copy in loads:
        copy.wait()
    for i in (2, 3, 4):
        swap[i].wait_recv()
    total = jnp.zeros((8, 512), F32)
    normal = ((0, cq, qg, 2), (2, nq, qg, 3), (3, nk, kg, 4))
    for index, raw, gain, i in normal:
        total = jnp.where(row == index, inner(raw, gain, back[i]), total)
    sums[0] = total
    exchange = [
        remote.start(sums.at[0], sums.at[step], ctx, (head + step) % 8) for step in range(1, 8)
    ]

    def pack_x(step, half, *others):
        value = mine(dv, step, 0, half)
        for other in others:
            value = value + other[...].astype(F32)
        x_out[step, half] = value.astype(BF16)

    v_half = []
    for half, target in ((0, to_left), (1, to_right)):
        v_opposite[half].wait_recv()
        pack_x(2, half)
        x_out[2, half, SHIFT:] = (
            mine(dv, 2, 0, half)[SHIFT:] + vy[2, half, SHIFT:].astype(F32)
        ).astype(BF16)
        v_half.append(remote.start(x_out.at[2, half], vh.at[half], target))
    send_v(1, 1)
    k_forward(0)
    turn(0, out_t, 0, 1.0)
    turn_noisy(dv_noisy, 5)
    k_x[1, 0].wait_recv()
    k_x[1, 1].wait_recv()
    for half in range(2):
        pack_k(1, 0, half, kx.at[1, 0, half], kx.at[1, 1, half])
    k_y = remote.start(k_out.at[1, 0], ky, to_y)
    send_v(0, None)

    v_y[3].wait_recv()
    v_half[0].wait_recv()
    pack_x(3, 0, vy.at[3, 0], vh.at[0])
    pack_x(3, 1, vy.at[3, 1])
    v_x = [remote.start(x_out.at[3], vx.at[0], to_left)]
    v_y[1].wait_recv()
    v_half[1].wait_recv()
    pack_x(1, 0, vy.at[1, 0])
    pack_x(1, 1, vy.at[1, 1], vh.at[1])
    v_x.append(remote.start(x_out.at[1], vx.at[1], to_right))

    for copy in exchange:
        copy.wait_recv()
    total = sums[0]
    for step in range(1, 8):
        total = total + sums[step]
    inverses = jnp.transpose(inv[...])
    means = jnp.transpose(total) / FEAT
    for index, raw, gain, i in normal:
        inverse = inverses[:, index : index + 1]
        factor = inverse * inverse * inverse * means[:, index : index + 1]
        back[i] = inverse * (gain[...] * back[i]) - raw[...].astype(F32) * factor

    def finish(index, ref, factor, terms):
        values = []
        for half in range(2):
            value = mine(ref, 0, 0, half) * factor
            for term in terms:
                value = value + term[half].astype(F32)
            values.append(value)
        first_core = core == 0
        fin[index, :, own_columns] = jnp.where(first_core, values[0], values[1])
        away[index] = jnp.where(first_core, values[1], values[0])
        return remote.start(away.at[index], fin.at[index, :, own_columns], partner)

    k_x[0, 0].wait_recv()
    k_x[0, 1].wait_recv()
    k_y.wait_recv()
    k_fin = finish(0, dk, score_scale, (kx.at[0, 0], kx.at[0, 1], ky))
    k_fin.wait_recv()
    sums[8] = inner(ck, kg, fin[0])
    k_exchange = [
        remote.start(sums.at[8], sums.at[8 + step], ctx, (head + step) % 8) for step in range(1, 8)
    ]
    v_y[0].wait_recv()
    v_x[0].wait_recv()
    v_x[1].wait_recv()
    v_fin = finish(1, dv, 1.0, (vy.at[0], vx.at[0], vx.at[1]))

    for copy in k_exchange:
        copy.wait_recv()
    total = sums[8]
    for step in range(1, 8):
        total = total + sums[8 + step]
    inner_out[...] = total
    v_fin.wait_recv()
    for i in (0, 1, 5):
        swap[i].wait_recv()
    for copy in remote.started:
        copy.wait_send()


def scatter_call(*operands):
    return pl.pallas_call(
        scatter_kernel,
        name="scatter_grads",
        out_shape=(
            jax.ShapeDtypeStruct((6, 512, 256), F32),
            jax.ShapeDtypeStruct((2, 512, 256), F32),
            jax.ShapeDtypeStruct((8, 512), F32),
        ),
        in_specs=[HBM] * 6 + [VMEM] * 7,
        out_specs=(VMEM, VMEM, VMEM),
        scratch_shapes=[
            pltpu.VMEM((4, 512, 256), BF16),
            pltpu.VMEM((1, 256), F32),
            pltpu.VMEM((1, 256), F32),
            pltpu.VMEM((6, 512, HD), F32),
            pltpu.VMEM((2, 4, 2, 512, HD), BF16),
            pltpu.VMEM((4, 2, 512, HD), BF16),
            pltpu.VMEM((4, 2, 512, HD), BF16),
            pltpu.VMEM((4, 2, 512, HD), BF16),
            pltpu.VMEM((2, SHIFT, HD), BF16),
            pltpu.VMEM((2, 512, HD), BF16),
            pltpu.VMEM((2, 2, 512, HD), BF16),
            pltpu.VMEM((2, 2, 512, HD), BF16),
            pltpu.VMEM((2, 2, 2, 512, HD), BF16),
            pltpu.VMEM((2, 512, HD), BF16),
            pltpu.VMEM((2, 512, HD), F32),
            pltpu.VMEM((16, 8, 512), F32),
            pltpu.SemaphoreType.DMA((48,)),
            pltpu.SemaphoreType.DMA((48,)),
            pltpu.SemaphoreType.DMA((8,)),
        ],
        compiler_params=pltpu.CompilerParams(
            collective_id=1, has_side_effects=True, vmem_limit_bytes=20 * 2**20
        ),
    )(*operands)


def finish_kernel(
    ck, kg, inv, inner, back, fin,
    out_clean, out_noisy, dq_clean, dk_clean, dv_clean, dq_noisy, dk_noisy, dv_noisy,
    dk, sems,
):
    local = Locals(sems)
    copies = [
        local.start(source, target)
        for source, target in (
            (back.at[0], out_clean),
            (back.at[1], out_noisy),
            (back.at[2], dq_clean),
            (back.at[3], dq_noisy),
            (back.at[4], dk_noisy),
            (back.at[5], dv_noisy),
            (fin.at[1], dv_clean),
        )
    ]
    inverse = jnp.transpose(inv[...])[:, 1:2]
    mean = jnp.transpose(inner[...])[:, :1] / FEAT
    factor = inverse * inverse * inverse * mean
    dk[...] = inverse * (kg[...] * fin[0]) - ck[...].astype(F32) * factor
    copies.append(local.start(dk, dk_clean))
    for copy in copies:
        copy.wait()


def finish_call(*operands):
    return pl.pallas_call(
        finish_kernel,
        name="finish",
        out_shape=tuple(jax.ShapeDtypeStruct((512, 256), F32) for _ in range(8)),
        in_specs=[VMEM] * 6,
        out_specs=(HBM,) * 8,
        scratch_shapes=[pltpu.VMEM((512, 256), F32), pltpu.SemaphoreType.DMA((8,))],
        compiler_params=pltpu.CompilerParams(vmem_limit_bytes=16 * 2**20),
    )(*operands)


def local(
    clean_q, clean_k, clean_v, noisy_q, noisy_k, noisy_v,
    q_gain, k_gain, grad_clean, grad_noisy, owned_blocks, block_doc,
):
    qg = q_gain.reshape(1, 256)
    kg = k_gain.reshape(1, 256)
    blocks = [a.reshape(2, BLK, 2 * HD) for a in (noisy_v, grad_clean, grad_noisy)]
    *pinned, docs = [
        pltpu.with_memory_space_constraint(a, pltpu.HBM)
        for a in (
            clean_q, clean_k, noisy_q, noisy_k, qg, kg, clean_v, *blocks, owned_blocks, block_doc,
        )
    ]
    *parts, inv, ids = gather_call(*pinned)
    grads = attention_call(ids, docs, *parts)
    back, fin, inner = scatter_call(*pinned[:6], inv, *grads)
    return finish_call(clean_k, kg, inv, inner, back, fin)


def solution(mesh):
    placed = (P("ctx", "head"),) * 6 + (P("head"),) * 2 + (P("ctx", "head"),) * 2 + (P("ctx"), P())
    return jax.shard_map(
        local,
        mesh=mesh,
        in_specs=placed,
        out_specs=(P("ctx", "head"),) * 8,
        check_vma=False,
    )
```

time: 105 us -> 101 us (0.962)
  the two profiles are of different devices: /device:TPU:5 before, /device:TPU:1 now
where the time goes in v3:
time: 101 us
  Pallas kernels  99.8 us (99%)
    pallas_call x1, Pallas kernels, scatter_call(): pl.pallas_call(scatter_kernel, name='scatter_grads', out_shape=(jax.Shape...  44 us
    pallas_call x1, Pallas kernels, gather_call(): pl.pallas_call(gather_kernel, name='gather_keys', out_shape=(jax.ShapeDty...  40 us
    pallas_call x1, Pallas kernels, attention_call(): pl.pallas_call(attention_kernel, name='attention', out_shape=(jax.ShapeDt...  13.8 us
    pallas_call x1, Pallas kernels, finish_call(): pl.pallas_call(finish_kernel, name='finish', out_shape=tuple((jax.ShapeDt...  2.07 us

profile of v3, /device:TPU:1, one launch (start us, length us, event | category | flops | bytes accessed | tf_op | source)
XLA Modules:
  0.0 100.5 jit_solution(13021230380616228304)
XLA Ops:
  0.6 40.0 %gather_keys.1 = (bf16[16,528,128]{2,1,0:T(8,128)(2,1)S(1)}, bf16[16,512,128]{2,1,0:T(8,128)(2,1)S(1)}, bf16[4,2,256,128]{3,2,1,0:T(8,128)(2,1)S(1)}, bf16[4,2,2...) custom-call(bf16[512,256]{1,0:T(8,128)(2,1)} %cq_h.3, ...), custom_call_target="tpu_custom_call" | custom-call | tf_op jit(solution)/shard_map/gather_keys/pallas_call | solution.py:277
  40.6 13.8 %attention.1 = (f32[4,128,512]{2,1,0:T(8,128)S(1)}, f32[4,128,512]{2,1,0:T(8,128)S(1)}, f32[4,256,128]{2,1,0:T(8,128)S(1)}, f32[4,256,128]{2,1,0:T(8,128)S(1)}, ...) custom-call(s32[16,128]{1,0:T(8,128)S(1)} %get-tuple-element.29.ids, s32[32]{0:T(128)} %docs.1, ...), custom_call_target="tpu_custom_call" | custom-call | tf_op jit(solution)/shard_map/attention/pallas_call | solution.py:463
  54.4 0.0 copy-start
  54.5 0.0 copy-start.1
  54.5 44.0 %scatter_grads.1 = (f32[6,512,256]{2,1,0:T(8,128)S(1)}, f32[2,512,256]{2,1,0:T(8,128)S(1)}, f32[8,512]{1,0:T(8,128)S(1)}) custom-call(bf16[512,256]{1,0:T(8,128)(2,1)} %cq_h.3, bf16[512,256]{1,0:T(8,128)(2,1)} %ck.1, bf16[512,256]{1,0:T(8,128)(2,1)} %nq_h.3, bf16[512,256]{1,0:T(8,128)(2,1)} %nk_h.3, f32[1,256]{1,0:T(1,128)} %bitcast.12, f32[1,256]{1,0:T(1,128)} %bitcast.6, ...), custom_call_target="tpu_custom_call" | custom-call | tf_op jit(solution)/shard_map/scatter_grads/pallas_call | solution.py:710
  98.4 0.0 copy-done
  98.4 0.0 copy-done.1
  98.5 2.1 %finish.1 = (f32[512,256]{1,0:T(8,128)}, f32[512,256]{1,0:T(8,128)}, f32[512,256]{1,0:T(8,128)}, f32[512,256]{1,0:T(8,128)}, f32[512,256]{1,0:T(8,128)}, /*index...) custom-call(bf16[512,256]{1,0:T(8,128)(2,1)S(1)} %copy-done, f32[1,256]{1,0:T(1,128)S(1)} %bitcast.7, ...), custom_call_target="tpu_custom_call" | custom-call | tf_op jit(solution)/shard_map/finish/pallas_call | solution.py:775
Async XLA Ops:
  54.4 44.0 %copy-start = (bf16[512,256]{1,0:T(8,128)(2,1)S(1)}, bf16[512,256]{1,0:T(8,128)(2,1)}, u32[]{:S(2)}) copy-start(bf16[512,256]{1,0:T(8,128)(2,1)} %ck.1) | copy-start | bytes 786436
  54.5 44.0 %copy-start.1 = (f32[256]{0:T(256)S(1)}, f32[256]{0:T(256)}, u32[]{:S(2)}) copy-start(f32[256]{0:T(256)} %param.19) | copy-start | bytes 3076

commit v4 on v3

--- a/solution.py
+++ b/solution.py
@@ -101,7 +101,7 @@
 
 def gather_kernel(
     cq_h, ck_h, nq_h, nk_h, qg_h, kg_h, cv, nv, gc, gn, owned,
-    kall, vall, qq, gg, kn, vn, own_s, own_d, grads_t, inv_out, ids_out,
+    kall, vall, qq, gg, kn, vn, own_s, grads_t, inv_out, ids_out,
     owned_s, raws, qg, kg, k_packet, normed, sums, send, recv, wide_send, wide_recv, lsem,
 ):
     ctx, head, core, y, x = place()
@@ -237,8 +237,6 @@
         grad_clean, grad_noisy = gg[index, 0], gg[index, 1]
         own_s[index, :, :BLK] = dot(kall[packet, rows, :], qq[index, 0], LAST)
         own_s[index, :, BLK:] = dot(kn[index], qq[index, 1], LAST)
-        own_d[index, :, :BLK] = dot(vall[packet, rows, :], grad_clean, LAST)
-        own_d[index, :, BLK:] = dot(vn[index], grad_noisy, LAST)
         grads_t[index, :, :BLK] = jnp.transpose(grad_clean.astype(F32))
         grads_t[index, :, BLK:] = jnp.transpose(grad_noisy.astype(F32))
 
@@ -285,13 +283,12 @@
             jax.ShapeDtypeStruct((4, BLK, HD), BF16),
             jax.ShapeDtypeStruct((4, BLK, HD), BF16),
             jax.ShapeDtypeStruct((4, BLK, 2 * BLK), F32),
-            jax.ShapeDtypeStruct((4, BLK, 2 * BLK), F32),
             jax.ShapeDtypeStruct((4, HD, 2 * BLK), F32),
             jax.ShapeDtypeStruct((8, 512), F32),
             jax.ShapeDtypeStruct((16, HD), jnp.int32),
         ),
         in_specs=[HBM] * 11,
-        out_specs=(VMEM,) * 11,
+        out_specs=(VMEM,) * 10,
         scratch_shapes=[
             pltpu.SMEM((2,), jnp.int32),
             pltpu.VMEM((4, 512, 256), BF16),
@@ -313,9 +310,10 @@
 
 
 def attention_kernel(
-    ids, docs, kall, vall, qq, gg, kn, vn, own_s, own_d, grads_t,
+    ids, docs, kall, vall, qq, gg, kn, vn, own_s, grads_t,
     out_t, dq_t, dk_noisy, dv_noisy, dk_acc, dv_acc,
-    where_is, first_of, tile_query, tile_key, weights, peaks, totals_of, deltas,
+    where_is, first_of, pair_query, pair_key, pair_bias,
+    scores, weights, own_weights, scaled_grads, peaks, sums, deltas,
 ):
     chip = lax.axis_index("ctx") // 2
     scale = 1.0 / math.sqrt(HD)
@@ -341,29 +339,38 @@
         start = pl.multiple_of((stored % 2) * BLK, BLK)
         return buf[stored // 2, pl.ds(start, BLK), :]
 
+    def key_pair(buf, pair):
+        return jnp.concatenate(
+            [key_rows(buf, pair_key[2 * pair]), key_rows(buf, pair_key[2 * pair + 1])], axis=0
+        )
+
     def both(ref, index):
         return ref[index].reshape(2 * BLK, HD)
 
-    def tops(scores):
-        return jnp.max(scores.reshape(BLK // 8, 8, scores.shape[1]), axis=0)
+    def tops(values):
+        return jnp.max(values.reshape(-1, 8, values.shape[1]), axis=0)
 
     def totals(values):
-        return jnp.sum(values.reshape(BLK // 8, 8, values.shape[1]), axis=0)
-
-    def two_blocks(side):
-        indices = [2 * side, 2 * side + 1]
+        return jnp.sum(values.reshape(-1, 8, values.shape[1]), axis=0)
+
+    @pl.loop(0, 2)
+    def _(side):
         count = 0
-        for half, index in enumerate(indices):
+        for half in range(2):
             block = ids[chip * 2 + side, half]
-
-            def enlist(key_block, count, index=index):
-                tile_query[count] = index
-                tile_key[count] = where_is[key_block]
+            begin = first_of[block]
+
+            def enlist(pair, count, half=half, block=block, begin=begin):
+                key = begin + 2 * pair
+                pair_query[count] = half
+                pair_key[2 * count] = where_is[key]
+                pair_key[2 * count + 1] = where_is[jnp.minimum(key + 1, block - 1)]
+                pair_bias[count] = jnp.where(key + 1 < block, 0, 1)
                 return count + 1
 
-            count = lax.fori_loop(first_of[block], block, enlist, count)
-
-        def over_tiles(body):
+            count = lax.fori_loop(0, (block - begin + 1) // 2, enlist, count)
+
+        def over_pairs(body):
             groups = count // GROUP
 
             @pl.loop(0, groups)
@@ -371,92 +378,103 @@
                 body([group * GROUP + i for i in range(GROUP)])
 
             @pl.loop(groups * GROUP, count)
-            def _(tile):
-                body([tile])
-
-        for index in indices:
-            peaks[index] = tops(own_s[index])
-
-        def score_tiles(tiles):
-            queries = [tile_query[tile] for tile in tiles]
-            scores = [
-                dot(key_rows(kall, tile_key[tile]), both(qq, query), LAST)
-                for tile, query in zip(tiles, queries)
+            def _(pair):
+                body([pair])
+
+        first = 2 * side
+        for half in range(2):
+            peaks[half] = tops(own_s[first + half])
+
+        def score_pairs(pairs):
+            queries = [pair_query[pair] for pair in pairs]
+            values = [
+                dot(key_pair(kall, pair), both(qq, first + query), LAST)
+                for pair, query in zip(pairs, queries)
             ]
-            for tile, query, score in zip(tiles, queries, scores):
-                weights[tile] = score
-                peaks[query] = jnp.maximum(peaks[query], tops(score))
-
-        over_tiles(score_tiles)
-
-        for index in indices:
-            peak = jnp.max(peaks[index], axis=0, keepdims=True) * scale2
-            peaks[index] = jnp.broadcast_to(peak, (8, 2 * BLK))
+            for pair, query, value in zip(pairs, queries, values):
+                scores[pair] = value
+                peaks[query] = jnp.maximum(peaks[query], tops(value))
+
+        over_pairs(score_pairs)
+
+        for half in range(2):
+            index = first + half
+            peak = jnp.max(peaks[half], axis=0, keepdims=True) * scale2
+            peaks[half] = jnp.broadcast_to(peak, (8, 2 * BLK))
             own = jnp.exp2(own_s[index] * scale2 - peak)
-            totals_of[index] = totals(own)
+            sums[half] = totals(own)
             own_low = own.astype(BF16)
+            own_weights[half] = own_low
             out_t[index, :, :BLK] = dot(key_rows(vall, chip * 4 + index), own_low[:, :BLK], FIRST)
             out_t[index, :, BLK:] = dot(vn[index], own_low[:, BLK:], FIRST)
 
-        def value_tiles(tiles):
-            queries = [tile_query[tile] for tile in tiles]
-            probs = [
-                jnp.exp2(weights[tile] * scale2 - peaks[query, :1])
-                for tile, query in zip(tiles, queries)
-            ]
-            outs = [
-                dot(key_rows(vall, tile_key[tile]), prob.astype(BF16), FIRST)
-                for tile, prob in zip(tiles, probs)
-            ]
-            for tile, query, prob, out in zip(tiles, queries, probs, outs):
-                weights[tile] = prob
-                totals_of[query] += totals(prob)
-                out_t[query] += out
-
-        over_tiles(value_tiles)
-
-        for index in indices:
+        def value_pairs(pairs):
+            queries = [pair_query[pair] for pair in pairs]
+            outs, parts = [], []
+            for pair, query in zip(pairs, queries):
+                peak = peaks[query, :1]
+                hidden = peak + jnp.where(pair_bias[pair] == 1, jnp.inf, 0.0)
+                upper = jnp.exp2(scores[pair, :BLK] * scale2 - peak)
+                lower = jnp.exp2(scores[pair, BLK:] * scale2 - hidden)
+                low = jnp.concatenate([upper.astype(BF16), lower.astype(BF16)], axis=0)
+                weights[pair] = low
+                outs.append(dot(key_pair(vall, pair), low, FIRST))
+                parts.append(totals(upper) + totals(lower))
+            for query, out, part in zip(queries, outs, parts):
+                sums[query] += part
+                out_t[first + query] += out
+
+        over_pairs(value_pairs)
+
+        for half in range(2):
+            index = first + half
             stored_own = chip * 4 + index
-            inverse_total = 1.0 / jnp.sum(totals_of[index], axis=0, keepdims=True)
-            out = out_t[index] * inverse_total
+            inverse_sum = 1.0 / jnp.sum(sums[half], axis=0, keepdims=True)
+            out = out_t[index] * inverse_sum
             out_t[index] = out
-            delta = jnp.sum(out * grads_t[index], axis=0, keepdims=True)
-            totals_of[index] = jnp.broadcast_to(inverse_total, (8, 2 * BLK))
-            deltas[index] = jnp.broadcast_to(delta, (8, 2 * BLK))
-            own = jnp.exp2(own_s[index] * scale2 - peaks[index, :1]) * inverse_total
-            own_low = own.astype(BF16)
-            own_ds = (own * (own_d[index] - delta)).astype(BF16)
-            dv_acc[stored_own] += dot(own_low[:, :BLK], gg[index, 0], PLAIN)
+            grad_rows = (grads_t[index] * inverse_sum).astype(BF16).astype(F32)
+            delta = jnp.sum(out * grad_rows, axis=0, keepdims=True)
+            deltas[half] = jnp.broadcast_to(delta, (8, 2 * BLK))
+            grads = jnp.transpose(grad_rows).astype(BF16)
+            scaled_grads[half] = grads
+            own_low = own_weights[half]
+            own_dp = jnp.concatenate(
+                [
+                    dot(key_rows(vall, stored_own), grads[:BLK], LAST),
+                    dot(vn[index], grads[BLK:], LAST),
+                ],
+                axis=1,
+            )
+            own_ds = (own_low.astype(F32) * (own_dp - delta)).astype(BF16)
+            dv_acc[stored_own] += dot(own_low[:, :BLK], grads[:BLK], PLAIN)
             dk_acc[stored_own] += dot(own_ds[:, :BLK], qq[index, 0], PLAIN)
-            dv_noisy[index] = dot(own_low[:, BLK:], gg[index, 1], PLAIN)
+            dv_noisy[index] = dot(own_low[:, BLK:], grads[BLK:], PLAIN)
             dk_noisy[index] = dot(own_ds[:, BLK:], qq[index, 1], PLAIN) * scale
             dq_t[index, :, :BLK] = dot(key_rows(kall, stored_own), own_ds[:, :BLK], FIRST)
             dq_t[index, :, BLK:] = dot(kn[index], own_ds[:, BLK:], FIRST)
 
-        def grad_tiles(tiles):
-            queries = [tile_query[tile] for tile in tiles]
-            stored = [tile_key[tile] for tile in tiles]
-            probs = [weights[tile] * totals_of[query, :1] for tile, query in zip(tiles, queries)]
-            dps = [
-                dot(key_rows(vall, key), both(gg, query), LAST) for key, query in zip(stored, queries)
-            ]
-            dvs = [dot(prob.astype(BF16), both(gg, query), PLAIN) for prob, query in zip(probs, queries)]
-            dss = [
-                (prob * (dp - deltas[query, :1])).astype(BF16)
-                for prob, dp, query in zip(probs, dps, queries)
-            ]
-            dks = [dot(ds, both(qq, query), PLAIN) for ds, query in zip(dss, queries)]
-            dqs = [dot(key_rows(kall, key), ds, FIRST) for key, ds in zip(stored, dss)]
-            for key, query, dv, dk, dq in zip(stored, queries, dvs, dks, dqs):
-                dv_acc[key] += dv
-                dk_acc[key] += dk
-                dq_t[query] += dq
-
-        over_tiles(grad_tiles)
-
-    @pl.loop(0, 2)
-    def _(side):
-        two_blocks(side)
+        def grad_pairs(pairs):
+            queries = [pair_query[pair] for pair in pairs]
+            results = []
+            for pair, query in zip(pairs, queries):
+                low = weights[pair]
+                dp = dot(key_pair(vall, pair), scaled_grads[query], LAST)
+                ds = (low.astype(F32) * (dp - deltas[query, :1])).astype(BF16)
+                results.append(
+                    (
+                        dot(low, scaled_grads[query], PLAIN),
+                        dot(ds, both(qq, first + query), PLAIN),
+                        dot(key_pair(kall, pair), ds, FIRST),
+                    )
+                )
+            for pair, query, (dv, dk, dq) in zip(pairs, queries, results):
+                for place in range(2):
+                    rows = slice(place * BLK, place * BLK + BLK)
+                    dv_acc[pair_key[2 * pair + place]] += dv[rows]
+                    dk_acc[pair_key[2 * pair + place]] += dk[rows]
+                dq_t[first + query] += dq
+
+        over_pairs(grad_pairs)
 
 
 def attention_call(ids, docs, *parts):
@@ -471,19 +489,23 @@
             jax.ShapeDtypeStruct((32, BLK, HD), F32),
             jax.ShapeDtypeStruct((32, BLK, HD), F32),
         ),
-        in_specs=[SMEM, SMEM] + [VMEM] * 9,
+        in_specs=[SMEM, SMEM] + [VMEM] * 8,
         out_specs=(VMEM,) * 6,
         scratch_shapes=[
             pltpu.SMEM((32,), jnp.int32),
             pltpu.SMEM((32,), jnp.int32),
+            pltpu.SMEM((16,), jnp.int32),
             pltpu.SMEM((32,), jnp.int32),
-            pltpu.SMEM((32,), jnp.int32),
-            pltpu.VMEM((30, BLK, 2 * BLK), F32),
-            pltpu.VMEM((4, 8, 2 * BLK), F32),
-            pltpu.VMEM((4, 8, 2 * BLK), F32),
-            pltpu.VMEM((4, 8, 2 * BLK), F32),
+            pltpu.SMEM((16,), jnp.int32),
+            pltpu.VMEM((16, 2 * BLK, 2 * BLK), F32),
+            pltpu.VMEM((16, 2 * BLK, 2 * BLK), BF16),
+            pltpu.VMEM((2, BLK, 2 * BLK), BF16),
+            pltpu.VMEM((2, 2 * BLK, HD), BF16),
+            pltpu.VMEM((2, 8, 2 * BLK), F32),
+            pltpu.VMEM((2, 8, 2 * BLK), F32),
+            pltpu.VMEM((2, 8, 2 * BLK), F32),
         ],
-        compiler_params=pltpu.CompilerParams(vmem_limit_bytes=28 * 2**20),
+        compiler_params=pltpu.CompilerParams(vmem_limit_bytes=34 * 2**20),
     )(ids, docs, *parts)
 
 

time: 101 us -> 104 us (1.030)
  Pallas kernels: 99.8 us -> 103 us
    pallas_call x1, Pallas kernels: 44 us -> 55.5 us  [scatter_call(): pl.pallas_call(scatter_kernel, name='scatter_grads', out_shape=(jax.Shape...]
    pallas_call x1, Pallas kernels: 13.8 us -> 5.6 us  [attention_call(): pl.pallas_call(attention_kernel, name='attention', out_shape=(jax.ShapeDt...]
where the time goes in v4:
time: 104 us
  Pallas kernels  103 us (99%)
    pallas_call x1, Pallas kernels, scatter_call(): pl.pallas_call(scatter_kernel, name='scatter_grads', out_shape=(jax.Shape...  55.5 us
    pallas_call x1, Pallas kernels, gather_call(): pl.pallas_call(gather_kernel, name='gather_keys', out_shape=(jax.ShapeDty...  40 us
    pallas_call x1, Pallas kernels, attention_call(): pl.pallas_call(attention_kernel, name='attention', out_shape=(jax.ShapeDt...  5.6 us

profile of v4, /device:TPU:1, one launch (start us, length us, event | category | flops | bytes accessed | tf_op | source)
XLA Modules:
  0.0 103.9 jit_solution(18408148600493848526)
XLA Ops:
  0.6 40.0 %gather_keys.1 = (bf16[16,528,128]{2,1,0:T(8,128)(2,1)S(1)}, bf16[16,512,128]{2,1,0:T(8,128)(2,1)S(1)}, bf16[4,2,256,128]{3,2,1,0:T(8,128)(2,1)S(1)}, bf16[4,2,2...) custom-call(bf16[512,256]{1,0:T(8,128)(2,1)} %cq_h.3, ...), custom_call_target="tpu_custom_call" | custom-call | tf_op jit(solution)/shard_map/gather_keys/pallas_call | solution.py:275
  40.6 5.6 %attention.1 = (f32[4,128,512]{2,1,0:T(8,128)S(1)}, f32[4,128,512]{2,1,0:T(8,128)S(1)}, f32[4,256,128]{2,1,0:T(8,128)S(1)}, f32[4,256,128]{2,1,0:T(8,128)S(1)}, ...) custom-call(s32[16,128]{1,0:T(8,128)S(1)} %get-tuple-element.28.ids, s32[32]{0:T(128)} %docs.1, ...), custom_call_target="tpu_custom_call" | custom-call | tf_op jit(solution)/shard_map/attention/pallas_call | solution.py:481
  46.2 0.0 copy-start
  46.2 0.0 copy-start.1
  46.2 55.5 %scatter_grads.1 = (f32[6,512,256]{2,1,0:T(8,128)S(1)}, f32[2,512,256]{2,1,0:T(8,128)S(1)}, f32[8,512]{1,0:T(8,128)S(1)}) custom-call(bf16[512,256]{1,0:T(8,128)(2,1)} %cq_h.3, bf16[512,256]{1,0:T(8,128)(2,1)} %ck.1, bf16[512,256]{1,0:T(8,128)(2,1)} %nq_h.3, bf16[512,256]{1,0:T(8,128)(2,1)} %nk_h.3, f32[1,256]{1,0:T(1,128)} %bitcast.12, f32[1,256]{1,0:T(1,128)} %bitcast.6, ...), custom_call_target="tpu_custom_call" | custom-call | tf_op jit(solution)/shard_map/scatter_grads/pallas_call | solution.py:732
  101.8 0.0 copy-done
  101.8 0.0 copy-done.1
  101.8 2.1 %finish.1 = (f32[512,256]{1,0:T(8,128)}, f32[512,256]{1,0:T(8,128)}, f32[512,256]{1,0:T(8,128)}, f32[512,256]{1,0:T(8,128)}, f32[512,256]{1,0:T(8,128)}, /*index...) custom-call(bf16[512,256]{1,0:T(8,128)(2,1)S(1)} %copy-done, f32[1,256]{1,0:T(1,128)S(1)} %bitcast.7, ...), custom_call_target="tpu_custom_call" | custom-call | tf_op jit(solution)/shard_map/finish/pallas_call | solution.py:797
Async XLA Ops:
  46.2 55.6 %copy-start = (bf16[512,256]{1,0:T(8,128)(2,1)S(1)}, bf16[512,256]{1,0:T(8,128)(2,1)}, u32[]{:S(2)}) copy-start(bf16[512,256]{1,0:T(8,128)(2,1)} %ck.1) | copy-start | bytes 786436
  46.2 55.6 %copy-start.1 = (f32[256]{0:T(256)S(1)}, f32[256]{0:T(256)}, u32[]{:S(2)}) copy-start(f32[256]{0:T(256)} %param.19) | copy-start | bytes 3076

commit v5 on v4

--- a/solution.py
+++ b/solution.py
@@ -211,16 +211,17 @@
     def spread(view, px, py):
         return remote.start(view, view, ctx_of(px, py, core))
 
-    v_half, v_y = [], []
-    for number, near, far, half in ((1, left, right, 0), (2, right, left, 1)):
+    v_half, v_y, k_half = [], [], []
+    sides = ((1, left, right, 0), (2, right, left, 1))
+    for number, near, far, half in sides:
         arrived(0, number, vall, half)
         v_half.append(spread(part(vall, near, y, half), far, y))
-        arrived(0, number, vall, 1 - half)
-        v_y.append(spread(slot(vall, near, y), x, 1 - y))
     arrived(3, 0, kall, 0)
     arrived(3, 0, kall, 1)
     k_right = spread(slot(kall, x, 1 - y), right, y)
     k_left = spread(slot(kall, x, 1 - y), left, y)
+    arrived(0, 1, vall, 1)
+    v_y.append(spread(slot(vall, left, y), x, 1 - y))
 
     v_own.wait()
     k_own.wait()
@@ -234,35 +235,36 @@
     def own_block(index):
         side, rows = index // 2, slice(index % 2 * BLK, index % 2 * BLK + BLK)
         packet = 2 * chip_of(x, y) + side
-        grad_clean, grad_noisy = gg[index, 0], gg[index, 1]
         own_s[index, :, :BLK] = dot(kall[packet, rows, :], qq[index, 0], LAST)
         own_s[index, :, BLK:] = dot(kn[index], qq[index, 1], LAST)
-        grads_t[index, :, :BLK] = jnp.transpose(grad_clean.astype(F32))
-        grads_t[index, :, BLK:] = jnp.transpose(grad_noisy.astype(F32))
+        for kind in range(2):
+            columns = slice(kind * BLK, kind * BLK + BLK)
+            grads_t[index, :, columns] = jnp.transpose(gg[index, kind].astype(F32))
 
     own_block(0)
-    own_block(1)
-    k_half = []
-    for number, near, far, half in ((1, left, right, 0), (2, right, left, 1)):
+    for number, near, far, half in sides:
         arrived(3, number, kall, half)
         k_half.append(spread(part(kall, near, y, half), far, y))
         arrived(3, number, kall, 1 - half)
+    own_block(1)
+    arrived(0, 2, vall, 0)
+    v_y.append(spread(slot(vall, right, y), x, 1 - y))
     own_block(2)
-    own_block(3)
+    v_half[0].wait_recv()
+    v_half[1].wait_recv()
+    v_y[0].wait_recv()
+    v_far = [spread(rows_of(left, 1 - y, 0, 0, SHIFT), right, y)]
     for half in range(2):
-        v_half[half].wait_recv()
         v_y.append(spread(rows_of(opposite, y, half, SHIFT, 512 - SHIFT), x, 1 - y))
-    arrived(0, 0, vall, 0)
-    arrived(0, 0, vall, 1)
-    v_far = []
-    for half, near, far in ((0, left, right), (1, right, left)):
-        v_y[half].wait_recv()
-        v_far.append(spread(rows_of(near, 1 - y, half, 0, SHIFT), far, y))
     k_right.wait_recv()
     k_half.append(spread(part(kall, left, 1 - y, 0), right, y))
     k_left.wait_recv()
     k_half.append(spread(part(kall, right, 1 - y, 1), left, y))
-
+    own_block(3)
+    v_y[1].wait_recv()
+    v_far.append(spread(rows_of(right, 1 - y, 1, 0, SHIFT), left, y))
+    arrived(0, 0, vall, 0)
+    arrived(0, 0, vall, 1)
     for copy in v_y[2:] + v_far + k_half:
         copy.wait_recv()
     names = jnp.max(kall[:, 512:, :].astype(F32), axis=1)
@@ -542,10 +544,17 @@
             value = value + other[...].astype(F32)
         k_out[row, step, half] = value.astype(BF16)
 
-    pack_v(2)
     pack_k(1, 2, 0)
     pack_k(1, 2, 1)
     enter(ctx, head, [partner, to_right, to_left, to_y])
+    k_half = {}
+
+    def start_half(row):
+        k_half[row, 0] = remote.start(k_out.at[row, 2, 0], kh.at[row, 0], to_left)
+        k_half[row, 1] = remote.start(k_out.at[row, 2, 1], kh.at[row, 1], to_right)
+
+    start_half(1)
+    pack_v(2)
     first, rest = pl.ds(0, SHIFT), pl.ds(SHIFT, 512 - SHIFT)
     v_far = [
         remote.start(v_out.at[2, 0, first], vq.at[0], to_left),
@@ -554,16 +563,6 @@
     v_opposite = [
         remote.start(v_out.at[2, half, rest], vy.at[2, half, rest], to_y) for half in range(2)
     ]
-    k_half = {}
-
-    def start_half(row):
-        k_half[row, 0] = remote.start(k_out.at[row, 2, 0], kh.at[row, 0], to_left)
-        k_half[row, 1] = remote.start(k_out.at[row, 2, 1], kh.at[row, 1], to_right)
-
-    start_half(1)
-    pack_k(0, 2, 0)
-    pack_k(0, 2, 1)
-    start_half(0)
     v_y = {}
 
     def send_v(step, half):
@@ -575,10 +574,11 @@
             ).astype(BF16)
         v_y[step] = remote.start(v_out.at[step], vy.at[step], to_y)
 
-    send_v(3, 0)
     for row in (1, 0):
         pack_k(row, 3, 1)
         pack_k(row, 1, 0)
+    pack_k(0, 2, 0)
+    pack_k(0, 2, 1)
 
     def landing(i):
         return back.at[i, :, own_columns]
@@ -608,9 +608,6 @@
             stage[i, rows, :] = ref[2 * (1 - core) + part]
         swap[i] = remote.start(stage.at[i], landing(i), partner)
 
-    turn(0, dq_t, 2, score_scale)
-    turn_noisy(dk_noisy, 4)
-
     k_x = {}
 
     def k_forward(row):
@@ -621,7 +618,26 @@
         pack_k(row, 1, 1, kh.at[row, 1])
         k_x[row, 1] = remote.start(k_out.at[row, 1], kx.at[row, 1], to_right)
 
+    turn_noisy(dk_noisy, 4)
+    send_v(3, 0)
     k_forward(1)
+    start_half(0)
+
+    def pack_x(step, half, *others):
+        value = mine(dv, step, 0, half)
+        for other in others:
+            value = value + other[...].astype(F32)
+        x_out[step, half] = value.astype(BF16)
+
+    v_half = []
+    for half, target in ((0, to_left), (1, to_right)):
+        v_opposite[half].wait_recv()
+        pack_x(2, half)
+        x_out[2, half, SHIFT:] = (
+            mine(dv, 2, 0, half)[SHIFT:] + vy[2, half, SHIFT:].astype(F32)
+        ).astype(BF16)
+        v_half.append(remote.start(x_out.at[2, half], vh.at[half], target))
+    turn(0, dq_t, 2, score_scale)
 
     row = lax.broadcasted_iota(jnp.int32, (8, 512), 0)
 
@@ -630,6 +646,13 @@
 
     for copy in loads:
         copy.wait()
+    k_x[1, 0].wait_recv()
+    k_x[1, 1].wait_recv()
+    for half in range(2):
+        pack_k(1, 0, half, kx.at[1, 0, half], kx.at[1, 1, half])
+    k_y = remote.start(k_out.at[1, 0], ky, to_y)
+    k_forward(0)
+    send_v(1, 1)
     for i in (2, 3, 4):
         swap[i].wait_recv()
     total = jnp.zeros((8, 512), F32)
@@ -640,42 +663,14 @@
     exchange = [
         remote.start(sums.at[0], sums.at[step], ctx, (head + step) % 8) for step in range(1, 8)
     ]
-
-    def pack_x(step, half, *others):
-        value = mine(dv, step, 0, half)
-        for other in others:
-            value = value + other[...].astype(F32)
-        x_out[step, half] = value.astype(BF16)
-
-    v_half = []
-    for half, target in ((0, to_left), (1, to_right)):
-        v_opposite[half].wait_recv()
-        pack_x(2, half)
-        x_out[2, half, SHIFT:] = (
-            mine(dv, 2, 0, half)[SHIFT:] + vy[2, half, SHIFT:].astype(F32)
-        ).astype(BF16)
-        v_half.append(remote.start(x_out.at[2, half], vh.at[half], target))
-    send_v(1, 1)
-    k_forward(0)
-    turn(0, out_t, 0, 1.0)
-    turn_noisy(dv_noisy, 5)
-    k_x[1, 0].wait_recv()
-    k_x[1, 1].wait_recv()
-    for half in range(2):
-        pack_k(1, 0, half, kx.at[1, 0, half], kx.at[1, 1, half])
-    k_y = remote.start(k_out.at[1, 0], ky, to_y)
-    send_v(0, None)
-
     v_y[3].wait_recv()
     v_half[0].wait_recv()
     pack_x(3, 0, vy.at[3, 0], vh.at[0])
     pack_x(3, 1, vy.at[3, 1])
     v_x = [remote.start(x_out.at[3], vx.at[0], to_left)]
-    v_y[1].wait_recv()
-    v_half[1].wait_recv()
-    pack_x(1, 0, vy.at[1, 0])
-    pack_x(1, 1, vy.at[1, 1], vh.at[1])
-    v_x.append(remote.start(x_out.at[1], vx.at[1], to_right))
+    turn(0, out_t, 0, 1.0)
+    turn_noisy(dv_noisy, 5)
+    send_v(0, None)
 
     for copy in exchange:
         copy.wait_recv()
@@ -701,9 +696,14 @@
         away[index] = jnp.where(first_core, values[1], values[0])
         return remote.start(away.at[index], fin.at[index, :, own_columns], partner)
 
+    k_y.wait_recv()
+    v_y[1].wait_recv()
+    v_half[1].wait_recv()
+    pack_x(1, 0, vy.at[1, 0])
+    pack_x(1, 1, vy.at[1, 1], vh.at[1])
+    v_x.append(remote.start(x_out.at[1], vx.at[1], to_right))
     k_x[0, 0].wait_recv()
     k_x[0, 1].wait_recv()
-    k_y.wait_recv()
     k_fin = finish(0, dk, score_scale, (kx.at[0, 0], kx.at[0, 1], ky))
     k_fin.wait_recv()
     sums[8] = inner(ck, kg, fin[0])

time: 104 us -> 106 us (1.019)
  Pallas kernels: 103 us -> 105 us
    pallas_call x1, Pallas kernels: 55.5 us -> 45.5 us  [scatter_call(): pl.pallas_call(scatter_kernel, name='scatter_grads', out_shape=(jax.Shape...]
    pallas_call x1, Pallas kernels: 5.6 us -> 15.6 us  [attention_call(): pl.pallas_call(attention_kernel, name='attention', out_shape=(jax.ShapeDt...]
    pallas_call x1, Pallas kernels: 40 us -> 42.1 us  [gather_call(): pl.pallas_call(gather_kernel, name='gather_keys', out_shape=(jax.ShapeDty...]
where the time goes in v5:
time: 106 us
  Pallas kernels  105 us (99%)
    pallas_call x1, Pallas kernels, scatter_call(): pl.pallas_call(scatter_kernel, name='scatter_grads', out_shape=(jax.Shape...  45.5 us
    pallas_call x1, Pallas kernels, gather_call(): pl.pallas_call(gather_kernel, name='gather_keys', out_shape=(jax.ShapeDty...  42.1 us
    pallas_call x1, Pallas kernels, attention_call(): pl.pallas_call(attention_kernel, name='attention', out_shape=(jax.ShapeDt...  15.6 us

profile of v5, /device:TPU:1, one launch (start us, length us, event | category | flops | bytes accessed | tf_op | source)
XLA Modules:
  0.0 106.0 jit_solution(6216896687604075534)
XLA Ops:
  0.6 42.1 %gather_keys.1 = (bf16[16,528,128]{2,1,0:T(8,128)(2,1)S(1)}, bf16[16,512,128]{2,1,0:T(8,128)(2,1)S(1)}, bf16[4,2,256,128]{3,2,1,0:T(8,128)(2,1)S(1)}, bf16[4,2,2...) custom-call(bf16[512,256]{1,0:T(8,128)(2,1)} %cq_h.3, ...), custom_call_target="tpu_custom_call" | custom-call | tf_op jit(solution)/shard_map/gather_keys/pallas_call | solution.py:277
  42.7 15.6 %attention.1 = (f32[4,128,512]{2,1,0:T(8,128)S(1)}, f32[4,128,512]{2,1,0:T(8,128)S(1)}, f32[4,256,128]{2,1,0:T(8,128)S(1)}, f32[4,256,128]{2,1,0:T(8,128)S(1)}, ...) custom-call(s32[16,128]{1,0:T(8,128)S(1)} %get-tuple-element.28.ids, s32[32]{0:T(128)} %docs.1, ...), custom_call_target="tpu_custom_call" | custom-call | tf_op jit(solution)/shard_map/attention/pallas_call | solution.py:483
  58.4 0.0 copy-start
  58.4 0.0 copy-start.1
  58.4 45.5 %scatter_grads.1 = (f32[6,512,256]{2,1,0:T(8,128)S(1)}, f32[2,512,256]{2,1,0:T(8,128)S(1)}, f32[8,512]{1,0:T(8,128)S(1)}) custom-call(bf16[512,256]{1,0:T(8,128)(2,1)} %cq_h.3, bf16[512,256]{1,0:T(8,128)(2,1)} %ck.1, bf16[512,256]{1,0:T(8,128)(2,1)} %nq_h.3, bf16[512,256]{1,0:T(8,128)(2,1)} %nk_h.3, f32[1,256]{1,0:T(1,128)} %bitcast.12, f32[1,256]{1,0:T(1,128)} %bitcast.6, ...), custom_call_target="tpu_custom_call" | custom-call | tf_op jit(solution)/shard_map/scatter_grads/pallas_call | solution.py:732
  103.9 0.0 copy-done
  103.9 0.0 copy-done.1
  103.9 2.1 %finish.1 = (f32[512,256]{1,0:T(8,128)}, f32[512,256]{1,0:T(8,128)}, f32[512,256]{1,0:T(8,128)}, f32[512,256]{1,0:T(8,128)}, f32[512,256]{1,0:T(8,128)}, /*index...) custom-call(bf16[512,256]{1,0:T(8,128)(2,1)S(1)} %copy-done, f32[1,256]{1,0:T(1,128)S(1)} %bitcast.7, ...), custom_call_target="tpu_custom_call" | custom-call | tf_op jit(solution)/shard_map/finish/pallas_call | solution.py:797
Async XLA Ops:
  58.4 45.5 %copy-start = (bf16[512,256]{1,0:T(8,128)(2,1)S(1)}, bf16[512,256]{1,0:T(8,128)(2,1)}, u32[]{:S(2)}) copy-start(bf16[512,256]{1,0:T(8,128)(2,1)} %ck.1) | copy-start | bytes 786436
  58.4 45.5 %copy-start.1 = (f32[256]{0:T(256)S(1)}, f32[256]{0:T(256)}, u32[]{:S(2)}) copy-start(f32[256]{0:T(256)} %param.19) | copy-start | bytes 3076

commit v6 on v5

--- a/solution.py
+++ b/solution.py
@@ -313,9 +313,9 @@
 
 def attention_kernel(
     ids, docs, kall, vall, qq, gg, kn, vn, own_s, grads_t,
-    out_t, dq_t, dk_noisy, dv_noisy, dk_acc, dv_acc,
-    where_is, first_of, pair_query, pair_key, pair_bias,
-    scores, weights, own_weights, scaled_grads, peaks, sums, deltas,
+    out_t, dq_t, dk_noisy, dv_noisy, dk_acc, dv_acc, keys_out, ds_out,
+    where_is, first_of, pair_query, pair_key, pair_bias, pair_slot, present,
+    weights, zeros, sems, pair_peaks, own_weights, scaled_grads, peaks, sums, deltas,
 ):
     chip = lax.axis_index("ctx") // 2
     scale = 1.0 / math.sqrt(HD)
@@ -355,128 +355,149 @@
     def totals(values):
         return jnp.sum(values.reshape(-1, 8, values.shape[1]), axis=0)
 
-    @pl.loop(0, 2)
-    def _(side):
-        count = 0
-        for half in range(2):
-            block = ids[chip * 2 + side, half]
-            begin = first_of[block]
-
-            def enlist(pair, count, half=half, block=block, begin=begin):
-                key = begin + 2 * pair
-                pair_query[count] = half
-                pair_key[2 * count] = where_is[key]
-                pair_key[2 * count + 1] = where_is[jnp.minimum(key + 1, block - 1)]
-                pair_bias[count] = jnp.where(key + 1 < block, 0, 1)
-                return count + 1
-
-            count = lax.fori_loop(0, (block - begin + 1) // 2, enlist, count)
-
-        def over_pairs(body):
-            groups = count // GROUP
-
-            @pl.loop(0, groups)
-            def _(group):
-                body([group * GROUP + i for i in range(GROUP)])
-
-            @pl.loop(groups * GROUP, count)
-            def _(pair):
-                body([pair])
-
-        first = 2 * side
-        for half in range(2):
-            peaks[half] = tops(own_s[first + half])
-
-        def score_pairs(pairs):
-            queries = [pair_query[pair] for pair in pairs]
-            values = [
-                dot(key_pair(kall, pair), both(qq, first + query), LAST)
-                for pair, query in zip(pairs, queries)
-            ]
-            for pair, query, value in zip(pairs, queries, values):
-                scores[pair] = value
-                peaks[query] = jnp.maximum(peaks[query], tops(value))
-
-        over_pairs(score_pairs)
-
-        for half in range(2):
-            index = first + half
-            peak = jnp.max(peaks[half], axis=0, keepdims=True) * scale2
-            peaks[half] = jnp.broadcast_to(peak, (8, 2 * BLK))
-            own = jnp.exp2(own_s[index] * scale2 - peak)
-            sums[half] = totals(own)
-            own_low = own.astype(BF16)
-            own_weights[half] = own_low
-            out_t[index, :, :BLK] = dot(key_rows(vall, chip * 4 + index), own_low[:, :BLK], FIRST)
-            out_t[index, :, BLK:] = dot(vn[index], own_low[:, BLK:], FIRST)
-
-        def value_pairs(pairs):
-            queries = [pair_query[pair] for pair in pairs]
-            outs, parts = [], []
-            for pair, query in zip(pairs, queries):
-                peak = peaks[query, :1]
-                hidden = peak + jnp.where(pair_bias[pair] == 1, jnp.inf, 0.0)
-                upper = jnp.exp2(scores[pair, :BLK] * scale2 - peak)
-                lower = jnp.exp2(scores[pair, BLK:] * scale2 - hidden)
-                low = jnp.concatenate([upper.astype(BF16), lower.astype(BF16)], axis=0)
-                weights[pair] = low
-                outs.append(dot(key_pair(vall, pair), low, FIRST))
-                parts.append(totals(upper) + totals(lower))
-            for query, out, part in zip(queries, outs, parts):
-                sums[query] += part
-                out_t[first + query] += out
-
-        over_pairs(value_pairs)
-
-        for half in range(2):
-            index = first + half
-            stored_own = chip * 4 + index
-            inverse_sum = 1.0 / jnp.sum(sums[half], axis=0, keepdims=True)
-            out = out_t[index] * inverse_sum
-            out_t[index] = out
-            grad_rows = (grads_t[index] * inverse_sum).astype(BF16).astype(F32)
-            delta = jnp.sum(out * grad_rows, axis=0, keepdims=True)
-            deltas[half] = jnp.broadcast_to(delta, (8, 2 * BLK))
-            grads = jnp.transpose(grad_rows).astype(BF16)
-            scaled_grads[half] = grads
-            own_low = own_weights[half]
-            own_dp = jnp.concatenate(
-                [
-                    dot(key_rows(vall, stored_own), grads[:BLK], LAST),
-                    dot(vn[index], grads[BLK:], LAST),
-                ],
-                axis=1,
+    @pl.loop(0, 32)
+    def _(slot):
+        present[slot] = 0
+
+    zeros[...] = jnp.zeros((2 * BLK, 2 * BLK), BF16)
+    count = 0
+    for index in range(4):
+        block = ids[chip * 2 + index // 2, index % 2]
+        begin = first_of[block]
+
+        def enlist(pair, count, index=index, block=block, begin=begin):
+            key = begin + 2 * pair
+            first = where_is[key]
+            second = where_is[jnp.minimum(key + 1, block - 1)]
+            slot = index * 8 + pair
+            pair_query[count] = index
+            pair_key[2 * count] = first
+            pair_key[2 * count + 1] = second
+            pair_bias[count] = jnp.where(key + 1 < block, 0, 1)
+            pair_slot[count] = slot
+            present[slot] = 1
+            return count + 1
+
+        count = lax.fori_loop(0, (block - begin + 1) // 2, enlist, count)
+
+    @pl.loop(0, 32)
+    def _(slot):
+        @pl.when(present[slot] == 0)
+        def _():
+            pltpu.make_async_copy(zeros, ds_out.at[slot], sems.at[slot]).start()
+            keys_out[slot] = jnp.zeros((2 * BLK, HD), BF16)
+
+    def over_pairs(body):
+        groups = count // GROUP
+
+        @pl.loop(0, groups)
+        def _(group):
+            body([group * GROUP + i for i in range(GROUP)])
+
+        @pl.loop(groups * GROUP, count)
+        def _(pair):
+            body([pair])
+
+    def spread_rows(row):
+        return jnp.broadcast_to(row, (8, 2 * BLK))
+
+    for index in range(4):
+        own = own_s[index]
+        peak = jnp.max(own, axis=0, keepdims=True) * scale2
+        peaks[index] = spread_rows(peak)
+        own = jnp.exp2(own * scale2 - peak)
+        sums[index] = totals(own)
+        own_low = own.astype(BF16)
+        own_weights[index] = own_low
+        out_t[index, :, :BLK] = dot(key_rows(vall, chip * 4 + index), own_low[:, :BLK], FIRST)
+        out_t[index, :, BLK:] = dot(vn[index], own_low[:, BLK:], FIRST)
+        pair_peaks[32 + index] = peaks[index]
+
+    def forward_pairs(pairs):
+        queries = [pair_query[pair] for pair in pairs]
+        scores = [
+            dot(key_pair(kall, pair), both(qq, query), LAST) for pair, query in zip(pairs, queries)
+        ]
+        tops_of = [jnp.max(tops(score), axis=0, keepdims=True) * scale2 for score in scores]
+        results = []
+        for pair, query, score, top in zip(pairs, queries, scores, tops_of):
+            before = peaks[query]
+            now = jnp.maximum(before, spread_rows(top))
+            peaks[query] = now
+            pair_peaks[pair] = now
+            peak = now[:1]
+            hidden = peak + jnp.where(pair_bias[pair] == 1, jnp.inf, 0.0)
+            upper = jnp.exp2(score[:BLK] * scale2 - peak)
+            lower = jnp.exp2(score[BLK:] * scale2 - hidden)
+            low = jnp.concatenate([upper.astype(BF16), lower.astype(BF16)], axis=0)
+            weights[pair] = low
+            results.append(
+                (
+                    jnp.exp2(before - now),
+                    dot(key_pair(vall, pair), low, FIRST),
+                    totals(upper) + totals(lower),
+                )
             )
-            own_ds = (own_low.astype(F32) * (own_dp - delta)).astype(BF16)
-            dv_acc[stored_own] += dot(own_low[:, :BLK], grads[:BLK], PLAIN)
-            dk_acc[stored_own] += dot(own_ds[:, :BLK], qq[index, 0], PLAIN)
-            dv_noisy[index] = dot(own_low[:, BLK:], grads[BLK:], PLAIN)
-            dk_noisy[index] = dot(own_ds[:, BLK:], qq[index, 1], PLAIN) * scale
-            dq_t[index, :, :BLK] = dot(key_rows(kall, stored_own), own_ds[:, :BLK], FIRST)
-            dq_t[index, :, BLK:] = dot(kn[index], own_ds[:, BLK:], FIRST)
-
-        def grad_pairs(pairs):
-            queries = [pair_query[pair] for pair in pairs]
-            results = []
-            for pair, query in zip(pairs, queries):
-                low = weights[pair]
-                dp = dot(key_pair(vall, pair), scaled_grads[query], LAST)
-                ds = (low.astype(F32) * (dp - deltas[query, :1])).astype(BF16)
-                results.append(
-                    (
-                        dot(low, scaled_grads[query], PLAIN),
-                        dot(ds, both(qq, first + query), PLAIN),
-                        dot(key_pair(kall, pair), ds, FIRST),
-                    )
-                )
-            for pair, query, (dv, dk, dq) in zip(pairs, queries, results):
-                for place in range(2):
-                    rows = slice(place * BLK, place * BLK + BLK)
-                    dv_acc[pair_key[2 * pair + place]] += dv[rows]
-                    dk_acc[pair_key[2 * pair + place]] += dk[rows]
-                dq_t[first + query] += dq
-
-        over_pairs(grad_pairs)
+        for query, (decay, out, part) in zip(queries, results):
+            sums[query] = sums[query] * decay + part
+            out_t[query] = out_t[query] * decay[:1] + out
+
+    over_pairs(forward_pairs)
+
+    for index in range(4):
+        stored_own = chip * 4 + index
+        own_decay = jnp.exp2(pair_peaks[32 + index] - peaks[index])[:1]
+        inverse_sum = 1.0 / jnp.sum(sums[index], axis=0, keepdims=True)
+        out = out_t[index] * inverse_sum
+        out_t[index] = out
+        grad_rows = (grads_t[index] * inverse_sum).astype(BF16).astype(F32)
+        delta = jnp.sum(out * grad_rows, axis=0, keepdims=True)
+        deltas[index] = spread_rows(delta)
+        grads = jnp.transpose(grad_rows).astype(BF16)
+        scaled_grads[index] = grads
+        own = own_weights[index].astype(F32) * own_decay
+        own_low = own.astype(BF16)
+        own_dp = jnp.concatenate(
+            [
+                dot(key_rows(vall, stored_own), grads[:BLK], LAST),
+                dot(vn[index], grads[BLK:], LAST),
+            ],
+            axis=1,
+        )
+        own_ds = (own * (own_dp - delta)).astype(BF16)
+        dv_acc[stored_own] += dot(own_low[:, :BLK], grads[:BLK], PLAIN)
+        dk_acc[stored_own] += dot(own_ds[:, :BLK], qq[index, 0], PLAIN)
+        dv_noisy[index] = dot(own_low[:, BLK:], grads[BLK:], PLAIN)
+        dk_noisy[index] = dot(own_ds[:, BLK:], qq[index, 1], PLAIN) * scale
+        dq_t[index, :, :BLK] = dot(key_rows(kall, stored_own), own_ds[:, :BLK], FIRST)
+        dq_t[index, :, BLK:] = dot(kn[index], own_ds[:, BLK:], FIRST)
+
+    def grad_pairs(pairs):
+        queries = [pair_query[pair] for pair in pairs]
+        results = []
+        for pair, query in zip(pairs, queries):
+            decay = jnp.exp2(pair_peaks[pair] - peaks[query])[:1]
+            prob = weights[pair].astype(F32) * decay
+            dp = dot(key_pair(vall, pair), scaled_grads[query], LAST)
+            ds = (prob * (dp - deltas[query, :1])).astype(BF16)
+            results.append(
+                (ds, dot(prob.astype(BF16), scaled_grads[query], PLAIN), dot(ds, both(qq, query), PLAIN))
+            )
+        for pair, (ds, dv, dk) in zip(pairs, results):
+            weights[pair] = ds
+            slot = pair_slot[pair]
+            keys_out[slot] = key_pair(kall, pair)
+            pltpu.make_async_copy(weights.at[pair], ds_out.at[slot], sems.at[slot]).start()
+            for place in range(2):
+                rows = slice(place * BLK, place * BLK + BLK)
+                dv_acc[pair_key[2 * pair + place]] += dv[rows]
+                dk_acc[pair_key[2 * pair + place]] += dk[rows]
+
+    over_pairs(grad_pairs)
+
+    @pl.loop(0, 32)
+    def _(slot):
+        pltpu.make_async_copy(zeros, ds_out.at[slot], sems.at[slot]).wait()
 
 
 def attention_call(ids, docs, *parts):
@@ -490,31 +511,38 @@
             jax.ShapeDtypeStruct((4, BLK, HD), F32),
             jax.ShapeDtypeStruct((32, BLK, HD), F32),
             jax.ShapeDtypeStruct((32, BLK, HD), F32),
+            jax.ShapeDtypeStruct((32, 2 * BLK, HD), BF16),
+            jax.ShapeDtypeStruct((32, 2 * BLK, 2 * BLK), BF16),
         ),
         in_specs=[SMEM, SMEM] + [VMEM] * 8,
-        out_specs=(VMEM,) * 6,
+        out_specs=(VMEM,) * 7 + (HBM,),
         scratch_shapes=[
             pltpu.SMEM((32,), jnp.int32),
             pltpu.SMEM((32,), jnp.int32),
-            pltpu.SMEM((16,), jnp.int32),
             pltpu.SMEM((32,), jnp.int32),
-            pltpu.SMEM((16,), jnp.int32),
-            pltpu.VMEM((16, 2 * BLK, 2 * BLK), F32),
-            pltpu.VMEM((16, 2 * BLK, 2 * BLK), BF16),
-            pltpu.VMEM((2, BLK, 2 * BLK), BF16),
-            pltpu.VMEM((2, 2 * BLK, HD), BF16),
-            pltpu.VMEM((2, 8, 2 * BLK), F32),
-            pltpu.VMEM((2, 8, 2 * BLK), F32),
-            pltpu.VMEM((2, 8, 2 * BLK), F32),
+            pltpu.SMEM((64,), jnp.int32),
+            pltpu.SMEM((32,), jnp.int32),
+            pltpu.SMEM((32,), jnp.int32),
+            pltpu.SMEM((32,), jnp.int32),
+            pltpu.VMEM((32, 2 * BLK, 2 * BLK), BF16),
+            pltpu.VMEM((2 * BLK, 2 * BLK), BF16),
+            pltpu.SemaphoreType.DMA((32,)),
+            pltpu.VMEM((36, 8, 2 * BLK), F32),
+            pltpu.VMEM((4, BLK, 2 * BLK), BF16),
+            pltpu.VMEM((4, 2 * BLK, HD), BF16),
+            pltpu.VMEM((4, 8, 2 * BLK), F32),
+            pltpu.VMEM((4, 8, 2 * BLK), F32),
+            pltpu.VMEM((4, 8, 2 * BLK), F32),
         ],
-        compiler_params=pltpu.CompilerParams(vmem_limit_bytes=34 * 2**20),
+        compiler_params=pltpu.CompilerParams(vmem_limit_bytes=30 * 2**20),
     )(ids, docs, *parts)
 
 
 def scatter_kernel(
     cq_h, ck_h, nq_h, nk_h, qg_h, kg_h, inv, out_t, dq_t, dk_noisy, dv_noisy, dk, dv,
+    pair_keys, ds_h,
     back, fin, inner_out,
-    raws, qg, kg, stage, k_out, v_out, x_out, vy, vq, vh, vx, kh, kx, ky, away, sums,
+    raws, qg, kg, stage, k_out, v_out, x_out, vy, vq, vh, vx, kh, kx, ky, away, sums, dq_acc, ds,
     send, recv, lsem,
 ):
     ctx, head, core, y, x = place()
@@ -528,6 +556,7 @@
     loads = [local.start(ref, raws.at[i]) for i, ref in enumerate((cq_h, ck_h, nq_h, nk_h))]
     loads += [local.start(qg_h, qg), local.start(kg_h, kg)]
     cq, ck, nq, nk = [raws.at[i] for i in range(4)]
+    ds_loads = [local.start(ds_h.at[pl.ds(8 * i, 8)], ds.at[i]) for i in range(2)]
     remote = Copies(send, recv, head)
 
     def mine(ref, step, row, half):
@@ -544,17 +573,10 @@
             value = value + other[...].astype(F32)
         k_out[row, step, half] = value.astype(BF16)
 
+    pack_v(2)
     pack_k(1, 2, 0)
     pack_k(1, 2, 1)
     enter(ctx, head, [partner, to_right, to_left, to_y])
-    k_half = {}
-
-    def start_half(row):
-        k_half[row, 0] = remote.start(k_out.at[row, 2, 0], kh.at[row, 0], to_left)
-        k_half[row, 1] = remote.start(k_out.at[row, 2, 1], kh.at[row, 1], to_right)
-
-    start_half(1)
-    pack_v(2)
     first, rest = pl.ds(0, SHIFT), pl.ds(SHIFT, 512 - SHIFT)
     v_far = [
         remote.start(v_out.at[2, 0, first], vq.at[0], to_left),
@@ -563,6 +585,16 @@
     v_opposite = [
         remote.start(v_out.at[2, half, rest], vy.at[2, half, rest], to_y) for half in range(2)
     ]
+    k_half = {}
+
+    def start_half(row):
+        k_half[row, 0] = remote.start(k_out.at[row, 2, 0], kh.at[row, 0], to_left)
+        k_half[row, 1] = remote.start(k_out.at[row, 2, 1], kh.at[row, 1], to_right)
+
+    start_half(1)
+    pack_k(0, 2, 0)
+    pack_k(0, 2, 1)
+    start_half(0)
     v_y = {}
 
     def send_v(step, half):
@@ -574,21 +606,16 @@
             ).astype(BF16)
         v_y[step] = remote.start(v_out.at[step], vy.at[step], to_y)
 
+    send_v(3, 0)
     for row in (1, 0):
         pack_k(row, 3, 1)
         pack_k(row, 1, 0)
-    pack_k(0, 2, 0)
-    pack_k(0, 2, 1)
 
     def landing(i):
         return back.at[i, :, own_columns]
 
     swap = {}
-    dk_pair, dv_pair = [
-        [ref.at[pl.ds(c * 2, 2)] for c in (core, 1 - core)] for ref in (dk_noisy, dv_noisy)
-    ]
-
-    def turn(index, ref, first, factor):
+    def turn(ref, first, factor):
         for part in range(2):
             rows = slice(part * BLK, part * BLK + BLK)
             for c, own in ((core, True), (1 - core, False)):
@@ -608,6 +635,8 @@
             stage[i, rows, :] = ref[2 * (1 - core) + part]
         swap[i] = remote.start(stage.at[i], landing(i), partner)
 
+    turn_noisy(dk_noisy, 4)
+
     k_x = {}
 
     def k_forward(row):
@@ -618,10 +647,7 @@
         pack_k(row, 1, 1, kh.at[row, 1])
         k_x[row, 1] = remote.start(k_out.at[row, 1], kx.at[row, 1], to_right)
 
-    turn_noisy(dk_noisy, 4)
-    send_v(3, 0)
     k_forward(1)
-    start_half(0)
 
     def pack_x(step, half, *others):
         value = mine(dv, step, 0, half)
@@ -637,22 +663,56 @@
             mine(dv, 2, 0, half)[SHIFT:] + vy[2, half, SHIFT:].astype(F32)
         ).astype(BF16)
         v_half.append(remote.start(x_out.at[2, half], vh.at[half], target))
-    turn(0, dq_t, 2, score_scale)
-
-    row = lax.broadcasted_iota(jnp.int32, (8, 512), 0)
-
-    def inner(raw, gain, values):
-        return row_sums(raw[...].astype(F32) * (gain[...] * values))
-
-    for copy in loads:
-        copy.wait()
+    send_v(1, 1)
+    k_forward(0)
+    turn(out_t, 0, 1.0)
+    turn_noisy(dv_noisy, 5)
+
+    def add_queries(block):
+        dq_acc[block] = dq_t[block]
+        ds_loads[block].wait()
+
+        @pl.loop(0, 4)
+        def _(two):
+            keys = pair_keys[pl.ds(block * 8 + two * 2, 2)].reshape(4 * BLK, HD)
+            values = ds[block % 2, pl.ds(two * 2, 2)].reshape(4 * BLK, 2 * BLK)
+            dq_acc[block] += dot(keys, values, FIRST)
+
+        if block < 2:
+            later = block + 2
+            ds_loads.append(local.start(ds_h.at[pl.ds(8 * later, 8)], ds.at[block]))
+
+    add_queries(0)
+    pack_v(0)
     k_x[1, 0].wait_recv()
     k_x[1, 1].wait_recv()
     for half in range(2):
         pack_k(1, 0, half, kx.at[1, 0, half], kx.at[1, 1, half])
     k_y = remote.start(k_out.at[1, 0], ky, to_y)
-    k_forward(0)
-    send_v(1, 1)
+    send_v(0, None)
+    add_queries(1)
+
+    v_y[3].wait_recv()
+    v_half[0].wait_recv()
+    pack_x(3, 0, vy.at[3, 0], vh.at[0])
+    pack_x(3, 1, vy.at[3, 1])
+    v_x = [remote.start(x_out.at[3], vx.at[0], to_left)]
+    add_queries(2)
+    v_y[1].wait_recv()
+    v_half[1].wait_recv()
+    pack_x(1, 0, vy.at[1, 0])
+    pack_x(1, 1, vy.at[1, 1], vh.at[1])
+    v_x.append(remote.start(x_out.at[1], vx.at[1], to_right))
+    add_queries(3)
+    turn(dq_acc, 2, score_scale)
+
+    row = lax.broadcasted_iota(jnp.int32, (8, 512), 0)
+
+    def inner(raw, gain, values):
+        return row_sums(raw[...].astype(F32) * (gain[...] * values))
+
+    for copy in loads:
+        copy.wait()
     for i in (2, 3, 4):
         swap[i].wait_recv()
     total = jnp.zeros((8, 512), F32)
@@ -663,15 +723,28 @@
     exchange = [
         remote.start(sums.at[0], sums.at[step], ctx, (head + step) % 8) for step in range(1, 8)
     ]
-    v_y[3].wait_recv()
-    v_half[0].wait_recv()
-    pack_x(3, 0, vy.at[3, 0], vh.at[0])
-    pack_x(3, 1, vy.at[3, 1])
-    v_x = [remote.start(x_out.at[3], vx.at[0], to_left)]
-    turn(0, out_t, 0, 1.0)
-    turn_noisy(dv_noisy, 5)
-    send_v(0, None)
-
+
+    def finish(index, ref, factor, terms):
+        values = []
+        for half in range(2):
+            value = mine(ref, 0, 0, half) * factor
+            for term in terms:
+                value = value + term[half].astype(F32)
+            values.append(value)
+        first_core = core == 0
+        fin[index, :, own_columns] = jnp.where(first_core, values[0], values[1])
+        away[index] = jnp.where(first_core, values[1], values[0])
+        return remote.start(away.at[index], fin.at[index, :, own_columns], partner)
+
+    k_x[0, 0].wait_recv()
+    k_x[0, 1].wait_recv()
+    k_y.wait_recv()
+    k_fin = finish(0, dk, score_scale, (kx.at[0, 0], kx.at[0, 1], ky))
+    k_fin.wait_recv()
+    sums[8] = inner(ck, kg, fin[0])
+    k_exchange = [
+        remote.start(sums.at[8], sums.at[8 + step], ctx, (head + step) % 8) for step in range(1, 8)
+    ]
     for copy in exchange:
         copy.wait_recv()
     total = sums[0]
@@ -684,32 +757,6 @@
         factor = inverse * inverse * inverse * means[:, index : index + 1]
         back[i] = inverse * (gain[...] * back[i]) - raw[...].astype(F32) * factor
 
-    def finish(index, ref, factor, terms):
-        values = []
-        for half in range(2):
-            value = mine(ref, 0, 0, half) * factor
-            for term in terms:
-                value = value + term[half].astype(F32)
-            values.append(value)
-        first_core = core == 0
-        fin[index, :, own_columns] = jnp.where(first_core, values[0], values[1])
-        away[index] = jnp.where(first_core, values[1], values[0])
-        return remote.start(away.at[index], fin.at[index, :, own_columns], partner)
-
-    k_y.wait_recv()
-    v_y[1].wait_recv()
-    v_half[1].wait_recv()
-    pack_x(1, 0, vy.at[1, 0])
-    pack_x(1, 1, vy.at[1, 1], vh.at[1])
-    v_x.append(remote.start(x_out.at[1], vx.at[1], to_right))
-    k_x[0, 0].wait_recv()
-    k_x[0, 1].wait_recv()
-    k_fin = finish(0, dk, score_scale, (kx.at[0, 0], kx.at[0, 1], ky))
-    k_fin.wait_recv()
-    sums[8] = inner(ck, kg, fin[0])
-    k_exchange = [
-        remote.start(sums.at[8], sums.at[8 + step], ctx, (head + step) % 8) for step in range(1, 8)
-    ]
     v_y[0].wait_recv()
     v_x[0].wait_recv()
     v_x[1].wait_recv()
@@ -737,7 +784,7 @@
             jax.ShapeDtypeStruct((2, 512, 256), F32),
             jax.ShapeDtypeStruct((8, 512), F32),
         ),
-        in_specs=[HBM] * 6 + [VMEM] * 7,
+        in_specs=[HBM] * 6 + [VMEM] * 8 + [HBM],
         out_specs=(VMEM, VMEM, VMEM),
         scratch_shapes=[
             pltpu.VMEM((4, 512, 256), BF16),
@@ -756,12 +803,14 @@
             pltpu.VMEM((2, 512, HD), BF16),
             pltpu.VMEM((2, 512, HD), F32),
             pltpu.VMEM((16, 8, 512), F32),
+            pltpu.VMEM((4, HD, 2 * BLK), F32),
+            pltpu.VMEM((2, 8, 2 * BLK, 2 * BLK), BF16),
             pltpu.SemaphoreType.DMA((48,)),
             pltpu.SemaphoreType.DMA((48,)),
-            pltpu.SemaphoreType.DMA((8,)),
+            pltpu.SemaphoreType.DMA((12,)),
         ],
         compiler_params=pltpu.CompilerParams(
-            collective_id=1, has_side_effects=True, vmem_limit_bytes=20 * 2**20
+            collective_id=1, has_side_effects=True, vmem_limit_bytes=30 * 2**20
         ),
     )(*operands)
 
@@ -820,7 +869,9 @@
     ]
     *parts, inv, ids = gather_call(*pinned)
     grads = attention_call(ids, docs, *parts)
-    back, fin, inner = scatter_call(*pinned[:6], inv, *grads)
+    *grads, ds = grads
+    ds = pltpu.with_memory_space_constraint(ds, pltpu.HBM)
+    back, fin, inner = scatter_call(*pinned[:6], inv, *grads, ds)
     return finish_call(clean_k, kg, inv, inner, back, fin)
 
 

time: 106 us -> 103 us (0.972)
  Pallas kernels: 105 us -> 102 us
    pallas_call x1, Pallas kernels: 45.5 us -> 38.5 us  [scatter_call(): pl.pallas_call(scatter_kernel, name='scatter_grads', out_shape=(jax.Shape...]
    pallas_call x1, Pallas kernels: 15.6 us -> 18.8 us  [attention_call(): pl.pallas_call(attention_kernel, name='attention', out_shape=(jax.ShapeDt...]
where the time goes in v6:
time: 103 us; the launch traced here: 102 us
  Pallas kernels  102 us (99%)
    pallas_call x1, Pallas kernels, gather_call(): pl.pallas_call(gather_kernel, name='gather_keys', out_shape=(jax.ShapeDty...  42.1 us
    pallas_call x1, Pallas kernels, scatter_call(): pl.pallas_call(scatter_kernel, name='scatter_grads', out_shape=(jax.Shape...  38.5 us
    pallas_call x1, Pallas kernels, attention_call(): pl.pallas_call(attention_kernel, name='attention', out_shape=(jax.ShapeDt...  18.8 us
    pallas_call x1, Pallas kernels, finish_call(): pl.pallas_call(finish_kernel, name='finish', out_shape=tuple((jax.ShapeDt...  2.07 us

profile of v6, /device:TPU:1, one launch (start us, length us, event | category | flops | bytes accessed | tf_op | source)
XLA Modules:
  0.0 102.4 jit_solution(13500849631879217331)
XLA Ops:
  0.6 42.1 %gather_keys.1 = (bf16[16,528,128]{2,1,0:T(8,128)(2,1)S(1)}, bf16[16,512,128]{2,1,0:T(8,128)(2,1)S(1)}, bf16[4,2,256,128]{3,2,1,0:T(8,128)(2,1)S(1)}, bf16[4,2,2...) custom-call(bf16[512,256]{1,0:T(8,128)(2,1)} %cq_h.3, ...), custom_call_target="tpu_custom_call" | custom-call | tf_op jit(solution)/shard_map/gather_keys/pallas_call | solution.py:277
  42.7 18.8 %attention.1 = (f32[4,128,512]{2,1,0:T(8,128)S(1)}, f32[4,128,512]{2,1,0:T(8,128)S(1)}, f32[4,256,128]{2,1,0:T(8,128)S(1)}, f32[4,256,128]{2,1,0:T(8,128)S(1)}, ...) custom-call(s32[16,128]{1,0:T(8,128)S(1)} %get-tuple-element.30.ids,, ...), custom_call_target="tpu_custom_call" | custom-call | tf_op jit(solution)/shard_map/attention/pallas_call | solution.py:504
  61.6 0.0 copy-start
  61.6 0.0 copy-start.1
  61.6 38.5 %scatter_grads.1 = (f32[6,512,256]{2,1,0:T(8,128)S(1)}, f32[2,512,256]{2,1,0:T(8,128)S(1)}, f32[8,512]{1,0:T(8,128)S(1)}) custom-call(bf16[512,256]{1,0:T(8,128)(2,1)} %cq_h.3, bf16[512,256]{1,0:T(8,128)(2,1)} %ck.1, bf16[512,256]{1,0:T(8,128)(2,1)} %nq_h.3, bf16[512,256]{1,0:T(8,128)(2,1)} %nk_h.3, f32[1,256]{1,0:T(1,128)} %bitcast.12, f32[1,256]{1,0:T(1,128)} %bitcast.6, ...), custom_call_target="tpu_custom_call" | custom-call | tf_op jit(solution)/shard_map/scatter_grads/pallas_call | solution.py:779
  100.1 0.0 copy-done
  100.1 0.0 copy-done.1
  100.1 2.1 %finish.1 = (f32[512,256]{1,0:T(8,128)}, f32[512,256]{1,0:T(8,128)}, f32[512,256]{1,0:T(8,128)}, f32[512,256]{1,0:T(8,128)}, f32[512,256]{1,0:T(8,128)}, /*index...) custom-call(bf16[512,256]{1,0:T(8,128)(2,1)S(1)} %copy-done, f32[1,256]{1,0:T(1,128)S(1)} %bitcast.7, ...), custom_call_target="tpu_custom_call" | custom-call | tf_op jit(solution)/shard_map/finish/pallas_call | solution.py:846
Async XLA Ops:
  61.6 38.6 %copy-start = (bf16[512,256]{1,0:T(8,128)(2,1)S(1)}, bf16[512,256]{1,0:T(8,128)(2,1)}, u32[]{:S(2)}) copy-start(bf16[512,256]{1,0:T(8,128)(2,1)} %ck.1) | copy-start | bytes 786436
  61.6 38.6 %copy-start.1 = (f32[256]{0:T(256)S(1)}, f32[256]{0:T(256)}, u32[]{:S(2)}) copy-start(f32[256]{0:T(256)} %param.19) | copy-start | bytes 3076

commit v7 on v6

--- a/solution.py
+++ b/solution.py
@@ -313,9 +313,9 @@
 
 def attention_kernel(
     ids, docs, kall, vall, qq, gg, kn, vn, own_s, grads_t,
-    out_t, dq_t, dk_noisy, dv_noisy, dk_acc, dv_acc, keys_out, ds_out,
-    where_is, first_of, pair_query, pair_key, pair_bias, pair_slot, present,
-    weights, zeros, sems, pair_peaks, own_weights, scaled_grads, peaks, sums, deltas,
+    out_t, dq_t, dk_noisy, dv_noisy, dk_acc, dv_acc,
+    where_is, first_of, pair_query, pair_key, pair_bias,
+    weights, pair_peaks, own_weights, scaled_grads, peaks, sums, deltas,
 ):
     chip = lax.axis_index("ctx") // 2
     scale = 1.0 / math.sqrt(HD)
@@ -355,11 +355,6 @@
     def totals(values):
         return jnp.sum(values.reshape(-1, 8, values.shape[1]), axis=0)
 
-    @pl.loop(0, 32)
-    def _(slot):
-        present[slot] = 0
-
-    zeros[...] = jnp.zeros((2 * BLK, 2 * BLK), BF16)
     count = 0
     for index in range(4):
         block = ids[chip * 2 + index // 2, index % 2]
@@ -369,23 +364,13 @@
             key = begin + 2 * pair
             first = where_is[key]
             second = where_is[jnp.minimum(key + 1, block - 1)]
-            slot = index * 8 + pair
             pair_query[count] = index
             pair_key[2 * count] = first
             pair_key[2 * count + 1] = second
             pair_bias[count] = jnp.where(key + 1 < block, 0, 1)
-            pair_slot[count] = slot
-            present[slot] = 1
             return count + 1
 
         count = lax.fori_loop(0, (block - begin + 1) // 2, enlist, count)
-
-    @pl.loop(0, 32)
-    def _(slot):
-        @pl.when(present[slot] == 0)
-        def _():
-            pltpu.make_async_copy(zeros, ds_out.at[slot], sems.at[slot]).start()
-            keys_out[slot] = jnp.zeros((2 * BLK, HD), BF16)
 
     def over_pairs(body):
         groups = count // GROUP
@@ -481,23 +466,20 @@
             dp = dot(key_pair(vall, pair), scaled_grads[query], LAST)
             ds = (prob * (dp - deltas[query, :1])).astype(BF16)
             results.append(
-                (ds, dot(prob.astype(BF16), scaled_grads[query], PLAIN), dot(ds, both(qq, query), PLAIN))
+                (
+                    dot(prob.astype(BF16), scaled_grads[query], PLAIN),
+                    dot(ds, both(qq, query), PLAIN),
+                    dot(key_pair(kall, pair), ds, FIRST),
+                )
             )
-        for pair, (ds, dv, dk) in zip(pairs, results):
-            weights[pair] = ds
-            slot = pair_slot[pair]
-            keys_out[slot] = key_pair(kall, pair)
-            pltpu.make_async_copy(weights.at[pair], ds_out.at[slot], sems.at[slot]).start()
+        for pair, query, (dv, dk, dq) in zip(pairs, queries, results):
             for place in range(2):
                 rows = slice(place * BLK, place * BLK + BLK)
                 dv_acc[pair_key[2 * pair + place]] += dv[rows]
                 dk_acc[pair_key[2 * pair + place]] += dk[rows]
+            dq_t[query] += dq
 
     over_pairs(grad_pairs)
-
-    @pl.loop(0, 32)
-    def _(slot):
-        pltpu.make_async_copy(zeros, ds_out.at[slot], sems.at[slot]).wait()
 
 
 def attention_call(ids, docs, *parts):
@@ -511,22 +493,16 @@
             jax.ShapeDtypeStruct((4, BLK, HD), F32),
             jax.ShapeDtypeStruct((32, BLK, HD), F32),
             jax.ShapeDtypeStruct((32, BLK, HD), F32),
-            jax.ShapeDtypeStruct((32, 2 * BLK, HD), BF16),
-            jax.ShapeDtypeStruct((32, 2 * BLK, 2 * BLK), BF16),
         ),
         in_specs=[SMEM, SMEM] + [VMEM] * 8,
-        out_specs=(VMEM,) * 7 + (HBM,),
+        out_specs=(VMEM,) * 6,
         scratch_shapes=[
             pltpu.SMEM((32,), jnp.int32),
             pltpu.SMEM((32,), jnp.int32),
             pltpu.SMEM((32,), jnp.int32),
             pltpu.SMEM((64,), jnp.int32),
             pltpu.SMEM((32,), jnp.int32),
-            pltpu.SMEM((32,), jnp.int32),
-            pltpu.SMEM((32,), jnp.int32),
             pltpu.VMEM((32, 2 * BLK, 2 * BLK), BF16),
-            pltpu.VMEM((2 * BLK, 2 * BLK), BF16),
-            pltpu.SemaphoreType.DMA((32,)),
             pltpu.VMEM((36, 8, 2 * BLK), F32),
             pltpu.VMEM((4, BLK, 2 * BLK), BF16),
             pltpu.VMEM((4, 2 * BLK, HD), BF16),
@@ -540,9 +516,8 @@
 
 def scatter_kernel(
     cq_h, ck_h, nq_h, nk_h, qg_h, kg_h, inv, out_t, dq_t, dk_noisy, dv_noisy, dk, dv,
-    pair_keys, ds_h,
     back, fin, inner_out,
-    raws, qg, kg, stage, k_out, v_out, x_out, vy, vq, vh, vx, kh, kx, ky, away, sums, dq_acc, ds,
+    raws, qg, kg, stage, k_out, v_out, x_out, vy, vq, vh, vx, kh, kx, ky, away, sums,
     send, recv, lsem,
 ):
     ctx, head, core, y, x = place()
@@ -556,7 +531,6 @@
     loads = [local.start(ref, raws.at[i]) for i, ref in enumerate((cq_h, ck_h, nq_h, nk_h))]
     loads += [local.start(qg_h, qg), local.start(kg_h, kg)]
     cq, ck, nq, nk = [raws.at[i] for i in range(4)]
-    ds_loads = [local.start(ds_h.at[pl.ds(8 * i, 8)], ds.at[i]) for i in range(2)]
     remote = Copies(send, recv, head)
 
     def mine(ref, step, row, half):
@@ -615,7 +589,11 @@
         return back.at[i, :, own_columns]
 
     swap = {}
-    def turn(ref, first, factor):
+    dk_pair, dv_pair = [
+        [ref.at[pl.ds(c * 2, 2)] for c in (core, 1 - core)] for ref in (dk_noisy, dv_noisy)
+    ]
+
+    def turn(index, ref, first, factor):
         for part in range(2):
             rows = slice(part * BLK, part * BLK + BLK)
             for c, own in ((core, True), (1 - core, False)):
@@ -635,6 +613,7 @@
             stage[i, rows, :] = ref[2 * (1 - core) + part]
         swap[i] = remote.start(stage.at[i], landing(i), partner)
 
+    turn(0, dq_t, 2, score_scale)
     turn_noisy(dk_noisy, 4)
 
     k_x = {}
@@ -648,63 +627,6 @@
         k_x[row, 1] = remote.start(k_out.at[row, 1], kx.at[row, 1], to_right)
 
     k_forward(1)
-
-    def pack_x(step, half, *others):
-        value = mine(dv, step, 0, half)
-        for other in others:
-            value = value + other[...].astype(F32)
-        x_out[step, half] = value.astype(BF16)
-
-    v_half = []
-    for half, target in ((0, to_left), (1, to_right)):
-        v_opposite[half].wait_recv()
-        pack_x(2, half)
-        x_out[2, half, SHIFT:] = (
-            mine(dv, 2, 0, half)[SHIFT:] + vy[2, half, SHIFT:].astype(F32)
-        ).astype(BF16)
-        v_half.append(remote.start(x_out.at[2, half], vh.at[half], target))
-    send_v(1, 1)
-    k_forward(0)
-    turn(out_t, 0, 1.0)
-    turn_noisy(dv_noisy, 5)
-
-    def add_queries(block):
-        dq_acc[block] = dq_t[block]
-        ds_loads[block].wait()
-
-        @pl.loop(0, 4)
-        def _(two):
-            keys = pair_keys[pl.ds(block * 8 + two * 2, 2)].reshape(4 * BLK, HD)
-            values = ds[block % 2, pl.ds(two * 2, 2)].reshape(4 * BLK, 2 * BLK)
-            dq_acc[block] += dot(keys, values, FIRST)
-
-        if block < 2:
-            later = block + 2
-            ds_loads.append(local.start(ds_h.at[pl.ds(8 * later, 8)], ds.at[block]))
-
-    add_queries(0)
-    pack_v(0)
-    k_x[1, 0].wait_recv()
-    k_x[1, 1].wait_recv()
-    for half in range(2):
-        pack_k(1, 0, half, kx.at[1, 0, half], kx.at[1, 1, half])
-    k_y = remote.start(k_out.at[1, 0], ky, to_y)
-    send_v(0, None)
-    add_queries(1)
-
-    v_y[3].wait_recv()
-    v_half[0].wait_recv()
-    pack_x(3, 0, vy.at[3, 0], vh.at[0])
-    pack_x(3, 1, vy.at[3, 1])
-    v_x = [remote.start(x_out.at[3], vx.at[0], to_left)]
-    add_queries(2)
-    v_y[1].wait_recv()
-    v_half[1].wait_recv()
-    pack_x(1, 0, vy.at[1, 0])
-    pack_x(1, 1, vy.at[1, 1], vh.at[1])
-    v_x.append(remote.start(x_out.at[1], vx.at[1], to_right))
-    add_queries(3)
-    turn(dq_acc, 2, score_scale)
 
     row = lax.broadcasted_iota(jnp.int32, (8, 512), 0)
 
@@ -724,6 +646,54 @@
         remote.start(sums.at[0], sums.at[step], ctx, (head + step) % 8) for step in range(1, 8)
     ]
 
+    def pack_x(step, half, *others):
+        value = mine(dv, step, 0, half)
+        for other in others:
+            value = value + other[...].astype(F32)
+        x_out[step, half] = value.astype(BF16)
+
+    v_half = []
+    for half, target in ((0, to_left), (1, to_right)):
+        v_opposite[half].wait_recv()
+        pack_x(2, half)
+        x_out[2, half, SHIFT:] = (
+            mine(dv, 2, 0, half)[SHIFT:] + vy[2, half, SHIFT:].astype(F32)
+        ).astype(BF16)
+        v_half.append(remote.start(x_out.at[2, half], vh.at[half], target))
+    send_v(1, 1)
+    k_forward(0)
+    turn(0, out_t, 0, 1.0)
+    turn_noisy(dv_noisy, 5)
+    k_x[1, 0].wait_recv()
+    k_x[1, 1].wait_recv()
+    for half in range(2):
+        pack_k(1, 0, half, kx.at[1, 0, half], kx.at[1, 1, half])
+    k_y = remote.start(k_out.at[1, 0], ky, to_y)
+    send_v(0, None)
+
+    v_y[3].wait_recv()
+    v_half[0].wait_recv()
+    pack_x(3, 0, vy.at[3, 0], vh.at[0])
+    pack_x(3, 1, vy.at[3, 1])
+    v_x = [remote.start(x_out.at[3], vx.at[0], to_left)]
+    v_y[1].wait_recv()
+    v_half[1].wait_recv()
+    pack_x(1, 0, vy.at[1, 0])
+    pack_x(1, 1, vy.at[1, 1], vh.at[1])
+    v_x.append(remote.start(x_out.at[1], vx.at[1], to_right))
+
+    for copy in exchange:
+        copy.wait_recv()
+    total = sums[0]
+    for step in range(1, 8):
+        total = total + sums[step]
+    inverses = jnp.transpose(inv[...])
+    means = jnp.transpose(total) / FEAT
+    for index, raw, gain, i in normal:
+        inverse = inverses[:, index : index + 1]
+        factor = inverse * inverse * inverse * means[:, index : index + 1]
+        back[i] = inverse * (gain[...] * back[i]) - raw[...].astype(F32) * factor
+
     def finish(index, ref, factor, terms):
         values = []
         for half in range(2):
@@ -745,18 +715,6 @@
     k_exchange = [
         remote.start(sums.at[8], sums.at[8 + step], ctx, (head + step) % 8) for step in range(1, 8)
     ]
-    for copy in exchange:
-        copy.wait_recv()
-    total = sums[0]
-    for step in range(1, 8):
-        total = total + sums[step]
-    inverses = jnp.transpose(inv[...])
-    means = jnp.transpose(total) / FEAT
-    for index, raw, gain, i in normal:
-        inverse = inverses[:, index : index + 1]
-        factor = inverse * inverse * inverse * means[:, index : index + 1]
-        back[i] = inverse * (gain[...] * back[i]) - raw[...].astype(F32) * factor
-
     v_y[0].wait_recv()
     v_x[0].wait_recv()
     v_x[1].wait_recv()
@@ -784,7 +742,7 @@
             jax.ShapeDtypeStruct((2, 512, 256), F32),
             jax.ShapeDtypeStruct((8, 512), F32),
         ),
-        in_specs=[HBM] * 6 + [VMEM] * 8 + [HBM],
+        in_specs=[HBM] * 6 + [VMEM] * 7,
         out_specs=(VMEM, VMEM, VMEM),
         scratch_shapes=[
             pltpu.VMEM((4, 512, 256), BF16),
@@ -803,14 +761,12 @@
             pltpu.VMEM((2, 512, HD), BF16),
             pltpu.VMEM((2, 512, HD), F32),
             pltpu.VMEM((16, 8, 512), F32),
-            pltpu.VMEM((4, HD, 2 * BLK), F32),
-            pltpu.VMEM((2, 8, 2 * BLK, 2 * BLK), BF16),
             pltpu.SemaphoreType.DMA((48,)),
             pltpu.SemaphoreType.DMA((48,)),
-            pltpu.SemaphoreType.DMA((12,)),
+            pltpu.SemaphoreType.DMA((8,)),
         ],
         compiler_params=pltpu.CompilerParams(
-            collective_id=1, has_side_effects=True, vmem_limit_bytes=30 * 2**20
+            collective_id=1, has_side_effects=True, vmem_limit_bytes=20 * 2**20
         ),
     )(*operands)
 
@@ -869,9 +825,7 @@
     ]
     *parts, inv, ids = gather_call(*pinned)
     grads = attention_call(ids, docs, *parts)
-    *grads, ds = grads
-    ds = pltpu.with_memory_space_constraint(ds, pltpu.HBM)
-    back, fin, inner = scatter_call(*pinned[:6], inv, *grads, ds)
+    back, fin, inner = scatter_call(*pinned[:6], inv, *grads)
     return finish_call(clean_k, kg, inv, inner, back, fin)
 
 

time: 103 us -> 107 us (1.039)
  Pallas kernels: 102 us -> 106 us
    pallas_call x1, Pallas kernels: 38.5 us -> 55.2 us  [scatter_call(): pl.pallas_call(scatter_kernel, name='scatter_grads', out_shape=(jax.Shape...]
    pallas_call x1, Pallas kernels: 18.8 us -> 6.14 us  [attention_call(): pl.pallas_call(attention_kernel, name='attention', out_shape=(jax.ShapeDt...]
where the time goes in v7:
time: 107 us; the launch traced here: 106 us
  Pallas kernels  106 us (99%)
    pallas_call x1, Pallas kernels, scatter_call(): pl.pallas_call(scatter_kernel, name='scatter_grads', out_shape=(jax.Shape...  55.2 us
    pallas_call x1, Pallas kernels, gather_call(): pl.pallas_call(gather_kernel, name='gather_keys', out_shape=(jax.ShapeDty...  42.1 us
    pallas_call x1, Pallas kernels, attention_call(): pl.pallas_call(attention_kernel, name='attention', out_shape=(jax.ShapeDt...  6.14 us

profile of v7, /device:TPU:1, one launch (start us, length us, event | category | flops | bytes accessed | tf_op | source)
XLA Modules:
  0.0 106.2 jit_solution(16698557123860809131)
XLA Ops:
  0.6 42.1 %gather_keys.1 = (bf16[16,528,128]{2,1,0:T(8,128)(2,1)S(1)}, bf16[16,512,128]{2,1,0:T(8,128)(2,1)S(1)}, bf16[4,2,256,128]{3,2,1,0:T(8,128)(2,1)S(1)}, bf16[4,2,2...) custom-call(bf16[512,256]{1,0:T(8,128)(2,1)} %cq_h.3, ...), custom_call_target="tpu_custom_call" | custom-call | tf_op jit(solution)/shard_map/gather_keys/pallas_call | solution.py:277
  42.7 6.1 %attention.1 = (f32[4,128,512]{2,1,0:T(8,128)S(1)}, f32[4,128,512]{2,1,0:T(8,128)S(1)}, f32[4,256,128]{2,1,0:T(8,128)S(1)}, f32[4,256,128]{2,1,0:T(8,128)S(1)}, ...) custom-call(s32[16,128]{1,0:T(8,128)S(1)} %get-tuple-element.28.ids, s32[32]{0:T(128)} %docs.1, ...), custom_call_target="tpu_custom_call" | custom-call | tf_op jit(solution)/shard_map/attention/pallas_call | solution.py:486
  48.9 0.0 copy-start
  48.9 0.0 copy-start.1
  48.9 55.2 %scatter_grads.1 = (f32[6,512,256]{2,1,0:T(8,128)S(1)}, f32[2,512,256]{2,1,0:T(8,128)S(1)}, f32[8,512]{1,0:T(8,128)S(1)}) custom-call(bf16[512,256]{1,0:T(8,128)(2,1)} %cq_h.3, bf16[512,256]{1,0:T(8,128)(2,1)} %ck.1, bf16[512,256]{1,0:T(8,128)(2,1)} %nq_h.3, bf16[512,256]{1,0:T(8,128)(2,1)} %nk_h.3, f32[1,256]{1,0:T(1,128)} %bitcast.12, f32[1,256]{1,0:T(1,128)} %bitcast.6, ...), custom_call_target="tpu_custom_call" | custom-call | tf_op jit(solution)/shard_map/scatter_grads/pallas_call | solution.py:737
  104.1 0.0 copy-done
  104.1 0.0 copy-done.1
  104.1 2.1 %finish.1 = (f32[512,256]{1,0:T(8,128)}, f32[512,256]{1,0:T(8,128)}, f32[512,256]{1,0:T(8,128)}, f32[512,256]{1,0:T(8,128)}, f32[512,256]{1,0:T(8,128)}, /*index...) custom-call(bf16[512,256]{1,0:T(8,128)(2,1)S(1)} %copy-done, f32[1,256]{1,0:T(1,128)S(1)} %bitcast.7, ...), custom_call_target="tpu_custom_call" | custom-call | tf_op jit(solution)/shard_map/finish/pallas_call | solution.py:802
Async XLA Ops:
  48.9 55.2 %copy-start = (bf16[512,256]{1,0:T(8,128)(2,1)S(1)}, bf16[512,256]{1,0:T(8,128)(2,1)}, u32[]{:S(2)}) copy-start(bf16[512,256]{1,0:T(8,128)(2,1)} %ck.1) | copy-start | bytes 786436
  48.9 55.2 %copy-start.1 = (f32[256]{0:T(256)S(1)}, f32[256]{0:T(256)}, u32[]{:S(2)}) copy-start(f32[256]{0:T(256)} %param.19) | copy-start | bytes 3076

commit v8 on v7

--- a/solution.py
+++ b/solution.py
@@ -23,8 +23,10 @@
 FIRST = (((0,), (0,)), ((), ()))
 PLAIN = (((1,), (0,)), ((), ()))
 PACKET = 528
-SHIFT = 160
+SHIFT = 32
 GROUP = 2
+SCALE = 1.0 / math.sqrt(HD)
+SCALE2 = SCALE * math.log2(math.e)
 
 
 def dot(a, b, dims):
@@ -101,7 +103,7 @@
 
 def gather_kernel(
     cq_h, ck_h, nq_h, nk_h, qg_h, kg_h, cv, nv, gc, gn, owned,
-    kall, vall, qq, gg, kn, vn, own_s, grads_t, inv_out, ids_out,
+    kall, vall, qq, gg, kn, vn, own_w, own_peak, own_sum, out_own, grads_t, inv_out, ids_out,
     owned_s, raws, qg, kg, k_packet, normed, sums, send, recv, wide_send, wide_recv, lsem,
 ):
     ctx, head, core, y, x = place()
@@ -235,10 +237,17 @@
     def own_block(index):
         side, rows = index // 2, slice(index % 2 * BLK, index % 2 * BLK + BLK)
         packet = 2 * chip_of(x, y) + side
-        own_s[index, :, :BLK] = dot(kall[packet, rows, :], qq[index, 0], LAST)
-        own_s[index, :, BLK:] = dot(kn[index], qq[index, 1], LAST)
-        for kind in range(2):
+        own = ((kall[packet, rows, :], vall[packet, rows, :]), (kn[index], vn[index]))
+        for kind, (keys, values) in enumerate(own):
             columns = slice(kind * BLK, kind * BLK + BLK)
+            scores = dot(keys, qq[index, kind], LAST) * SCALE2
+            peak = jnp.max(scores, axis=0, keepdims=True)
+            weights = jnp.exp2(scores - peak)
+            low = weights.astype(BF16)
+            own_peak[index, :, columns] = jnp.broadcast_to(peak, (8, BLK))
+            own_sum[index, :, columns] = jnp.sum(weights.reshape(BLK // 8, 8, BLK), axis=0)
+            own_w[index, :, columns] = low
+            out_own[index, :, columns] = dot(values, low, FIRST)
             grads_t[index, :, columns] = jnp.transpose(gg[index, kind].astype(F32))
 
     own_block(0)
@@ -284,13 +293,16 @@
             jax.ShapeDtypeStruct((4, 2, BLK, HD), BF16),
             jax.ShapeDtypeStruct((4, BLK, HD), BF16),
             jax.ShapeDtypeStruct((4, BLK, HD), BF16),
-            jax.ShapeDtypeStruct((4, BLK, 2 * BLK), F32),
+            jax.ShapeDtypeStruct((4, BLK, 2 * BLK), BF16),
+            jax.ShapeDtypeStruct((4, 8, 2 * BLK), F32),
+            jax.ShapeDtypeStruct((4, 8, 2 * BLK), F32),
+            jax.ShapeDtypeStruct((4, HD, 2 * BLK), F32),
             jax.ShapeDtypeStruct((4, HD, 2 * BLK), F32),
             jax.ShapeDtypeStruct((8, 512), F32),
             jax.ShapeDtypeStruct((16, HD), jnp.int32),
         ),
         in_specs=[HBM] * 11,
-        out_specs=(VMEM,) * 10,
+        out_specs=(VMEM,) * 13,
         scratch_shapes=[
             pltpu.SMEM((2,), jnp.int32),
             pltpu.VMEM((4, 512, 256), BF16),
@@ -312,30 +324,25 @@
 
 
 def attention_kernel(
-    ids, docs, kall, vall, qq, gg, kn, vn, own_s, grads_t,
+    ids, docs, kall, vall, qq, gg, kn, vn, own_w, own_peak, own_sum, out_own, grads_t,
     out_t, dq_t, dk_noisy, dv_noisy, dk_acc, dv_acc,
     where_is, first_of, pair_query, pair_key, pair_bias,
-    weights, pair_peaks, own_weights, scaled_grads, peaks, sums, deltas,
+    weights, pair_peaks, scaled_grads, peaks, sums, deltas,
 ):
     chip = lax.axis_index("ctx") // 2
-    scale = 1.0 / math.sqrt(HD)
-    scale2 = scale * math.log2(math.e)
-
-    @pl.loop(0, 16)
-    def _(packet):
-        where_is[ids[packet, 0]] = packet * 2
-        where_is[ids[packet, 1]] = packet * 2 + 1
-
-    first_of[0] = 0
-
-    @pl.loop(1, 32)
-    def _(block):
-        first_of[block] = jnp.where(docs[block] == docs[block - 1], first_of[block - 1], block)
-
-    @pl.loop(0, 32)
-    def _(block):
-        dk_acc[block] = jnp.zeros((BLK, HD), F32)
-        dv_acc[block] = jnp.zeros((BLK, HD), F32)
+
+    def clear(stored):
+        dk_acc[stored] = jnp.zeros((BLK, HD), F32)
+        dv_acc[stored] = jnp.zeros((BLK, HD), F32)
+
+    def begin_of(block, begin):
+        clear(block)
+        where_is[ids[block // 2, block % 2]] = block
+        begin = jnp.where(docs[block] == docs[jnp.maximum(block - 1, 0)], begin, block)
+        first_of[block] = begin
+        return begin
+
+    lax.fori_loop(0, 32, begin_of, 0)
 
     def key_rows(buf, stored):
         start = pl.multiple_of((stored % 2) * BLK, BLK)
@@ -387,23 +394,16 @@
         return jnp.broadcast_to(row, (8, 2 * BLK))
 
     for index in range(4):
-        own = own_s[index]
-        peak = jnp.max(own, axis=0, keepdims=True) * scale2
-        peaks[index] = spread_rows(peak)
-        own = jnp.exp2(own * scale2 - peak)
-        sums[index] = totals(own)
-        own_low = own.astype(BF16)
-        own_weights[index] = own_low
-        out_t[index, :, :BLK] = dot(key_rows(vall, chip * 4 + index), own_low[:, :BLK], FIRST)
-        out_t[index, :, BLK:] = dot(vn[index], own_low[:, BLK:], FIRST)
-        pair_peaks[32 + index] = peaks[index]
+        peaks[index] = own_peak[index]
+        sums[index] = own_sum[index]
+        out_t[index] = out_own[index]
 
     def forward_pairs(pairs):
         queries = [pair_query[pair] for pair in pairs]
         scores = [
             dot(key_pair(kall, pair), both(qq, query), LAST) for pair, query in zip(pairs, queries)
         ]
-        tops_of = [jnp.max(tops(score), axis=0, keepdims=True) * scale2 for score in scores]
+        tops_of = [jnp.max(tops(score), axis=0, keepdims=True) * SCALE2 for score in scores]
         results = []
         for pair, query, score, top in zip(pairs, queries, scores, tops_of):
             before = peaks[query]
@@ -412,8 +412,8 @@
             pair_peaks[pair] = now
             peak = now[:1]
             hidden = peak + jnp.where(pair_bias[pair] == 1, jnp.inf, 0.0)
-            upper = jnp.exp2(score[:BLK] * scale2 - peak)
-            lower = jnp.exp2(score[BLK:] * scale2 - hidden)
+            upper = jnp.exp2(score[:BLK] * SCALE2 - peak)
+            lower = jnp.exp2(score[BLK:] * SCALE2 - hidden)
             low = jnp.concatenate([upper.astype(BF16), lower.astype(BF16)], axis=0)
             weights[pair] = low
             results.append(
@@ -431,7 +431,7 @@
 
     for index in range(4):
         stored_own = chip * 4 + index
-        own_decay = jnp.exp2(pair_peaks[32 + index] - peaks[index])[:1]
+        own_decay = jnp.exp2(own_peak[index] - peaks[index])[:1]
         inverse_sum = 1.0 / jnp.sum(sums[index], axis=0, keepdims=True)
         out = out_t[index] * inverse_sum
         out_t[index] = out
@@ -440,7 +440,7 @@
         deltas[index] = spread_rows(delta)
         grads = jnp.transpose(grad_rows).astype(BF16)
         scaled_grads[index] = grads
-        own = own_weights[index].astype(F32) * own_decay
+        own = own_w[index].astype(F32) * own_decay
         own_low = own.astype(BF16)
         own_dp = jnp.concatenate(
             [
@@ -453,7 +453,7 @@
         dv_acc[stored_own] += dot(own_low[:, :BLK], grads[:BLK], PLAIN)
         dk_acc[stored_own] += dot(own_ds[:, :BLK], qq[index, 0], PLAIN)
         dv_noisy[index] = dot(own_low[:, BLK:], grads[BLK:], PLAIN)
-        dk_noisy[index] = dot(own_ds[:, BLK:], qq[index, 1], PLAIN) * scale
+        dk_noisy[index] = dot(own_ds[:, BLK:], qq[index, 1], PLAIN) * SCALE
         dq_t[index, :, :BLK] = dot(key_rows(kall, stored_own), own_ds[:, :BLK], FIRST)
         dq_t[index, :, BLK:] = dot(kn[index], own_ds[:, BLK:], FIRST)
 
@@ -494,7 +494,7 @@
             jax.ShapeDtypeStruct((32, BLK, HD), F32),
             jax.ShapeDtypeStruct((32, BLK, HD), F32),
         ),
-        in_specs=[SMEM, SMEM] + [VMEM] * 8,
+        in_specs=[SMEM, SMEM] + [VMEM] * 11,
         out_specs=(VMEM,) * 6,
         scratch_shapes=[
             pltpu.SMEM((32,), jnp.int32),
@@ -503,8 +503,7 @@
             pltpu.SMEM((64,), jnp.int32),
             pltpu.SMEM((32,), jnp.int32),
             pltpu.VMEM((32, 2 * BLK, 2 * BLK), BF16),
-            pltpu.VMEM((36, 8, 2 * BLK), F32),
-            pltpu.VMEM((4, BLK, 2 * BLK), BF16),
+            pltpu.VMEM((32, 8, 2 * BLK), F32),
             pltpu.VMEM((4, 2 * BLK, HD), BF16),
             pltpu.VMEM((4, 8, 2 * BLK), F32),
             pltpu.VMEM((4, 8, 2 * BLK), F32),

time: 107 us -> 109 us (1.019)
  Pallas kernels: 106 us -> 108 us
    pallas_call x1, Pallas kernels: 6.14 us -> 22.1 us  [attention_call(): pl.pallas_call(attention_kernel, name='attention', out_shape=(jax.ShapeDt...]
    pallas_call x1, Pallas kernels: 55.2 us -> 40.5 us  [scatter_call(): pl.pallas_call(scatter_kernel, name='scatter_grads', out_shape=(jax.Shape...]
    pallas_call x1, Pallas kernels: 42.1 us -> 43.5 us  [gather_call(): pl.pallas_call(gather_kernel, name='gather_keys', out_shape=(jax.ShapeDty...]
where the time goes in v8:
time: 109 us
  Pallas kernels  108 us (99%)
    pallas_call x1, Pallas kernels, gather_call(): pl.pallas_call(gather_kernel, name='gather_keys', out_shape=(jax.ShapeDty...  43.5 us
    pallas_call x1, Pallas kernels, scatter_call(): pl.pallas_call(scatter_kernel, name='scatter_grads', out_shape=(jax.Shape...  40.5 us
    pallas_call x1, Pallas kernels, attention_call(): pl.pallas_call(attention_kernel, name='attention', out_shape=(jax.ShapeDt...  22.1 us

profile of v8, /device:TPU:1, one launch (start us, length us, event | category | flops | bytes accessed | tf_op | source)
XLA Modules:
  0.0 109.0 jit_solution(6827759997052637958)
XLA Ops:
  0.6 43.5 %gather_keys.1 = (bf16[16,528,128]{2,1,0:T(8,128)(2,1)S(1)}, bf16[16,512,128]{2,1,0:T(8,128)(2,1)S(1)}, bf16[4,2,256,128]{3,2,1,0:T(8,128)(2,1)S(1)}, bf16[4,2,2...) custom-call(bf16[512,256]{1,0:T(8,128)(2,1)} %cq_h.3, ...), custom_call_target="tpu_custom_call" | custom-call | tf_op jit(solution)/shard_map/gather_keys/pallas_call | solution.py:286
  44.1 22.1 %attention.1 = (f32[4,128,512]{2,1,0:T(8,128)S(1)}, f32[4,128,512]{2,1,0:T(8,128)S(1)}, f32[4,256,128]{2,1,0:T(8,128)S(1)}, f32[4,256,128]{2,1,0:T(8,128)S(1)}, ...) custom-call(s32[16,128]{1,0:T(8,128)S(1)} %get-tuple-element.31.ids, s32[32]{0:T(128)} %docs.1, ...), custom_call_target="tpu_custom_call" | custom-call | tf_op jit(solution)/shard_map/attention/pallas_call | solution.py:486
  66.2 0.0 copy-start
  66.3 0.0 copy-start.1
  66.3 40.5 %scatter_grads.1 = (f32[6,512,256]{2,1,0:T(8,128)S(1)}, f32[2,512,256]{2,1,0:T(8,128)S(1)}, f32[8,512]{1,0:T(8,128)S(1)}) custom-call(bf16[512,256]{1,0:T(8,128)(2,1)} %cq_h.3, bf16[512,256]{1,0:T(8,128)(2,1)} %ck.1, bf16[512,256]{1,0:T(8,128)(2,1)} %nq_h.3, bf16[512,256]{1,0:T(8,128)(2,1)} %nk_h.3, f32[1,256]{1,0:T(1,128)} %bitcast.12, f32[1,256]{1,0:T(1,128)} %bitcast.6, ...), custom_call_target="tpu_custom_call" | custom-call | tf_op jit(solution)/shard_map/scatter_grads/pallas_call | solution.py:736
  106.8 0.0 copy-done
  106.8 0.0 copy-done.1
  106.8 2.1 %finish.1 = (f32[512,256]{1,0:T(8,128)}, f32[512,256]{1,0:T(8,128)}, f32[512,256]{1,0:T(8,128)}, f32[512,256]{1,0:T(8,128)}, f32[512,256]{1,0:T(8,128)}, /*index...) custom-call(bf16[512,256]{1,0:T(8,128)(2,1)S(1)} %copy-done, f32[1,256]{1,0:T(1,128)S(1)} %bitcast.7, ...), custom_call_target="tpu_custom_call" | custom-call | tf_op jit(solution)/shard_map/finish/pallas_call | solution.py:801
Async XLA Ops:
  66.2 40.5 %copy-start = (bf16[512,256]{1,0:T(8,128)(2,1)S(1)}, bf16[512,256]{1,0:T(8,128)(2,1)}, u32[]{:S(2)}) copy-start(bf16[512,256]{1,0:T(8,128)(2,1)} %ck.1) | copy-start | bytes 786436
  66.3 40.5 %copy-start.1 = (f32[256]{0:T(256)S(1)}, f32[256]{0:T(256)}, u32[]{:S(2)}) copy-start(f32[256]{0:T(256)} %param.19) | copy-start | bytes 3076

commit v9 on v4

--- a/solution.py
+++ b/solution.py
@@ -25,6 +25,8 @@
 PACKET = 528
 SHIFT = 160
 GROUP = 2
+SCALE = 1.0 / math.sqrt(HD)
+SCALE2 = SCALE * math.log2(math.e)
 
 
 def dot(a, b, dims):
@@ -101,7 +103,7 @@
 
 def gather_kernel(
     cq_h, ck_h, nq_h, nk_h, qg_h, kg_h, cv, nv, gc, gn, owned,
-    kall, vall, qq, gg, kn, vn, own_s, grads_t, inv_out, ids_out,
+    kall, vall, qq, gg, kn, vn, own_w, own_peak, own_sum, out_own, grads_t, inv_out, ids_out,
     owned_s, raws, qg, kg, k_packet, normed, sums, send, recv, wide_send, wide_recv, lsem,
 ):
     ctx, head, core, y, x = place()
@@ -211,16 +213,17 @@
     def spread(view, px, py):
         return remote.start(view, view, ctx_of(px, py, core))
 
-    v_half, v_y = [], []
-    for number, near, far, half in ((1, left, right, 0), (2, right, left, 1)):
+    v_half, v_y, k_half = [], [], []
+    sides = ((1, left, right, 0), (2, right, left, 1))
+    for number, near, far, half in sides:
         arrived(0, number, vall, half)
         v_half.append(spread(part(vall, near, y, half), far, y))
-        arrived(0, number, vall, 1 - half)
-        v_y.append(spread(slot(vall, near, y), x, 1 - y))
     arrived(3, 0, kall, 0)
     arrived(3, 0, kall, 1)
     k_right = spread(slot(kall, x, 1 - y), right, y)
     k_left = spread(slot(kall, x, 1 - y), left, y)
+    arrived(0, 1, vall, 1)
+    v_y.append(spread(slot(vall, left, y), x, 1 - y))
 
     v_own.wait()
     k_own.wait()
@@ -234,35 +237,43 @@
     def own_block(index):
         side, rows = index // 2, slice(index % 2 * BLK, index % 2 * BLK + BLK)
         packet = 2 * chip_of(x, y) + side
-        grad_clean, grad_noisy = gg[index, 0], gg[index, 1]
-        own_s[index, :, :BLK] = dot(kall[packet, rows, :], qq[index, 0], LAST)
-        own_s[index, :, BLK:] = dot(kn[index], qq[index, 1], LAST)
-        grads_t[index, :, :BLK] = jnp.transpose(grad_clean.astype(F32))
-        grads_t[index, :, BLK:] = jnp.transpose(grad_noisy.astype(F32))
+        own = ((kall[packet, rows, :], vall[packet, rows, :]), (kn[index], vn[index]))
+        for kind, (keys, values) in enumerate(own):
+            columns = slice(kind * BLK, kind * BLK + BLK)
+            scores = dot(keys, qq[index, kind], LAST) * SCALE2
+            peak = jnp.max(scores, axis=0, keepdims=True)
+            weights = jnp.exp2(scores - peak)
+            low = weights.astype(BF16)
+            own_peak[index, :, columns] = jnp.broadcast_to(peak, (8, BLK))
+            own_sum[index, :, columns] = jnp.sum(weights.reshape(BLK // 8, 8, BLK), axis=0)
+            own_w[index, :, columns] = low
+            out_own[index, :, columns] = dot(values, low, FIRST)
+            grads_t[index, :, columns] = jnp.transpose(gg[index, kind].astype(F32))
 
     own_block(0)
-    own_block(1)
-    k_half = []
-    for number, near, far, half in ((1, left, right, 0), (2, right, left, 1)):
+    for number, near, far, half in sides:
         arrived(3, number, kall, half)
         k_half.append(spread(part(kall, near, y, half), far, y))
         arrived(3, number, kall, 1 - half)
+    own_block(1)
+    arrived(0, 2, vall, 0)
+    v_y.append(spread(slot(vall, right, y), x, 1 - y))
     own_block(2)
-    own_block(3)
+    v_half[0].wait_recv()
+    v_half[1].wait_recv()
+    v_y[0].wait_recv()
+    v_far = [spread(rows_of(left, 1 - y, 0, 0, SHIFT), right, y)]
     for half in range(2):
-        v_half[half].wait_recv()
         v_y.append(spread(rows_of(opposite, y, half, SHIFT, 512 - SHIFT), x, 1 - y))
-    arrived(0, 0, vall, 0)
-    arrived(0, 0, vall, 1)
-    v_far = []
-    for half, near, far in ((0, left, right), (1, right, left)):
-        v_y[half].wait_recv()
-        v_far.append(spread(rows_of(near, 1 - y, half, 0, SHIFT), far, y))
     k_right.wait_recv()
     k_half.append(spread(part(kall, left, 1 - y, 0), right, y))
     k_left.wait_recv()
     k_half.append(spread(part(kall, right, 1 - y, 1), left, y))
-
+    own_block(3)
+    v_y[1].wait_recv()
+    v_far.append(spread(rows_of(right, 1 - y, 1, 0, SHIFT), left, y))
+    arrived(0, 0, vall, 0)
+    arrived(0, 0, vall, 1)
     for copy in v_y[2:] + v_far + k_half:
         copy.wait_recv()
     names = jnp.max(kall[:, 512:, :].astype(F32), axis=1)
@@ -282,13 +293,16 @@
             jax.ShapeDtypeStruct((4, 2, BLK, HD), BF16),
             jax.ShapeDtypeStruct((4, BLK, HD), BF16),
             jax.ShapeDtypeStruct((4, BLK, HD), BF16),
-            jax.ShapeDtypeStruct((4, BLK, 2 * BLK), F32),
+            jax.ShapeDtypeStruct((4, BLK, 2 * BLK), BF16),
+            jax.ShapeDtypeStruct((4, 8, 2 * BLK), F32),
+            jax.ShapeDtypeStruct((4, 8, 2 * BLK), F32),
+            jax.ShapeDtypeStruct((4, HD, 2 * BLK), F32),
             jax.ShapeDtypeStruct((4, HD, 2 * BLK), F32),
             jax.ShapeDtypeStruct((8, 512), F32),
             jax.ShapeDtypeStruct((16, HD), jnp.int32),
         ),
         in_specs=[HBM] * 11,
-        out_specs=(VMEM,) * 10,
+        out_specs=(VMEM,) * 13,
         scratch_shapes=[
             pltpu.SMEM((2,), jnp.int32),
             pltpu.VMEM((4, 512, 256), BF16),
@@ -310,30 +324,25 @@
 
 
 def attention_kernel(
-    ids, docs, kall, vall, qq, gg, kn, vn, own_s, grads_t,
+    ids, docs, kall, vall, qq, gg, kn, vn, own_w, own_peak, own_sum, out_own, grads_t,
     out_t, dq_t, dk_noisy, dv_noisy, dk_acc, dv_acc,
     where_is, first_of, pair_query, pair_key, pair_bias,
-    scores, weights, own_weights, scaled_grads, peaks, sums, deltas,
+    scores, weights, scaled_grads, peaks, sums, decays, deltas,
 ):
     chip = lax.axis_index("ctx") // 2
-    scale = 1.0 / math.sqrt(HD)
-    scale2 = scale * math.log2(math.e)
-
-    @pl.loop(0, 16)
-    def _(packet):
-        where_is[ids[packet, 0]] = packet * 2
-        where_is[ids[packet, 1]] = packet * 2 + 1
-
-    first_of[0] = 0
-
-    @pl.loop(1, 32)
-    def _(block):
-        first_of[block] = jnp.where(docs[block] == docs[block - 1], first_of[block - 1], block)
-
-    @pl.loop(0, 32)
-    def _(block):
-        dk_acc[block] = jnp.zeros((BLK, HD), F32)
-        dv_acc[block] = jnp.zeros((BLK, HD), F32)
+
+    def clear(stored):
+        dk_acc[stored] = jnp.zeros((BLK, HD), F32)
+        dv_acc[stored] = jnp.zeros((BLK, HD), F32)
+
+    def begin_of(block, begin):
+        clear(block)
+        where_is[ids[block // 2, block % 2]] = block
+        begin = jnp.where(docs[block] == docs[jnp.maximum(block - 1, 0)], begin, block)
+        first_of[block] = begin
+        return begin
+
+    lax.fori_loop(0, 32, begin_of, 0)
 
     def key_rows(buf, stored):
         start = pl.multiple_of((stored % 2) * BLK, BLK)
@@ -383,7 +392,7 @@
 
         first = 2 * side
         for half in range(2):
-            peaks[half] = tops(own_s[first + half])
+            peaks[half] = own_peak[first + half]
 
         def score_pairs(pairs):
             queries = [pair_query[pair] for pair in pairs]
@@ -393,20 +402,18 @@
             ]
             for pair, query, value in zip(pairs, queries, values):
                 scores[pair] = value
-                peaks[query] = jnp.maximum(peaks[query], tops(value))
+                peaks[query] = jnp.maximum(peaks[query], tops(value) * SCALE2)
 
         over_pairs(score_pairs)
 
         for half in range(2):
             index = first + half
-            peak = jnp.max(peaks[half], axis=0, keepdims=True) * scale2
+            peak = jnp.max(peaks[half], axis=0, keepdims=True)
+            decay = jnp.exp2(own_peak[index] - peak)
             peaks[half] = jnp.broadcast_to(peak, (8, 2 * BLK))
-            own = jnp.exp2(own_s[index] * scale2 - peak)
-            sums[half] = totals(own)
-            own_low = own.astype(BF16)
-            own_weights[half] = own_low
-            out_t[index, :, :BLK] = dot(key_rows(vall, chip * 4 + index), own_low[:, :BLK], FIRST)
-            out_t[index, :, BLK:] = dot(vn[index], own_low[:, BLK:], FIRST)
+            decays[half] = decay
+            sums[half] = own_sum[index] * decay
+            out_t[index] = out_own[index] * decay[:1]
 
         def value_pairs(pairs):
             queries = [pair_query[pair] for pair in pairs]
@@ -414,8 +421,8 @@
             for pair, query in zip(pairs, queries):
                 peak = peaks[query, :1]
                 hidden = peak + jnp.where(pair_bias[pair] == 1, jnp.inf, 0.0)
-                upper = jnp.exp2(scores[pair, :BLK] * scale2 - peak)
-                lower = jnp.exp2(scores[pair, BLK:] * scale2 - hidden)
+                upper = jnp.exp2(scores[pair, :BLK] * SCALE2 - peak)
+                lower = jnp.exp2(scores[pair, BLK:] * SCALE2 - hidden)
                 low = jnp.concatenate([upper.astype(BF16), lower.astype(BF16)], axis=0)
                 weights[pair] = low
                 outs.append(dot(key_pair(vall, pair), low, FIRST))
@@ -437,7 +444,8 @@
             deltas[half] = jnp.broadcast_to(delta, (8, 2 * BLK))
             grads = jnp.transpose(grad_rows).astype(BF16)
             scaled_grads[half] = grads
-            own_low = own_weights[half]
+            own = own_w[index].astype(F32) * decays[half, :1]
+            own_low = own.astype(BF16)
             own_dp = jnp.concatenate(
                 [
                     dot(key_rows(vall, stored_own), grads[:BLK], LAST),
@@ -445,11 +453,11 @@
                 ],
                 axis=1,
             )
-            own_ds = (own_low.astype(F32) * (own_dp - delta)).astype(BF16)
+            own_ds = (own * (own_dp - delta)).astype(BF16)
             dv_acc[stored_own] += dot(own_low[:, :BLK], grads[:BLK], PLAIN)
             dk_acc[stored_own] += dot(own_ds[:, :BLK], qq[index, 0], PLAIN)
             dv_noisy[index] = dot(own_low[:, BLK:], grads[BLK:], PLAIN)
-            dk_noisy[index] = dot(own_ds[:, BLK:], qq[index, 1], PLAIN) * scale
+            dk_noisy[index] = dot(own_ds[:, BLK:], qq[index, 1], PLAIN) * SCALE
             dq_t[index, :, :BLK] = dot(key_rows(kall, stored_own), own_ds[:, :BLK], FIRST)
             dq_t[index, :, BLK:] = dot(kn[index], own_ds[:, BLK:], FIRST)
 
@@ -489,18 +497,18 @@
             jax.ShapeDtypeStruct((32, BLK, HD), F32),
             jax.ShapeDtypeStruct((32, BLK, HD), F32),
         ),
-        in_specs=[SMEM, SMEM] + [VMEM] * 8,
+        in_specs=[SMEM, SMEM] + [VMEM] * 11,
         out_specs=(VMEM,) * 6,
         scratch_shapes=[
             pltpu.SMEM((32,), jnp.int32),
             pltpu.SMEM((32,), jnp.int32),
-            pltpu.SMEM((16,), jnp.int32),
+            pltpu.SMEM((32,), jnp.int32),
             pltpu.SMEM((32,), jnp.int32),
             pltpu.SMEM((16,), jnp.int32),
             pltpu.VMEM((16, 2 * BLK, 2 * BLK), F32),
             pltpu.VMEM((16, 2 * BLK, 2 * BLK), BF16),
-            pltpu.VMEM((2, BLK, 2 * BLK), BF16),
             pltpu.VMEM((2, 2 * BLK, HD), BF16),
+            pltpu.VMEM((2, 8, 2 * BLK), F32),
             pltpu.VMEM((2, 8, 2 * BLK), F32),
             pltpu.VMEM((2, 8, 2 * BLK), F32),
             pltpu.VMEM((2, 8, 2 * BLK), F32),

time: 104 us -> 99.4 us (0.956)
  Pallas kernels: 103 us -> 98.2 us
    pallas_call x1, Pallas kernels: 55.5 us -> 35.5 us  [scatter_call(): pl.pallas_call(scatter_kernel, name='scatter_grads', out_shape=(jax.Shape...]
    pallas_call x1, Pallas kernels: 5.6 us -> 18.5 us  [attention_call(): pl.pallas_call(attention_kernel, name='attention', out_shape=(jax.ShapeDt...]
    pallas_call x1, Pallas kernels: 40 us -> 42.1 us  [gather_call(): pl.pallas_call(gather_kernel, name='gather_keys', out_shape=(jax.ShapeDty...]
where the time goes in v9:
time: 99.4 us; the launch traced here: 98.9 us
  Pallas kernels  98.2 us (99%)
    pallas_call x1, Pallas kernels, gather_call(): pl.pallas_call(gather_kernel, name='gather_keys', out_shape=(jax.ShapeDty...  42.1 us
    pallas_call x1, Pallas kernels, scatter_call(): pl.pallas_call(scatter_kernel, name='scatter_grads', out_shape=(jax.Shape...  35.5 us
    pallas_call x1, Pallas kernels, attention_call(): pl.pallas_call(attention_kernel, name='attention', out_shape=(jax.ShapeDt...  18.5 us
    pallas_call x1, Pallas kernels, finish_call(): pl.pallas_call(finish_kernel, name='finish', out_shape=tuple((jax.ShapeDt...  2.07 us

profile of v9, /device:TPU:1, one launch (start us, length us, event | category | flops | bytes accessed | tf_op | source)
XLA Modules:
  0.0 98.9 jit_solution(16269629362405164168)
XLA Ops:
  0.6 42.1 %gather_keys.1 = (bf16[16,528,128]{2,1,0:T(8,128)(2,1)S(1)}, bf16[16,512,128]{2,1,0:T(8,128)(2,1)S(1)}, bf16[4,2,256,128]{3,2,1,0:T(8,128)(2,1)S(1)}, bf16[4,2,2...) custom-call(bf16[512,256]{1,0:T(8,128)(2,1)} %cq_h.3, ...), custom_call_target="tpu_custom_call" | custom-call | tf_op jit(solution)/shard_map/gather_keys/pallas_call | solution.py:286
  42.7 18.5 %attention.1 = (f32[4,128,512]{2,1,0:T(8,128)S(1)}, f32[4,128,512]{2,1,0:T(8,128)S(1)}, f32[4,256,128]{2,1,0:T(8,128)S(1)}, f32[4,256,128]{2,1,0:T(8,128)S(1)}, ...) custom-call(s32[16,128]{1,0:T(8,128)S(1)} %get-tuple-element.31.ids, s32[32]{0:T(128)} %docs.1, ...), custom_call_target="tpu_custom_call" | custom-call | tf_op jit(solution)/shard_map/attention/pallas_call | solution.py:489
  61.2 0.0 copy-start
  61.3 0.0 copy-start.1
  61.3 35.5 %scatter_grads.1 = (f32[6,512,256]{2,1,0:T(8,128)S(1)}, f32[2,512,256]{2,1,0:T(8,128)S(1)}, f32[8,512]{1,0:T(8,128)S(1)}) custom-call(bf16[512,256]{1,0:T(8,128)(2,1)} %cq_h.3, bf16[512,256]{1,0:T(8,128)(2,1)} %ck.1, bf16[512,256]{1,0:T(8,128)(2,1)} %nq_h.3, bf16[512,256]{1,0:T(8,128)(2,1)} %nk_h.3, f32[1,256]{1,0:T(1,128)} %bitcast.12, f32[1,256]{1,0:T(1,128)} %bitcast.6, ...), custom_call_target="tpu_custom_call" | custom-call | tf_op jit(solution)/shard_map/scatter_grads/pallas_call | solution.py:740
  96.8 0.0 copy-done
  96.8 0.0 copy-done.1
  96.8 2.1 %finish.1 = (f32[512,256]{1,0:T(8,128)}, f32[512,256]{1,0:T(8,128)}, f32[512,256]{1,0:T(8,128)}, f32[512,256]{1,0:T(8,128)}, f32[512,256]{1,0:T(8,128)}, /*index...) custom-call(bf16[512,256]{1,0:T(8,128)(2,1)S(1)} %copy-done, f32[1,256]{1,0:T(1,128)S(1)} %bitcast.7, ...), custom_call_target="tpu_custom_call" | custom-call | tf_op jit(solution)/shard_map/finish/pallas_call | solution.py:805
Async XLA Ops:
  61.2 35.5 %copy-start = (bf16[512,256]{1,0:T(8,128)(2,1)S(1)}, bf16[512,256]{1,0:T(8,128)(2,1)}, u32[]{:S(2)}) copy-start(bf16[512,256]{1,0:T(8,128)(2,1)} %ck.1) | copy-start | bytes 786436
  61.3 35.5 %copy-start.1 = (f32[256]{0:T(256)S(1)}, f32[256]{0:T(256)}, u32[]{:S(2)}) copy-start(f32[256]{0:T(256)} %param.19) | copy-start | bytes 3076

commit v10 on v9

--- a/solution.py
+++ b/solution.py
@@ -24,7 +24,7 @@
 PLAIN = (((1,), (0,)), ((), ()))
 PACKET = 528
 SHIFT = 160
-GROUP = 2
+GROUP = 1
 SCALE = 1.0 / math.sqrt(HD)
 SCALE2 = SCALE * math.log2(math.e)
 

time: 99.4 us -> 99 us (level)
    pallas_call x1, Pallas kernels: 18.5 us -> 7.21 us  [attention_call(): pl.pallas_call(attention_kernel, name='attention', out_shape=(jax.ShapeDt...]
    pallas_call x1, Pallas kernels: 35.5 us -> 46.7 us  [scatter_call(): pl.pallas_call(scatter_kernel, name='scatter_grads', out_shape=(jax.Shape...]
where the time goes in v10:
time: 99 us; the launch traced here: 98.7 us
  Pallas kernels  98 us (99%)
    pallas_call x1, Pallas kernels, scatter_call(): pl.pallas_call(scatter_kernel, name='scatter_grads', out_shape=(jax.Shape...  46.7 us
    pallas_call x1, Pallas kernels, gather_call(): pl.pallas_call(gather_kernel, name='gather_keys', out_shape=(jax.ShapeDty...  42.1 us
    pallas_call x1, Pallas kernels, attention_call(): pl.pallas_call(attention_kernel, name='attention', out_shape=(jax.ShapeDt...  7.21 us
    pallas_call x1, Pallas kernels, finish_call(): pl.pallas_call(finish_kernel, name='finish', out_shape=tuple((jax.ShapeDt...  2.07 us

profile of v10, /device:TPU:1, one launch (start us, length us, event | category | flops | bytes accessed | tf_op | source)
XLA Modules:
  0.0 98.7 jit_solution(16521057411697605819)
XLA Ops:
  0.6 42.1 %gather_keys.1 = (bf16[16,528,128]{2,1,0:T(8,128)(2,1)S(1)}, bf16[16,512,128]{2,1,0:T(8,128)(2,1)S(1)}, bf16[4,2,256,128]{3,2,1,0:T(8,128)(2,1)S(1)}, bf16[4,2,2...) custom-call(bf16[512,256]{1,0:T(8,128)(2,1)} %cq_h.3, ...), custom_call_target="tpu_custom_call" | custom-call | tf_op jit(solution)/shard_map/gather_keys/pallas_call | solution.py:286
  42.7 7.2 %attention.1 = (f32[4,128,512]{2,1,0:T(8,128)S(1)}, f32[4,128,512]{2,1,0:T(8,128)S(1)}, f32[4,256,128]{2,1,0:T(8,128)S(1)}, f32[4,256,128]{2,1,0:T(8,128)S(1)}, ...) custom-call(s32[16,128]{1,0:T(8,128)S(1)} %get-tuple-element.31.ids, s32[32]{0:T(128)} %docs.1, ...), custom_call_target="tpu_custom_call" | custom-call | tf_op jit(solution)/shard_map/attention/pallas_call | solution.py:489
  50.0 0.0 copy-start
  50.0 0.0 copy-start.1
  50.0 46.7 %scatter_grads.1 = (f32[6,512,256]{2,1,0:T(8,128)S(1)}, f32[2,512,256]{2,1,0:T(8,128)S(1)}, f32[8,512]{1,0:T(8,128)S(1)}) custom-call(bf16[512,256]{1,0:T(8,128)(2,1)} %cq_h.3, bf16[512,256]{1,0:T(8,128)(2,1)} %ck.1, bf16[512,256]{1,0:T(8,128)(2,1)} %nq_h.3, bf16[512,256]{1,0:T(8,128)(2,1)} %nk_h.3, f32[1,256]{1,0:T(1,128)} %bitcast.12, f32[1,256]{1,0:T(1,128)} %bitcast.6, ...), custom_call_target="tpu_custom_call" | custom-call | tf_op jit(solution)/shard_map/scatter_grads/pallas_call | solution.py:740
  96.7 0.0 copy-done
  96.7 0.0 copy-done.1
  96.7 2.1 %finish.1 = (f32[512,256]{1,0:T(8,128)}, f32[512,256]{1,0:T(8,128)}, f32[512,256]{1,0:T(8,128)}, f32[512,256]{1,0:T(8,128)}, f32[512,256]{1,0:T(8,128)}, /*index...) custom-call(bf16[512,256]{1,0:T(8,128)(2,1)S(1)} %copy-done, f32[1,256]{1,0:T(1,128)S(1)} %bitcast.7, ...), custom_call_target="tpu_custom_call" | custom-call | tf_op jit(solution)/shard_map/finish/pallas_call | solution.py:805
Async XLA Ops:
  50.0 46.7 %copy-start = (bf16[512,256]{1,0:T(8,128)(2,1)S(1)}, bf16[512,256]{1,0:T(8,128)(2,1)}, u32[]{:S(2)}) copy-start(bf16[512,256]{1,0:T(8,128)(2,1)} %ck.1) | copy-start | bytes 786436
  50.0 46.7 %copy-start.1 = (f32[256]{0:T(256)S(1)}, f32[256]{0:T(256)}, u32[]{:S(2)}) copy-start(f32[256]{0:T(256)} %param.19) | copy-start | bytes 3076
